TPU v7x, 512 devices: a whole 4x4x16 slice. The times are simulated.
512 devices in a mesh: hid: 64 (over z, x), mdl: 8 (over y, core).
Axes of the slice: x: 4, y: 4, z: 16, core: 2. Of those that a mesh axis runs over, the one named last changes fastest.
Arguments:
- inputs: bfloat16 [768, 8192], P('hid', 'mdl'), may hold values from -6 to 6
- cotangent: bfloat16 [768, 8192], P('hid', 'mdl'), may hold values from -6 to 6
- w_gate: bfloat16 [8192, 16384], P('mdl', 'hid'), may hold values from -0.0625 to 0.0625
- w_up: bfloat16 [8192, 16384], P('mdl', 'hid'), may hold values from -0.0625 to 0.0625
- w_down: bfloat16 [16384, 8192], P('hid', 'mdl'), may hold values from -0.046875 to 0.046875
- keep_mask: int32 [12, 128], P(None, 'hid'), may hold values 0 or 1
Outputs:
- grad_input: bfloat16 [768, 8192], P('hid', 'mdl')
- grad_gate: bfloat16 [8192, 16384], P('mdl', 'hid')
- grad_up: bfloat16 [8192, 16384], P('mdl', 'hid')
- grad_down: bfloat16 [16384, 8192], P('hid', 'mdl')
All inputs are finite; a program needn't handle non-finite values. No bound on the sum of `keep_mask` on one device may be relied on, other than what follows from the above.
Results may differ from a plain program's by a relative error of at most 0.0049.
Values may be sent and summed in bfloat16 or wider, within the bound.
No kernel may reach another device: no remote copies, remote signals or barrier semaphores. Data moves between devices by JAX's collectives and lax.ppermute only.
A program may use at most 64 MiB of HBM per device.

v0:
```python
import jax
import jax.numpy as jnp
from jax import lax
from jax.sharding import PartitionSpec as P


def pointwise_parts(gate_pre, up_pre, grad_hidden, keep_full):
    sigmoid_gate = jax.nn.sigmoid(gate_pre)
    silu_gate = gate_pre * sigmoid_gate
    hidden_kept = (silu_gate * up_pre * keep_full).astype(jnp.bfloat16)
    slope = sigmoid_gate * (1.0 + gate_pre * (1.0 - sigmoid_gate))
    grad_gate_pre = (grad_hidden * up_pre * slope).astype(jnp.bfloat16)
    grad_up_pre = (grad_hidden * silu_gate).astype(jnp.bfloat16)
    return (hidden_kept, grad_gate_pre, grad_up_pre)


def shards(inputs, cotangent, w_gate, w_up, w_down, keep_mask):
    inner = (((1,), (1,)), ((), ()))
    outer = (((0,), (0,)), ((), ()))
    all_inputs, all_cotangent = (
        lax.all_gather(inputs, "hid", axis=0, tiled=True),
        lax.all_gather(cotangent, "hid", axis=0, tiled=True),
    )
    total_rows = all_inputs.shape[0]
    local_hidden = w_gate.shape[1]
    tiles, local_blocks = keep_mask.shape
    tile_rows = total_rows // tiles
    block_cols = local_hidden // local_blocks
    keep_full = jnp.broadcast_to(
        keep_mask.astype(jnp.float32)[:, None, :, None],
        (tiles, tile_rows, local_blocks, block_cols),
    ).reshape(total_rows, local_hidden)
    part_gate = jnp.dot(all_inputs, w_gate, preferred_element_type=jnp.float32)
    part_up = jnp.dot(all_inputs, w_up, preferred_element_type=jnp.float32)
    part_hidden = lax.dot_general(all_cotangent, w_down, inner, preferred_element_type=jnp.float32)
    gate_pre, up_pre, grad_hidden = lax.psum((part_gate, part_up, part_hidden), "mdl")
    hidden_kept, grad_gate_pre, grad_up_pre = pointwise_parts(
        gate_pre, up_pre, grad_hidden, keep_full
    )
    grad_down = lax.dot_general(
        hidden_kept, all_cotangent, outer, preferred_element_type=jnp.float32
    ).astype(jnp.bfloat16)
    grad_gate = lax.dot_general(
        all_inputs, grad_gate_pre, outer, preferred_element_type=jnp.float32
    ).astype(jnp.bfloat16)
    grad_up = lax.dot_general(
        all_inputs, grad_up_pre, outer, preferred_element_type=jnp.float32
    ).astype(jnp.bfloat16)
    result = lax.dot_general(grad_gate_pre, w_gate, inner, preferred_element_type=jnp.float32)
    grad_input = lax.psum_scatter(
        result + lax.dot_general(grad_up_pre, w_up, inner, preferred_element_type=jnp.float32),
        "hid",
        scatter_dimension=0,
        tiled=True,
    ).astype(jnp.bfloat16)
    return (grad_input, grad_gate, grad_up, grad_down)


def solution(mesh):
    placed = (
        P("hid", "mdl"),
        P("hid", "mdl"),
        P("mdl", "hid"),
        P("mdl", "hid"),
        P("hid", "mdl"),
        P(None, "hid"),
    )
    return jax.shard_map(
        shards,
        mesh=mesh,
        in_specs=placed,
        out_specs=(P("hid", "mdl"), P("mdl", "hid"), P("mdl", "hid"), P("hid", "mdl")),
        check_vma=False,
    )
```

profile of v0, /device:TPU:6, one launch (start us, length us, event | category | flops | bytes accessed | tf_op | source)
XLA Modules:
  0.0 631.5 jit_solution(13518086702169299675)
XLA Ops:
  8.7 146.4 %all-gather.7.cloned.1.call-done = bf16[64,12,1024]{2,1,0:T(8,128)(2,1)} async-done(((bf16[1,12,1024]{2,1,0:T(8,128)(2,1)}), bf16[64,12,1024]{2,1,0:T(8,128)(2,1)}) %all-gather.7.cloned.1.call-update) | async-done | bytes 1572880 | tf_op jit(solution)/shard_map/all_gather | solution.py:21
  155.1 2.5 reshape.16
  157.6 1.4 fusion.11
  159.1 1.5 fusion.10
  160.5 134.5 %all-gather.5.cloned.1.call-done = bf16[64,12,1024]{2,1,0:T(8,128)(2,1)} async-done(((bf16[1,12,1024]{2,1,0:T(8,128)(2,1)}), bf16[64,12,1024]{2,1,0:T(8,128)(2,1)}) %all-gather.5.cloned.1.call-update) | async-done | bytes 1572880 | tf_op jit(solution)/shard_map/all_gather | solution.py:22
  295.0 3.6 reshape.14
  298.6 2.9 fusion.9
  301.5 79.5 %all-reduce.5.cloned.1.call-done = (f32[768,256]{1,0:T(8,128)}, f32[768,256]{1,0:T(8,128)}, f32[768,256]{1,0:T(8,128)}) async-done(((f32[768,256]{1,0:T(8,128)}, f32[768,256]{1,0:T(8,128)}, f32[768,256]{1,0:T(8,128)}), (f32[768,256]{1,0:T(8,128)}, f32[768,256]{1,0:T(8,128)}, f32[768,256]{1,0:T(8,128)})) %all-reduce.5.cloned.1.call-update) | async-done | bytes 2359312 | tf_op jit(solution)/shard_map/psum | solution.py:36
  381.1 2.0 multiply_convert_fusion
  383.7 2.4 convolution_add_fusion
  386.0 162.8 %fusion = f32[16,1024]{1,0:T(8,128)S(1)} fusion(f32[768,1024]{1,0:T(8,128)} %convolution_add_fusion), kind=kCustom, calls=%all-reduce-scatter | all-reduce-scatter fusion | flops 1048577 | bytes 3213312
  548.9 7.0 %collective-permute-start.15 = (bf16[12,1024]{1,0:T(8,128)(2,1)S(1)}, bf16[12,1024]{1,0:T(8,128)(2,1)S(1)}, u32[]{:S(2)}, u32[]{:S(2)}) collective-permute-start(bf16[12,1024]{1,0:T(8,128)(2,1)S(1)} %slice), channel_id=1, source_target_pairs={{0,128},{8,136},{16,144},{24,152},{32,160},{40,168},{48,176},{56,1... | collective-permute-start | bytes 73736
  557.9 2.2 collective-permute-start.1
  560.1 1.9 collective-permute-start.2
  562.0 7.8 %collective-permute-start.3 = (bf16[16,1024]{1,0:T(8,128)(2,1)S(1)}, bf16[16,1024]{1,0:T(8,128)(2,1)S(1)}, u32[]{:S(2)}, u32[]{:S(2)}) collective-permute-start(bf16[16,1024]{1,0:T(8,128)(2,1)S(1)} %convert.30), channel_id=1, source_target_pairs={{0,32},{8,40},{16,48},{24,56},{32,64},{40,72},{48,80},{56,88},{64,... | collective-permute-start | bytes 98312
  569.8 11.3 %collective-permute-start.4 = (bf16[16,1024]{1,0:T(8,128)(2,1)S(1)}, bf16[16,1024]{1,0:T(8,128)(2,1)S(1)}, u32[]{:S(2)}, u32[]{:S(2)}) collective-permute-start(bf16[16,1024]{1,0:T(8,128)(2,1)S(1)} %convert.30), channel_id=1, source_target_pairs={{0,40},{8,48},{16,56},{24,64},{32,72},{40,80},{48,88},{56,96},{64,... | collective-permute-start | bytes 98312
  581.1 1.3 collective-permute-start.5
  582.7 3.4 convolution_convert_fusion
  586.1 1.3 collective-permute-start.6
  587.4 5.6 collective-permute-start.7
  593.0 4.1 collective-permute-start.8
  597.1 2.7 collective-permute-start.9
  599.8 1.4 collective-permute-start.10
  601.2 1.4 fusion.2
  602.7 2.0 collective-permute-start.11
  604.7 2.1 collective-permute-start.12
  606.9 2.4 collective-permute-start.13
  609.3 1.9 collective-permute-start.14
  611.2 4.0 collective-permute-start
  615.2 1.4 fusion.1
  616.6 2.1 copy.17
  619.9 4.4 concatenate
  (73 shorter events, 5.5 us)
Async XLA Ops:
  7.2 150.4 %copy-start = (bf16[1024,256]{1,0:T(8,128)(2,1)S(1)}, bf16[1024,256]{1,0:T(8,128)(2,1)}, u32[]{:S(2)}) copy-start(bf16[1024,256]{1,0:T(8,128)(2,1)} %param.8) | copy-start | bytes 1572868
  7.2 147.9 %all-gather.7.cloned.1.call-start = ((), (), s32[]{:S(2)}) async-start(), calls=%async_computation.1 | async-start | bytes 2129920 | tf_op jit(solution)/shard_map/all_gather | solution.py:21
  7.9 287.1 %all-gather.5.cloned.1.call-start = ((), (), s32[]{:S(2)}) async-start(), calls=%async_computation | async-start | bytes 2129920 | tf_op jit(solution)/shard_map/all_gather | solution.py:22
  8.7 372.4 %all-reduce.5.cloned.1.call-start = ((), (), s32[]{:S(2)}) async-start(), calls=%async_computation.2 | async-start | bytes 4718592 | tf_op jit(solution)/shard_map/psum | solution.py:36
  160.5 138.1 %copy-start.3 = (bf16[256,1024]{1,0:T(8,128)(2,1)S(1)}, bf16[256,1024]{1,0:T(8,128)(2,1)}, u32[]{:S(2)}) copy-start(bf16[256,1024]{1,0:T(8,128)(2,1)} %param.10) | copy-start | bytes 1572868
  386.0 169.8 %copy-start.20 = (s32[12,2]{0,1:T(2,128)S(1)}, s32[12,2]{0,1:T(2,128)}, u32[]{:S(2)}) copy-start(s32[12,2]{0,1:T(2,128)} %param.11) | copy-start | bytes 292
  548.9 32.2 %collective-permute-start.15 = (bf16[12,1024]{1,0:T(8,128)(2,1)S(1)}, bf16[12,1024]{1,0:T(8,128)(2,1)S(1)}, u32[]{:S(2)}, u32[]{:S(2)}) collective-permute-start(bf16[12,1024]{1,0:T(8,128)(2,1)S(1)} %slice), channel_id=1, source_target_pairs={{0,128},{8,136},{16,144},{24,152},{32,160},{40,168},{48,176},{56,1... | collective-permute-start | bytes 73736
  557.9 28.2 %collective-permute-start.1 = (bf16[16,1024]{1,0:T(8,128)(2,1)S(1)}, bf16[16,1024]{1,0:T(8,128)(2,1)S(1)}, u32[]{:S(2)}, u32[]{:S(2)}) collective-permute-start(bf16[16,1024]{1,0:T(8,128)(2,1)S(1)} %convert.30), channel_id=1, source_target_pairs={{0,16},{8,24},{16,32},{24,40},{32,48},{40,56},{48,64},{56,72},{64,... | collective-permute-start | bytes 98312
  560.1 27.3 %collective-permute-start.2 = (bf16[16,1024]{1,0:T(8,128)(2,1)S(1)}, bf16[16,1024]{1,0:T(8,128)(2,1)S(1)}, u32[]{:S(2)}, u32[]{:S(2)}) collective-permute-start(bf16[16,1024]{1,0:T(8,128)(2,1)S(1)} %convert.30), channel_id=1, source_target_pairs={{0,24},{8,32},{16,40},{24,48},{32,56},{40,64},{48,72},{56,80},{64,... | collective-permute-start | bytes 98312
  562.0 31.0 %collective-permute-start.3 = (bf16[16,1024]{1,0:T(8,128)(2,1)S(1)}, bf16[16,1024]{1,0:T(8,128)(2,1)S(1)}, u32[]{:S(2)}, u32[]{:S(2)}) collective-permute-start(bf16[16,1024]{1,0:T(8,128)(2,1)S(1)} %convert.30), channel_id=1, source_target_pairs={{0,32},{8,40},{16,48},{24,56},{32,64},{40,72},{48,80},{56,88},{64,... | collective-permute-start | bytes 98312
  569.8 27.3 %collective-permute-start.4 = (bf16[16,1024]{1,0:T(8,128)(2,1)S(1)}, bf16[16,1024]{1,0:T(8,128)(2,1)S(1)}, u32[]{:S(2)}, u32[]{:S(2)}) collective-permute-start(bf16[16,1024]{1,0:T(8,128)(2,1)S(1)} %convert.30), channel_id=1, source_target_pairs={{0,40},{8,48},{16,56},{24,64},{32,72},{40,80},{48,88},{56,96},{64,... | collective-permute-start | bytes 98312
  581.1 18.7 %collective-permute-start.5 = (bf16[16,1024]{1,0:T(8,128)(2,1)S(1)}, bf16[16,1024]{1,0:T(8,128)(2,1)S(1)}, u32[]{:S(2)}, u32[]{:S(2)}) collective-permute-start(bf16[16,1024]{1,0:T(8,128)(2,1)S(1)} %convert.30), channel_id=1, source_target_pairs={{0,48},{8,56},{16,64},{24,72},{32,80},{40,88},{48,96},{56,104},{64... | collective-permute-start | bytes 98312
  586.1 16.6 %collective-permute-start.6 = (bf16[16,1024]{1,0:T(8,128)(2,1)S(1)}, bf16[16,1024]{1,0:T(8,128)(2,1)S(1)}, u32[]{:S(2)}, u32[]{:S(2)}) collective-permute-start(bf16[16,1024]{1,0:T(8,128)(2,1)S(1)} %convert.30), channel_id=1, source_target_pairs={{0,56},{8,64},{16,72},{24,80},{32,88},{40,96},{48,104},{56,112},{6... | collective-permute-start | bytes 98312
  587.4 17.3 %collective-permute-start.7 = (bf16[16,1024]{1,0:T(8,128)(2,1)S(1)}, bf16[16,1024]{1,0:T(8,128)(2,1)S(1)}, u32[]{:S(2)}, u32[]{:S(2)}) collective-permute-start(bf16[16,1024]{1,0:T(8,128)(2,1)S(1)} %convert.30), channel_id=1, source_target_pairs={{0,64},{8,72},{16,80},{24,88},{32,96},{40,104},{48,112},{56,120},{... | collective-permute-start | bytes 98312
  593.0 8.2 %copy-start.4 = (bf16[16,1024]{1,0:T(8,128)(2,1)}, bf16[16,1024]{1,0:T(8,128)(2,1)S(1)}, u32[]{:S(2)}) copy-start(bf16[16,1024]{1,0:T(8,128)(2,1)S(1)} %collective-permute-done.3) | copy-start | bytes 98308
  593.0 13.8 %collective-permute-start.8 = (bf16[16,1024]{1,0:T(8,128)(2,1)S(1)}, bf16[16,1024]{1,0:T(8,128)(2,1)S(1)}, u32[]{:S(2)}, u32[]{:S(2)}) collective-permute-start(bf16[16,1024]{1,0:T(8,128)(2,1)S(1)} %convert.30), channel_id=1, source_target_pairs={{0,72},{8,80},{16,88},{24,96},{32,104},{40,112},{48,120},{56,128},... | collective-permute-start | bytes 98312
  597.1 4.1 copy-start.6
  597.1 12.2 %collective-permute-start.9 = (bf16[16,1024]{1,0:T(8,128)(2,1)S(1)}, bf16[16,1024]{1,0:T(8,128)(2,1)S(1)}, u32[]{:S(2)}, u32[]{:S(2)}) collective-permute-start(bf16[16,1024]{1,0:T(8,128)(2,1)S(1)} %convert.30), channel_id=1, source_target_pairs={{0,80},{8,88},{16,96},{24,104},{32,112},{40,120},{48,128},{56,136}... | collective-permute-start | bytes 98312
  599.8 11.3 %collective-permute-start.10 = (bf16[16,1024]{1,0:T(8,128)(2,1)S(1)}, bf16[16,1024]{1,0:T(8,128)(2,1)S(1)}, u32[]{:S(2)}, u32[]{:S(2)}) collective-permute-start(bf16[16,1024]{1,0:T(8,128)(2,1)S(1)} %convert.30), channel_id=1, source_target_pairs={{0,88},{8,96},{16,104},{24,112},{32,120},{40,128},{48,136},{56,144... | collective-permute-start | bytes 98312
  602.7 16.1 %copy-start.2 = (bf16[1024,256]{0,1:T(8,128)(2,1)S(1)}, bf16[1024,256]{0,1:T(8,128)(2,1)}, u32[]{:S(2)}) copy-start(bf16[1024,256]{0,1:T(8,128)(2,1)} %fusion.2) | copy-start | bytes 1572868
  602.7 12.5 %copy-start.10 = (bf16[16,1024]{1,0:T(8,128)(2,1)}, bf16[16,1024]{1,0:T(8,128)(2,1)S(1)}, u32[]{:S(2)}) copy-start(bf16[16,1024]{1,0:T(8,128)(2,1)S(1)} %collective-permute-done.6) | copy-start | bytes 98308
  602.7 17.1 %collective-permute-start.11 = (bf16[16,1024]{1,0:T(8,128)(2,1)S(1)}, bf16[16,1024]{1,0:T(8,128)(2,1)S(1)}, u32[]{:S(2)}, u32[]{:S(2)}) collective-permute-start(bf16[16,1024]{1,0:T(8,128)(2,1)S(1)} %convert.30), channel_id=1, source_target_pairs={{0,96},{8,104},{16,112},{24,120},{32,128},{40,136},{48,144},{56,15... | collective-permute-start | bytes 98312
  604.7 10.4 %copy-start.12 = (bf16[16,1024]{1,0:T(8,128)(2,1)}, bf16[16,1024]{1,0:T(8,128)(2,1)S(1)}, u32[]{:S(2)}) copy-start(bf16[16,1024]{1,0:T(8,128)(2,1)S(1)} %collective-permute-done.7) | copy-start | bytes 98308
  604.7 15.0 %collective-permute-start.12 = (bf16[16,1024]{1,0:T(8,128)(2,1)S(1)}, bf16[16,1024]{1,0:T(8,128)(2,1)S(1)}, u32[]{:S(2)}, u32[]{:S(2)}) collective-permute-start(bf16[16,1024]{1,0:T(8,128)(2,1)S(1)} %convert.30), channel_id=1, source_target_pairs={{0,104},{8,112},{16,120},{24,128},{32,136},{40,144},{48,152},{56,1... | collective-permute-start | bytes 98312
  606.8 8.3 %copy-start.14 = (bf16[16,1024]{1,0:T(8,128)(2,1)}, bf16[16,1024]{1,0:T(8,128)(2,1)S(1)}, u32[]{:S(2)}) copy-start(bf16[16,1024]{1,0:T(8,128)(2,1)S(1)} %collective-permute-done.8) | copy-start | bytes 98308
  606.9 12.9 %collective-permute-start.13 = (bf16[16,1024]{1,0:T(8,128)(2,1)S(1)}, bf16[16,1024]{1,0:T(8,128)(2,1)}, u32[]{:S(2)}, u32[]{:S(2)}) collective-permute-start(bf16[16,1024]{1,0:T(8,128)(2,1)S(1)} %convert.30), channel_id=1, source_target_pairs={{0,112},{8,120},{16,128},{24,136},{32,144},{40,152},{48,160},{56,1... | collective-permute-start | bytes 98312
  609.3 5.9 copy-start.16
  609.3 10.5 %collective-permute-start.14 = (bf16[16,1024]{1,0:T(8,128)(2,1)S(1)}, bf16[16,1024]{1,0:T(8,128)(2,1)}, u32[]{:S(2)}, u32[]{:S(2)}) collective-permute-start(bf16[16,1024]{1,0:T(8,128)(2,1)S(1)} %convert.30), channel_id=1, source_target_pairs={{0,120},{8,128},{16,136},{24,144},{32,152},{40,160},{48,168},{56,1... | collective-permute-start | bytes 98312
  611.2 4.0 copy-start.18
  611.2 8.6 %collective-permute-start = (bf16[16,1024]{1,0:T(8,128)(2,1)S(1)}, bf16[16,1024]{1,0:T(8,128)(2,1)}, u32[]{:S(2)}, u32[]{:S(2)}) collective-permute-start(bf16[16,1024]{1,0:T(8,128)(2,1)S(1)} %convert.30), channel_id=1, source_target_pairs={{0,8},{8,16},{16,24},{24,32},{32,40},{40,48},{48,56},{56,64},{64,7... | collective-permute-start | bytes 98312
  616.6 3.2 copy-start.13
  616.6 3.2 copy-start.15
  (8 other events, 22.2 us)
Sparse Core Ops, SparseCore 0:
  11.0 144.0 all-gather.6
  158.0 136.9 all-gather.4
  301.7 79.3 all-reduce.4
where the time goes:
time: 633 us; the launch traced here: 631 us
  waiting for transfers between devices  362 us (57%)
  blocking collectives  163 us (26%)
  starting transfers between devices  58.9 us (9%)
  local copies, waits for them, and re-layouts  16 us (3%)
  matrix products  15 us (2%)
  between operations  14.9 us (2%)
    unnamed x1, blocking collectives  163 us
    all_gather x1, waiting for transfers between devices, shards(): lax.all_gather(inputs, 'hid', axis=0, tiled=True)  146 us
    all_gather x1, waiting for transfers between devices, shards(): lax.all_gather(cotangent, 'hid', axis=0, tiled=True)  134 us
    psum x1, waiting for transfers between devices, shards(): lax.psum((part_gate, part_up, part_hidden), 'mdl')  79.5 us
    unnamed x16, starting transfers between devices  58.8 us
    unnamed x49, local copies, waits for them, and re-layouts  15 us
  transfers between devices with their start and end apart: 19, of which 3 were waited for; matrix products, arithmetic and copies ran while one was open for 3% of the time, Pallas kernels for 0%

commit v1 on v0

v1 whole, which is shorter than its diff:
```python
import jax
import jax.numpy as jnp
from jax import lax
from jax.sharding import Mesh, PartitionSpec as P

F32, BF16 = jnp.float32, jnp.bfloat16
INNER = (((1,), (1,)), ((), ()))
OUTER = (((0,), (0,)), ((), ()))
ALONG_X = (0, -1, 1, 2)


def ring(size, step):
    return [(i, (i + step) % size) for i in range(size)]


def dot(a, b, dims):
    return lax.dot_general(a, b, dims, preferred_element_type=F32)


def pointwise_parts(gate_pre, up_pre, grad_hidden, keep_rows):
    sigmoid_gate = jax.nn.sigmoid(gate_pre)
    silu_gate = gate_pre * sigmoid_gate
    hidden_kept = (silu_gate * up_pre * keep_rows).astype(BF16)
    slope = sigmoid_gate * (1.0 + gate_pre * (1.0 - sigmoid_gate))
    grad_gate_pre = (grad_hidden * up_pre * slope).astype(BF16)
    grad_up_pre = (grad_hidden * silu_gate).astype(BF16)
    return hidden_kept, grad_gate_pre, grad_up_pre


def keep_of_rows(keep_mask, rows, own_tokens, nz, nx, total):
    tiles, blocks = keep_mask.shape
    part = lax.axis_index("c") * 4 + lax.axis_index("y")
    place = part * rows + lax.broadcasted_iota(jnp.int32, (rows, 1), 0)
    per_chunk = nz * own_tokens
    chunk, inside = place // per_chunk, place % per_chunk
    shift = jnp.where(chunk == 1, -1, jnp.where(chunk == 2, 1, jnp.where(chunk == 3, 2, 0)))
    from_x = (lax.axis_index("x") + shift + nx) % nx
    token = (inside // own_tokens * nx + from_x) * own_tokens + inside % own_tokens
    tile = token // (total // tiles)
    chosen = tile == lax.broadcasted_iota(jnp.int32, (rows, tiles), 1)
    keep = [
        jnp.sum(jnp.where(chosen, keep_mask[:, b][None, :], 0), axis=1, keepdims=True)
        for b in range(blocks)
    ]
    return jnp.concatenate([jnp.broadcast_to(k, (rows, 128)) for k in keep], axis=1).astype(F32)


def shards(inputs, cotangent, w_gate, w_up, w_down, keep_mask):
    own_tokens, width = inputs.shape
    hidden = w_gate.shape[1]
    nz, nx, ny, nc = 16, 4, 4, 2
    total = own_tokens * nz * nx
    rows = total // (ny * nc)
    flat = own_tokens * width // 128

    keep_rows = keep_of_rows(keep_mask, rows, own_tokens, nz, nx, total)

    packed = jnp.concatenate([inputs.reshape(flat, 128), cotangent.reshape(flat, 128)])
    along_z = lax.all_gather(packed, ("zh", "zl"))
    own = [along_z[:, i * flat : (i + 1) * flat].reshape(nz * own_tokens, width) for i in range(2)]
    own = jnp.stack(own)
    right = lax.ppermute(own, "x", ring(nx, 1))
    left = lax.ppermute(own, "x", ring(nx, -1))
    far_in = lax.ppermute(right[0], "x", ring(nx, 1))
    far_cot = lax.ppermute(left[1], "x", ring(nx, -1))
    x_parts = [own[0], right[0], left[0], far_in]
    c_parts = [own[1], right[1], left[1], far_cot]
    all_inputs = jnp.concatenate(x_parts)
    all_cotangent = jnp.concatenate(c_parts)

    part_gate = dot(all_inputs, w_gate, (((1,), (0,)), ((), ())))
    part_up = dot(all_inputs, w_up, (((1,), (0,)), ((), ())))
    part_hidden = dot(all_cotangent, w_down, INNER)
    parts = jnp.stack(
        [p.reshape(nc, ny, rows, hidden) for p in (part_gate, part_up, part_hidden)], axis=2
    )
    summed = jnp.sum(lax.all_to_all(parts, "c", 0, 0), axis=0)
    summed = jnp.sum(lax.all_to_all(summed, "y", 0, 0), axis=0)
    hidden_kept, grad_gate_pre, grad_up_pre = pointwise_parts(
        summed[0], summed[1], summed[2], keep_rows
    )

    def over_mdl(a):
        return lax.all_gather(lax.all_gather(a, "y"), "c")

    both = over_mdl(jnp.stack([grad_gate_pre, grad_up_pre]))
    all_gate = both[:, :, 0].reshape(total, hidden)
    all_up = both[:, :, 1].reshape(total, hidden)
    all_kept = over_mdl(hidden_kept).reshape(total, hidden)

    result = (dot(all_gate, w_gate, INNER) + dot(all_up, w_up, INNER)).astype(BF16)
    result = result.reshape(nx, nz * own_tokens, width)
    arrived = [lax.ppermute(result[k], "x", ring(nx, ALONG_X[k])) for k in (1, 2, 3)]
    kept = result[0].astype(F32) + sum(a.astype(F32) for a in arrived)
    kept = kept.astype(BF16).reshape(4, 4, flat, 128).transpose(1, 0, 2, 3)
    kept = jnp.sum(lax.all_to_all(kept, "zl", 0, 0).astype(F32), axis=0).astype(BF16)
    kept = jnp.sum(lax.all_to_all(kept, "zh", 0, 0).astype(F32), axis=0).astype(BF16)
    grad_input = kept.reshape(own_tokens, width)

    grad_down = dot(all_kept, all_cotangent, OUTER).astype(BF16)
    grad_gate = dot(all_inputs, all_gate, OUTER).astype(BF16)
    grad_up = dot(all_inputs, all_up, OUTER).astype(BF16)
    return grad_input, grad_gate, grad_up, grad_down


def solution(mesh):
    fine = Mesh(mesh.devices.reshape(4, 4, 4, 4, 2), ("zh", "zl", "x", "y", "c"))
    hid, mdl = ("zh", "zl", "x"), ("y", "c")
    placed = (P(hid, mdl), P(hid, mdl), P(mdl, hid), P(mdl, hid), P(hid, mdl), P(None, hid))
    return jax.shard_map(
        shards,
        mesh=fine,
        in_specs=placed,
        out_specs=(P(hid, mdl), P(mdl, hid), P(mdl, hid), P(hid, mdl)),
        check_vma=False,
    )
```

time: 633 us -> 199 us (0.31)
  waiting for transfers between devices: 362 us -> 60.9 us
  blocking collectives: 163 us -> 75.4 us
  starting transfers between devices: 58.9 us -> 35.2 us
  between operations: 14.9 us -> 1.05 us
  local copies, waits for them, and re-layouts: 16 us -> 8.5 us
    all_gather x2 -> x0, waiting for transfers between devices: 281 us -> none  [the longest x1 146 us: shards(): lax.all_gather(inputs, 'hid', axis=0, tiled=True)]
    unnamed x1 -> x0, blocking collectives: 163 us -> none
    psum x1 -> x0, waiting for transfers between devices: 79.5 us -> none  [shards(): lax.psum((part_gate, part_up, part_hidden), 'mdl')]
    all_gather x0 -> x5, blocking collectives: none -> 69.7 us  [the longest x1 40.1 us: shards(): along_z = lax.all_gather(packed, ('zh', 'zl'))]
    unnamed x16 -> x0, starting transfers between devices: 58.8 us -> none
    ppermute x0 -> x7, waiting for transfers between devices: none -> 30.8 us  [the longest x3 14.7 us: shards(): lax.ppermute(result[k], 'x', ring(nx, ALONG_X[k]))]
    all_to_all x0 -> x3, waiting for transfers between devices: none -> 30.1 us  [the longest x1 16.7 us: shards(): summed = jnp.sum(lax.all_to_all(summed, 'y', 0, 0), axis=0)]
    ppermute x0 -> x7, starting transfers between devices: none -> 20.8 us  [the longest x3 9.11 us: shards(): lax.ppermute(result[k], 'x', ring(nx, ALONG_X[k]))]
  transfers between devices with their start and end apart: 19 -> 10, of which waited for: 3 -> 7; matrix products, arithmetic and copies ran while one was open for 3% -> 6% of each run, Pallas kernels for 0% -> 0%
where the time goes in v1:
time: 199 us; the launch traced here: 196 us
  blocking collectives  75.4 us (38%)
  waiting for transfers between devices  60.9 us (31%)
  starting transfers between devices  35.2 us (18%)
  matrix products  12.5 us (6%)
  local copies, waits for them, and re-layouts  8.5 us (4%)
  other arithmetic  2.84 us (1%)
    all_gather x1, blocking collectives, shards(): along_z = lax.all_gather(packed, ('zh', 'zl'))  40.1 us
    all_gather x4, blocking collectives, over_mdl(): return lax.all_gather(lax.all_gather(a, 'y'), 'c')  29.6 us
    all_to_all x1, waiting for transfers between devices, shards(): summed = jnp.sum(lax.all_to_all(summed, 'y', 0, 0), axis=0)  16.7 us
    ppermute x3, waiting for transfers between devices, shards(): lax.ppermute(result[k], 'x', ring(nx, ALONG_X[k]))  14.7 us
    all_to_all x1, waiting for transfers between devices, shards(): lax.all_to_all(kept, 'zh', 0, 0).astype(F32)  13.5 us
    dot_general x8, matrix products, dot(): return lax.dot_general(a, b, dims, preferred_element_type=F32)  12.5 us
    ppermute x1, waiting for transfers between devices, shards(): right = lax.ppermute(own, 'x', ring(nx, 1))  12 us
    ppermute x3, starting transfers between devices, shards(): lax.ppermute(result[k], 'x', ring(nx, ALONG_X[k]))  9.11 us
  transfers between devices with their start and end apart: 10, of which 7 were waited for; matrix products, arithmetic and copies ran while one was open for 6% of the time, Pallas kernels for 0%

profile of v1, /device:TPU:6, one launch (start us, length us, event | category | flops | bytes accessed | tf_op | source)
XLA Modules:
  0.0 196.4 jit_solution(13820543080513042487)
XLA Ops:
  0.6 0.9 reshape.202
  1.5 0.8 reshape.203
  2.3 40.1 %all-gather = bf16[3072,128]{1,0:T(8,128)(2,1)S(1)} all-gather(bf16[192,128]{1,0:T(8,128)(2,1)S(1)} %pad_maximum_fusion.6), channel_id=2, replica_groups=mesh['zh'=4,'zl'=4,'x'=4,'y'=4,'c'=2] {'zh','zl'}, dimensions={0}, use_global_device_ids=true | all-gather | bytes 835584 | tf_op jit(solution)/shard_map/all_gather | solution.py:59
  42.7 0.8 constant_dynamic-update-slice_fusion.1
  44.4 2.4 %collective-permute-start = (bf16[2,192,1024]{2,1,0:T(8,128)(2,1)}, bf16[2,192,1024]{2,1,0:T(8,128)(2,1)S(1)}, u32[]{:S(2)}, u32[]{:S(2)}) collective-permute-start(bf16[2,192,1024]{2,1,0:T(8,128)(2,1)} %constant_dynamic-update-slice_fusion), channel_id=1, source_target_pairs={{0,8},{8,16},{16,24},{24,0},{1,9},{9,17},{17,25},{25,1},{2,10},{10... | collective-permute-start | bytes 2359304 | tf_op jit(solution)/shard_map/ppermute | solution.py:62
  46.8 3.5 %collective-permute-start.1 = (bf16[2,192,1024]{2,1,0:T(8,128)(2,1)}, bf16[2,192,1024]{2,1,0:T(8,128)(2,1)S(1)}, u32[]{:S(2)}, u32[]{:S(2)}) collective-permute-start(bf16[2,192,1024]{2,1,0:T(8,128)(2,1)} %constant_dynamic-update-slice_fusion), channel_id=1, source_target_pairs={{0,24},{8,0},{16,8},{24,16},{1,25},{9,1},{17,9},{25,17},{2,26},{10... | collective-permute-start | bytes 2359304 | tf_op jit(solution)/shard_map/ppermute | solution.py:63
  50.2 12.0 %collective-permute-done = bf16[2,192,1024]{2,1,0:T(8,128)(2,1)S(1)} collective-permute-done((bf16[2,192,1024]{2,1,0:T(8,128)(2,1)}, bf16[2,192,1024]{2,1,0:T(8,128)(2,1)S(1)}, u32[]{:S(2)}, u32[]{:S(2)}) %collective-permute-start) | collective-permute-done | bytes 786464 | tf_op jit(solution)/shard_map/ppermute | solution.py:62
  62.3 2.4 %collective-permute-start.2 = (bf16[192,1024]{1,0:T(8,128)(2,1)S(1)}, bf16[192,1024]{1,0:T(8,128)(2,1)}, u32[]{:S(2)}, u32[]{:S(2)}) collective-permute-start(bf16[192,1024]{1,0:T(8,128)(2,1)S(1)} %get-tuple-element.13), channel_id=1, source_target_pairs={{0,8},{8,16},{16,24},{24,0},{1,9},{9,17},{17,25},{25,1},{2,10},{10... | collective-permute-start | bytes 1179656 | tf_op jit(solution)/shard_map/ppermute | solution.py:64
  65.2 3.5 %collective-permute-start.3 = (bf16[192,1024]{1,0:T(8,128)(2,1)S(1)}, bf16[192,1024]{1,0:T(8,128)(2,1)S(1)}, u32[]{:S(2)}, u32[]{:S(2)}) collective-permute-start(bf16[192,1024]{1,0:T(8,128)(2,1)S(1)} %get-tuple-element.12), channel_id=1, source_target_pairs={{0,24},{8,0},{16,8},{24,16},{1,25},{9,1},{17,9},{25,17},{2,26},{10... | collective-permute-start | bytes 1179656 | tf_op jit(solution)/shard_map/ppermute | solution.py:65
  68.6 3.4 %collective-permute-done.2 = bf16[192,1024]{1,0:T(8,128)(2,1)} collective-permute-done((bf16[192,1024]{1,0:T(8,128)(2,1)S(1)}, bf16[192,1024]{1,0:T(8,128)(2,1)}, u32[]{:S(2)}, u32[]{:S(2)}) %collective-permute-start.2) | collective-permute-done | bytes 393248 | tf_op jit(solution)/shard_map/ppermute | solution.py:64
  72.1 1.6 fusion.12
  73.8 1.6 fusion.11
  77.0 5.6 %all_to_all.20 = f32[2,4,3,96,256]{4,3,1,2,0:T(8,128)S(1)} all-to-all(f32[2,4,3,96,256]{4,3,1,2,0:T(8,128)S(1)} %pad_maximum_fusion), channel_id=1, replica_groups=mesh['zh'=4,'zl'=4,'x'=4,'y'=4,'c'=2] {'c'}, dimensions={0} | all-to-all | bytes 4718592 | tf_op jit(solution)/shard_map/all_to_all | solution.py:77
  82.7 1.3 reduce_sum.60
  84.0 2.4 %copy.25 = f32[4,3,96,256]{3,2,1,0:T(8,128)} copy(f32[4,3,96,256]{3,2,0,1:T(8,128)} %reduce_sum.60) | data formatting | bytes 2359296 | tf_op jit(solution)/shard_map/reduce_sum | solution.py:77
  86.4 4.5 %all-to-all-start.1 = ((f32[4,3,96,256]{3,2,1,0:T(8,128)}), f32[4,3,96,256]{3,2,1,0:T(8,128)S(1)}, u32[]{:S(2)}, u32[]{:S(2)}) async-start(f32[4,3,96,256]{3,2,1,0:T(8,128)} %copy.25), calls=%async_computation.1 | async-start | bytes 2359296 | tf_op jit(solution)/shard_map/all_to_all | solution.py:78
  91.0 16.7 %all-to-all-done.1 = f32[4,3,96,256]{3,2,1,0:T(8,128)S(1)} async-done(((f32[4,3,96,256]{3,2,1,0:T(8,128)}), f32[4,3,96,256]{3,2,1,0:T(8,128)S(1)}, u32[]{:S(2)}, u32[]{:S(2)}) %all-to-all-start.1) | async-done | bytes 1179680 | tf_op jit(solution)/shard_map/all_to_all | solution.py:78
  108.0 13.0 %all-gather.1 = bf16[8,96,256]{2,1,0:T(8,128)(2,1)S(1)} all-gather(bf16[2,96,256]{2,1,0:T(8,128)(2,1)S(1)} %pad_maximum_fusion.5), channel_id=3, replica_groups=mesh['zh'=4,'zl'=4,'x'=4,'y'=4,'c'=2] {'y'}, dimensions={0}, use_global_device_ids=true | all-gather | bytes 491520 | tf_op jit(solution)/shard_map/all_gather | solution.py:84
  121.0 2.4 %all-gather.2 = bf16[8,2,96,256]{3,2,1,0:T(8,128)(2,1)S(1)} all-gather(bf16[4,2,96,256]{3,2,1,0:T(8,128)(2,1)S(1)} %bitcast.42), channel_id=4, replica_groups=mesh['zh'=4,'zl'=4,'x'=4,'y'=4,'c'=2] {'c'}, dimensions={0}, use_global_device_ids=true | all-gather | bytes 1179648 | tf_op jit(solution)/shard_map/all_gather | solution.py:84
  124.8 2.3 %collective-permute-start.4 = (bf16[192,1024]{1,0:T(8,128)(2,1)S(1)}, bf16[192,1024]{1,0:T(8,128)(2,1)S(1)}, u32[]{:S(2)}, u32[]{:S(2)}) collective-permute-start(bf16[192,1024]{1,0:T(8,128)(2,1)S(1)} %get-tuple-element.6), channel_id=1, source_target_pairs={{0,24},{8,0},{16,8},{24,16},{1,25},{9,1},{17,9},{25,17},{2,26},{10... | collective-permute-start | bytes 1179656 | tf_op jit(solution)/shard_map/ppermute | solution.py:93
  127.0 4.8 %collective-permute-start.5 = (bf16[192,1024]{1,0:T(8,128)(2,1)S(1)}, bf16[192,1024]{1,0:T(8,128)(2,1)S(1)}, u32[]{:S(2)}, u32[]{:S(2)}) collective-permute-start(bf16[192,1024]{1,0:T(8,128)(2,1)S(1)} %get-tuple-element.8), channel_id=1, source_target_pairs={{0,8},{8,16},{16,24},{24,0},{1,9},{9,17},{17,25},{25,1},{2,10},{10... | collective-permute-start | bytes 1179656 | tf_op jit(solution)/shard_map/ppermute | solution.py:93
  131.9 2.1 %collective-permute-start.6 = (bf16[192,1024]{1,0:T(8,128)(2,1)S(1)}, bf16[192,1024]{1,0:T(8,128)(2,1)S(1)}, u32[]{:S(2)}, u32[]{:S(2)}) collective-permute-start(bf16[192,1024]{1,0:T(8,128)(2,1)S(1)} %get-tuple-element.7), channel_id=1, source_target_pairs={{0,16},{8,24},{16,0},{24,8},{1,17},{9,25},{17,1},{25,9},{2,18},{10... | collective-permute-start | bytes 1179656 | tf_op jit(solution)/shard_map/ppermute | solution.py:93
  133.9 13.5 %collective-permute-done.4 = bf16[192,1024]{1,0:T(8,128)(2,1)S(1)} collective-permute-done((bf16[192,1024]{1,0:T(8,128)(2,1)S(1)}, bf16[192,1024]{1,0:T(8,128)(2,1)S(1)}, u32[]{:S(2)}, u32[]{:S(2)}) %collective-permute-start.4) | collective-permute-done | bytes 393248 | tf_op jit(solution)/shard_map/ppermute | solution.py:93
  147.5 1.2 collective-permute-done.5
  149.9 3.5 %all-to-all-start.2 = ((bf16[4,4,96,128]{3,2,1,0:T(8,128)(2,1)}), bf16[4,4,96,128]{3,2,1,0:T(8,128)(2,1)S(1)}, u32[]{:S(2)}, u32[]{:S(2)}) async-start(bf16[4,4,96,128]{3,2,1,0:T(8,128)(2,1)} %bitcast.39), calls=%async_computation.2 | async-start | bytes 786432 | tf_op jit(solution)/shard_map/all_to_all | solution.py:96
  153.3 12.1 %all_gather.34 = bf16[4,96,256]{2,1,0:T(8,128)(2,1)S(1)} all-gather(bf16[1,96,256]{2,1,0:T(8,128)(2,1)S(1)} %get-tuple-element.17), channel_id=1, replica_groups=mesh['zh'=4,'zl'=4,'x'=4,'y'=4,'c'=2] {'y'}, dimensions={0}, use_global_device_ids=true | all-gather | bytes 245760 | tf_op jit(solution)/shard_map/all_gather | solution.py:84
  165.5 2.1 %all-gather.3 = bf16[8,96,256]{2,1,0:T(8,128)(2,1)S(1)} all-gather(bf16[4,96,256]{2,1,0:T(8,128)(2,1)S(1)} %all_gather.34), channel_id=5, replica_groups=mesh['zh'=4,'zl'=4,'x'=4,'y'=4,'c'=2] {'c'}, dimensions={0}, use_global_device_ids=true | all-gather | bytes 589824 | tf_op jit(solution)/shard_map/all_gather | solution.py:84
  167.6 2.5 %convolution_convert_fusion.1 = bf16[1024,256]{1,0:T(8,128)(2,1)} fusion(bf16[768,256]{1,0:T(8,128)(2,1)S(1)} %bitcast.46, bf16[192,1024]{1,0:T(8,128)(2,1)} %collective-permute-done.2, bf16[192,1024]{1,0:T(8,128)(2,1)S(1)} %copy-done.14, bf16[192,1024]{1,0:T(8,128)(2,1)S(1)} %copy-done.11, bf16[192,1024]{1,0:T(8,128)(2,1)S(1)} %copy-done.5), kind=kOutput, calls=%fused_computation.5 | convolution fusion | flops 409206784 | bytes 2490368 | tf_op jit(solution)/shard_map/dot_general | solution.py:17
  170.1 2.5 %convolution_convert_fusion.2 = bf16[1024,256]{1,0:T(8,128)(2,1)} fusion(bf16[768,256]{1,0:T(8,128)(2,1)S(1)} %bitcast.44, bf16[192,1024]{1,0:T(8,128)(2,1)} %collective-permute-done.2, bf16[192,1024]{1,0:T(8,128)(2,1)S(1)} %copy-done.15, bf16[192,1024]{1,0:T(8,128)(2,1)S(1)} %copy-done.12, bf16[192,1024]{1,0:T(8,128)(2,1)S(1)} %copy-done.5), kind=kOutput, calls=%fused_computation.6 | convolution fusion | flops 409206784 | bytes 2490368 | tf_op jit(solution)/shard_map/dot_general | solution.py:17
  173.3 6.5 %all-to-all-start.3 = ((bf16[4,96,128]{2,1,0:T(8,128)(2,1)}), bf16[4,96,128]{2,1,0:T(8,128)(2,1)S(1)}, u32[]{:S(2)}, u32[]{:S(2)}) async-start(bf16[4,96,128]{2,1,0:T(8,128)(2,1)} %reduce_sum.62), calls=%async_computation.3 | async-start | bytes 196608 | tf_op jit(solution)/shard_map/all_to_all | solution.py:97
  179.9 2.4 %convolution_convert_fusion = bf16[256,1024]{1,0:T(8,128)(2,1)} fusion(bf16[768,256]{1,0:T(8,128)(2,1)S(1)} %bitcast.50, bf16[192,1024]{1,0:T(8,128)(2,1)} %copy-done.18, bf16[192,1024]{1,0:T(8,128)(2,1)S(1)} %copy-done.9, bf16[192,1024]{1,0:T(8,128)(2,1)S(1)} %copy-done.7, bf16[192,1024]{1,0:T(8,128)(2,1)S(1)} %copy-done.3), kind=kOutput, calls=%fused_computation.4 | convolution fusion | flops 409206784 | bytes 2490368 | tf_op jit(solution)/shard_map/dot_general | solution.py:17
  182.2 13.5 %all-to-all-done.3 = bf16[4,96,128]{2,1,0:T(8,128)(2,1)S(1)} async-done(((bf16[4,96,128]{2,1,0:T(8,128)(2,1)}), bf16[4,96,128]{2,1,0:T(8,128)(2,1)S(1)}, u32[]{:S(2)}, u32[]{:S(2)}) %all-to-all-start.3) | async-done | bytes 98336 | tf_op jit(solution)/shard_map/all_to_all | solution.py:97
  (71 shorter events, 7.7 us)
Async XLA Ops:
  0.6 71.5 %copy-start = (bf16[1024,256]{1,0:T(8,128)(2,1)S(1)}, bf16[1024,256]{1,0:T(8,128)(2,1)}, u32[]{:S(2)}) copy-start(bf16[1024,256]{1,0:T(8,128)(2,1)} %param.8) | copy-start | bytes 1572868
  44.4 17.8 %collective-permute-start = (bf16[2,192,1024]{2,1,0:T(8,128)(2,1)}, bf16[2,192,1024]{2,1,0:T(8,128)(2,1)S(1)}, u32[]{:S(2)}, u32[]{:S(2)}) collective-permute-start(bf16[2,192,1024]{2,1,0:T(8,128)(2,1)} %constant_dynamic-update-slice_fusion), channel_id=1, source_target_pairs={{0,8},{8,16},{16,24},{24,0},{1,9},{9,17},{17,25},{25,1},{2,10},{10... | collective-permute-start | bytes 2359304 | tf_op jit(solution)/shard_map/ppermute | solution.py:62
  46.8 18.3 %collective-permute-start.1 = (bf16[2,192,1024]{2,1,0:T(8,128)(2,1)}, bf16[2,192,1024]{2,1,0:T(8,128)(2,1)S(1)}, u32[]{:S(2)}, u32[]{:S(2)}) collective-permute-start(bf16[2,192,1024]{2,1,0:T(8,128)(2,1)} %constant_dynamic-update-slice_fusion), channel_id=1, source_target_pairs={{0,24},{8,0},{16,8},{24,16},{1,25},{9,1},{17,9},{25,17},{2,26},{10... | collective-permute-start | bytes 2359304 | tf_op jit(solution)/shard_map/ppermute | solution.py:63
  62.3 11.4 %copy-start.10 = (bf16[192,1024]{1,0:T(8,128)(2,1)}, bf16[192,1024]{1,0:T(8,128)(2,1)S(1)}, u32[]{:S(2)}) copy-start(bf16[192,1024]{1,0:T(8,128)(2,1)S(1)} %get-tuple-element.13) | copy-start | bytes 1179652
  62.3 13.8 %copy-start.6 = (bf16[192,1024]{1,0:T(8,128)(2,1)}, bf16[192,1024]{1,0:T(8,128)(2,1)S(1)}, u32[]{:S(2)}) copy-start(bf16[192,1024]{1,0:T(8,128)(2,1)S(1)} %get-tuple-element.14) | copy-start | bytes 1179652
  62.3 9.8 %collective-permute-start.2 = (bf16[192,1024]{1,0:T(8,128)(2,1)S(1)}, bf16[192,1024]{1,0:T(8,128)(2,1)}, u32[]{:S(2)}, u32[]{:S(2)}) collective-permute-start(bf16[192,1024]{1,0:T(8,128)(2,1)S(1)} %get-tuple-element.13), channel_id=1, source_target_pairs={{0,8},{8,16},{16,24},{24,0},{1,9},{9,17},{17,25},{25,1},{2,10},{10... | collective-permute-start | bytes 1179656 | tf_op jit(solution)/shard_map/ppermute | solution.py:64
  64.9 8.9 %copy-start.4 = (bf16[192,1024]{1,0:T(8,128)(2,1)}, bf16[192,1024]{1,0:T(8,128)(2,1)S(1)}, u32[]{:S(2)}) copy-start(bf16[192,1024]{1,0:T(8,128)(2,1)S(1)} %squeeze_stack_reshape.6) | copy-start | bytes 1179652
  65.1 11.0 %copy-start.2 = (bf16[192,1024]{1,0:T(8,128)(2,1)}, bf16[192,1024]{1,0:T(8,128)(2,1)S(1)}, u32[]{:S(2)}) copy-start(bf16[192,1024]{1,0:T(8,128)(2,1)S(1)} %squeeze_stack_reshape.7) | copy-start | bytes 1179652
  65.2 8.6 %copy-start.13 = (bf16[192,1024]{1,0:T(8,128)(2,1)}, bf16[192,1024]{1,0:T(8,128)(2,1)S(1)}, u32[]{:S(2)}) copy-start(bf16[192,1024]{1,0:T(8,128)(2,1)S(1)} %get-tuple-element.11) | copy-start | bytes 1179652
  65.2 10.9 %copy-start.8 = (bf16[192,1024]{1,0:T(8,128)(2,1)}, bf16[192,1024]{1,0:T(8,128)(2,1)S(1)}, u32[]{:S(2)}) copy-start(bf16[192,1024]{1,0:T(8,128)(2,1)S(1)} %get-tuple-element.12) | copy-start | bytes 1179652
  65.2 10.9 %collective-permute-start.3 = (bf16[192,1024]{1,0:T(8,128)(2,1)S(1)}, bf16[192,1024]{1,0:T(8,128)(2,1)S(1)}, u32[]{:S(2)}, u32[]{:S(2)}) collective-permute-start(bf16[192,1024]{1,0:T(8,128)(2,1)S(1)} %get-tuple-element.12), channel_id=1, source_target_pairs={{0,24},{8,0},{16,8},{24,16},{1,25},{9,1},{17,9},{25,17},{2,26},{10... | collective-permute-start | bytes 1179656 | tf_op jit(solution)/shard_map/ppermute | solution.py:65
  72.1 1.7 copy-start.1
  73.8 2.3 %copy-start.17 = (bf16[256,1024]{1,0:T(8,128)(2,1)S(1)}, bf16[256,1024]{1,0:T(8,128)(2,1)}, u32[]{:S(2)}) copy-start(bf16[256,1024]{1,0:T(8,128)(2,1)} %param.10) | copy-start | bytes 1572868
  76.1 0.8 copy-start.18
  84.0 6.9 %copy-start.16 = (s32[12,2]{0,1:T(2,128)S(1)}, s32[12,2]{0,1:T(2,128)}, u32[]{:S(2)}) copy-start(s32[12,2]{0,1:T(2,128)} %param.11) | copy-start | bytes 292
  86.4 21.3 %all-to-all-start.1 = ((f32[4,3,96,256]{3,2,1,0:T(8,128)}), f32[4,3,96,256]{3,2,1,0:T(8,128)S(1)}, u32[]{:S(2)}, u32[]{:S(2)}) async-start(f32[4,3,96,256]{3,2,1,0:T(8,128)} %copy.25), calls=%async_computation.1 | async-start | bytes 2359296 | tf_op jit(solution)/shard_map/all_to_all | solution.py:78
  124.8 22.7 %collective-permute-start.4 = (bf16[192,1024]{1,0:T(8,128)(2,1)S(1)}, bf16[192,1024]{1,0:T(8,128)(2,1)S(1)}, u32[]{:S(2)}, u32[]{:S(2)}) collective-permute-start(bf16[192,1024]{1,0:T(8,128)(2,1)S(1)} %get-tuple-element.6), channel_id=1, source_target_pairs={{0,24},{8,0},{16,8},{24,16},{1,25},{9,1},{17,9},{25,17},{2,26},{10... | collective-permute-start | bytes 1179656 | tf_op jit(solution)/shard_map/ppermute | solution.py:93
  127.0 21.6 %collective-permute-start.5 = (bf16[192,1024]{1,0:T(8,128)(2,1)S(1)}, bf16[192,1024]{1,0:T(8,128)(2,1)S(1)}, u32[]{:S(2)}, u32[]{:S(2)}) collective-permute-start(bf16[192,1024]{1,0:T(8,128)(2,1)S(1)} %get-tuple-element.8), channel_id=1, source_target_pairs={{0,8},{8,16},{16,24},{24,0},{1,9},{9,17},{17,25},{25,1},{2,10},{10... | collective-permute-start | bytes 1179656 | tf_op jit(solution)/shard_map/ppermute | solution.py:93
  131.8 35.7 %copy-start.5 = (bf16[192,1024]{1,0:T(8,128)(2,1)S(1)}, bf16[192,1024]{1,0:T(8,128)(2,1)}, u32[]{:S(2)}) copy-start(bf16[192,1024]{1,0:T(8,128)(2,1)} %copy-done.4) | copy-start | bytes 1179652
  131.9 35.7 %copy-start.11 = (bf16[192,1024]{1,0:T(8,128)(2,1)S(1)}, bf16[192,1024]{1,0:T(8,128)(2,1)}, u32[]{:S(2)}) copy-start(bf16[192,1024]{1,0:T(8,128)(2,1)} %copy-done.10) | copy-start | bytes 1179652
  131.9 35.7 %copy-start.14 = (bf16[192,1024]{1,0:T(8,128)(2,1)S(1)}, bf16[192,1024]{1,0:T(8,128)(2,1)}, u32[]{:S(2)}) copy-start(bf16[192,1024]{1,0:T(8,128)(2,1)} %copy-done.13) | copy-start | bytes 1179652
  131.9 16.8 %collective-permute-start.6 = (bf16[192,1024]{1,0:T(8,128)(2,1)S(1)}, bf16[192,1024]{1,0:T(8,128)(2,1)S(1)}, u32[]{:S(2)}, u32[]{:S(2)}) collective-permute-start(bf16[192,1024]{1,0:T(8,128)(2,1)S(1)} %get-tuple-element.7), channel_id=1, source_target_pairs={{0,16},{8,24},{16,0},{24,8},{1,17},{9,25},{17,1},{25,9},{2,18},{10... | collective-permute-start | bytes 1179656 | tf_op jit(solution)/shard_map/ppermute | solution.py:93
  149.9 22.7 %all-to-all-start.2 = ((bf16[4,4,96,128]{3,2,1,0:T(8,128)(2,1)}), bf16[4,4,96,128]{3,2,1,0:T(8,128)(2,1)S(1)}, u32[]{:S(2)}, u32[]{:S(2)}) async-start(bf16[4,4,96,128]{3,2,1,0:T(8,128)(2,1)} %bitcast.39), calls=%async_computation.2 | async-start | bytes 786432 | tf_op jit(solution)/shard_map/all_to_all | solution.py:96
  167.6 2.5 %copy-start.12 = (bf16[192,1024]{1,0:T(8,128)(2,1)S(1)}, bf16[192,1024]{1,0:T(8,128)(2,1)}, u32[]{:S(2)}) copy-start(bf16[192,1024]{1,0:T(8,128)(2,1)} %copy-done.10) | copy-start | bytes 1179652
  167.6 2.5 %copy-start.15 = (bf16[192,1024]{1,0:T(8,128)(2,1)S(1)}, bf16[192,1024]{1,0:T(8,128)(2,1)}, u32[]{:S(2)}) copy-start(bf16[192,1024]{1,0:T(8,128)(2,1)} %copy-done.13) | copy-start | bytes 1179652
  170.1 9.8 %copy-start.3 = (bf16[192,1024]{1,0:T(8,128)(2,1)S(1)}, bf16[192,1024]{1,0:T(8,128)(2,1)}, u32[]{:S(2)}) copy-start(bf16[192,1024]{1,0:T(8,128)(2,1)} %copy-done.2) | copy-start | bytes 1179652
  170.1 9.8 %copy-start.7 = (bf16[192,1024]{1,0:T(8,128)(2,1)S(1)}, bf16[192,1024]{1,0:T(8,128)(2,1)}, u32[]{:S(2)}) copy-start(bf16[192,1024]{1,0:T(8,128)(2,1)} %copy-done.6) | copy-start | bytes 1179652
  170.1 9.8 %copy-start.9 = (bf16[192,1024]{1,0:T(8,128)(2,1)S(1)}, bf16[192,1024]{1,0:T(8,128)(2,1)}, u32[]{:S(2)}) copy-start(bf16[192,1024]{1,0:T(8,128)(2,1)} %copy-done.8) | copy-start | bytes 1179652
  173.3 22.4 %all-to-all-start.3 = ((bf16[4,96,128]{2,1,0:T(8,128)(2,1)}), bf16[4,96,128]{2,1,0:T(8,128)(2,1)S(1)}, u32[]{:S(2)}, u32[]{:S(2)}) async-start(bf16[4,96,128]{2,1,0:T(8,128)(2,1)} %reduce_sum.62), calls=%async_computation.3 | async-start | bytes 196608 | tf_op jit(solution)/shard_map/all_to_all | solution.py:97

commit v2 on v1

v2 whole, which is shorter than its diff:
```python
import functools

import jax
import jax.numpy as jnp
from jax import lax
from jax.experimental import pallas as pl
from jax.experimental.pallas import tpu as pltpu
from jax.sharding import Mesh, PartitionSpec as P

F32, BF16 = jnp.float32, jnp.bfloat16
INNER = (((1,), (1,)), ((), ()))
PLAIN = (((1,), (0,)), ((), ()))
OUTER = (((0,), (0,)), ((), ()))


def ring(size, step):
    return [(i, (i + step) % size) for i in range(size)]


def dot(a, b, dims):
    return lax.dot_general(a, b, dims, preferred_element_type=F32)


def pointwise_parts(gate_pre, up_pre, grad_hidden, keep_rows):
    sigmoid_gate = jax.nn.sigmoid(gate_pre)
    silu_gate = gate_pre * sigmoid_gate
    hidden_kept = (silu_gate * up_pre * keep_rows).astype(BF16)
    slope = sigmoid_gate * (1.0 + gate_pre * (1.0 - sigmoid_gate))
    grad_gate_pre = (grad_hidden * up_pre * slope).astype(BF16)
    grad_up_pre = (grad_hidden * silu_gate).astype(BF16)
    return hidden_kept, grad_gate_pre, grad_up_pre


def keep_of_rows(keep_mask, rows, own_tokens, nx, total):
    tiles, blocks = keep_mask.shape
    chunk = lax.axis_index("y")
    inside = lax.axis_index("c") * rows + lax.broadcasted_iota(jnp.int32, (rows, 1), 0)
    shift = jnp.where(chunk == 1, -1, jnp.where(chunk == 2, 1, jnp.where(chunk == 3, 2, 0)))
    from_x = (lax.axis_index("x") + shift + nx) % nx
    token = (inside // own_tokens * nx + from_x) * own_tokens + inside % own_tokens
    tile = token // (total // tiles)
    chosen = tile == lax.broadcasted_iota(jnp.int32, (rows, tiles), 1)
    keep = [
        jnp.sum(jnp.where(chosen, keep_mask[:, b][None, :], 0), axis=1, keepdims=True)
        for b in range(blocks)
    ]
    return jnp.concatenate([jnp.broadcast_to(k, (rows, 128)) for k in keep], axis=1).astype(F32)


def forward_kernel(rows, x_ref, c_ref, wg_ref, wu_ref, wd_ref, *rest):
    out_ref = rest[-1]
    x, c = x_ref[...], c_ref[...]
    for place, value in enumerate(
        (dot(x, wg_ref[...], PLAIN), dot(x, wu_ref[...], PLAIN), dot(c, wd_ref[...], INNER))
    ):
        out_ref[0, place] = value[:rows]
        out_ref[1, place] = value[rows:]


def forward(chunk, x, c, weights, held, chunks):
    tokens, width = x.shape[-2:]
    hidden = weights[0].shape[1]
    rows = tokens // 2

    def half(a, which):
        if a.ndim == 2:
            return pl.BlockSpec((tokens, width), lambda i: (0, 0))
        return pl.BlockSpec((None, tokens, width), lambda i: (which, 0, 0))

    whole = [pl.BlockSpec(w.shape, lambda i: (0, 0)) for w in weights]
    operands, specs, alias = [x, c, *weights], [half(x, 0), half(c, 1), *whole], {}
    if held is not None:
        operands.append(held)
        specs.append(pl.BlockSpec(memory_space=pl.ANY))
        alias = {5: 0}
    return pl.pallas_call(
        functools.partial(forward_kernel, rows),
        out_shape=jax.ShapeDtypeStruct((2, chunks, 3, rows, hidden), F32),
        grid=(1,),
        in_specs=specs,
        out_specs=pl.BlockSpec((2, None, 3, rows, hidden), lambda i: (0, chunk, 0, 0, 0)),
        input_output_aliases=alias,
        compiler_params=pltpu.CompilerParams(vmem_limit_bytes=32 << 20),
        cost_estimate=pl.CostEstimate(
            flops=6 * tokens * width * hidden,
            bytes_accessed=4 * tokens * width + 6 * width * hidden + 12 * tokens * hidden,
            transcendentals=0,
        ),
        name="forward_chunk",
    )(*operands)


def input_grad_kernel(x_index, g_ref, wg_ref, wu_ref, out_ref):
    tokens = out_ref.shape[0]
    hidden = g_ref.shape[-1]
    grad_gate, grad_up = (g_ref[:, i].reshape(tokens, hidden) for i in range(2))
    total = dot(grad_gate, wg_ref[...], INNER) + dot(grad_up, wu_ref[...], INNER)
    out_ref[...] = total.astype(out_ref.dtype)


def input_grad(both, w_gate, w_up, chunks):
    parts, _, rows, hidden = both.shape
    width = w_gate.shape[0]
    tokens = parts * rows // chunks
    place = jnp.array([0, 2, 3, 1], jnp.int32)
    x = lax.axis_index("x")
    order = jnp.stack([place[(d - x + chunks) % chunks] for d in range(chunks)])
    whole = pl.BlockSpec((width, hidden), lambda d, order: (0, 0))
    return pl.pallas_call(
        input_grad_kernel,
        out_shape=jax.ShapeDtypeStruct((chunks, tokens, width), BF16),
        grid_spec=pltpu.PrefetchScalarGridSpec(
            num_scalar_prefetch=1,
            grid=(chunks,),
            in_specs=[
                pl.BlockSpec(
                    (parts // chunks, 2, rows, hidden), lambda d, order: (order[d], 0, 0, 0)
                ),
                whole,
                whole,
            ],
            out_specs=pl.BlockSpec((None, tokens, width), lambda d, order: (d, 0, 0)),
        ),
        compiler_params=pltpu.CompilerParams(vmem_limit_bytes=32 << 20),
        cost_estimate=pl.CostEstimate(
            flops=4 * chunks * tokens * width * hidden,
            bytes_accessed=4 * chunks * tokens * hidden + 4 * width * hidden + 2 * chunks * tokens * width,
            transcendentals=0,
        ),
        name="input_grad",
    )(order, both, w_gate, w_up)


def shards(inputs, cotangent, w_gate, w_up, w_down, keep_mask):
    own_tokens, width = inputs.shape
    hidden = w_gate.shape[1]
    nz, nx, nc = 16, 4, 2
    total = own_tokens * nz * nx
    tokens = own_tokens * nz
    rows = tokens // nc
    flat = own_tokens * width // 128
    weights = (w_gate, w_up, w_down)

    packed = jnp.concatenate([inputs.reshape(flat, 128), cotangent.reshape(flat, 128)])
    along_z = lax.all_gather(packed, "z")
    own = jnp.stack(
        [along_z[:, i * flat : (i + 1) * flat].reshape(tokens, width) for i in range(2)]
    )
    right = lax.ppermute(own, "x", ring(nx, 1))
    left = lax.ppermute(own, "x", ring(nx, -1))
    far_in = lax.ppermute(right[0], "x", ring(nx, 1))
    far_cot = lax.ppermute(left[1], "x", ring(nx, -1))

    parts = forward(0, own, own, weights, None, nx)
    parts = forward(1, right, right, weights, parts, nx)
    parts = forward(2, left, left, weights, parts, nx)
    parts = forward(3, far_in, far_cot, weights, parts, nx)

    summed = jnp.sum(lax.all_to_all(parts, "c", 0, 0), axis=0)
    summed = jnp.sum(lax.all_to_all(summed, "y", 0, 0), axis=0)
    keep_rows = keep_of_rows(keep_mask, rows, own_tokens, nx, total)
    hidden_kept, grad_gate_pre, grad_up_pre = pointwise_parts(
        summed[0], summed[1], summed[2], keep_rows
    )
    both = lax.all_gather(jnp.stack([grad_gate_pre, grad_up_pre]), ("y", "c"))

    result = input_grad(both, w_gate, w_up, nx)
    result, hidden_kept = lax.optimization_barrier((result, hidden_kept))
    arrived = lax.all_to_all(result, "x", 0, 0)
    all_kept = lax.all_gather(hidden_kept, ("y", "c")).reshape(total, hidden)
    all_inputs = jnp.concatenate([own[0], right[0], left[0], far_in])
    all_cotangent = jnp.concatenate([own[1], right[1], left[1], far_cot])
    arrived, all_kept, all_inputs, all_cotangent = lax.optimization_barrier(
        (arrived, all_kept, all_inputs, all_cotangent)
    )
    kept = jnp.sum(arrived.astype(F32), axis=0).astype(BF16).reshape(nz, flat, 128)
    kept, all_kept, all_inputs, all_cotangent, both = lax.optimization_barrier(
        (kept, all_kept, all_inputs, all_cotangent, both)
    )
    kept = jnp.sum(lax.all_to_all(kept, "z", 0, 0).astype(F32), axis=0).astype(BF16)
    grad_input = kept.reshape(own_tokens, width)

    all_gate = both[:, 0].reshape(total, hidden)
    all_up = both[:, 1].reshape(total, hidden)
    grad_down = dot(all_kept, all_cotangent, OUTER).astype(BF16)
    grad_gate = dot(all_inputs, all_gate, OUTER).astype(BF16)
    grad_up = dot(all_inputs, all_up, OUTER).astype(BF16)
    return grad_input, grad_gate, grad_up, grad_down


def solution(mesh):
    fine = Mesh(mesh.devices.reshape(16, 4, 4, 2), ("z", "x", "y", "c"))
    hid, mdl = ("z", "x"), ("y", "c")
    placed = (P(hid, mdl), P(hid, mdl), P(mdl, hid), P(mdl, hid), P(hid, mdl), P(None, hid))
    return jax.shard_map(
        shards,
        mesh=fine,
        in_specs=placed,
        out_specs=(P(hid, mdl), P(mdl, hid), P(mdl, hid), P(hid, mdl)),
        check_vma=False,
    )
```

time: 199 us -> 185 us (0.930)
  waiting for transfers between devices: 60.9 us -> 50.6 us
  other arithmetic: 2.84 us -> 12.8 us
  matrix products: 12.5 us -> 4.23 us
  starting transfers between devices: 35.2 us -> 27.6 us
  Pallas kernels: 0 us -> 5.77 us
  blocking collectives: 75.4 us -> 73.1 us
    ppermute x3 -> x0, waiting for transfers between devices: 14.7 us -> none  [shards(): lax.ppermute(result[k], 'x', ring(nx, ALONG_X[k]))]
    ppermute x3 -> x0, starting transfers between devices: 9.11 us -> none  [shards(): lax.ppermute(result[k], 'x', ring(nx, ALONG_X[k]))]
    dot_general x8 -> x3, matrix products: 12.5 us -> 4.23 us  [dot(): return lax.dot_general(a, b, dims, preferred_element_type=F32)]
    all_to_all x2, waiting for transfers between devices: 13.5 us -> 20.4 us  [the longest x1 18.7 us: shards(): lax.all_to_all(kept, 'z', 0, 0).astype(F32)]
    pallas_call x0 -> x5, Pallas kernels: none -> 5.77 us  [the longest x1 3.59 us: input_grad(): pl.pallas_call(input_grad_kernel, out_shape=jax.ShapeDtypeStruct((chunks,...]
    ppermute x1, waiting for transfers between devices: 0.63 us -> 4.4 us  [shards(): far_cot = lax.ppermute(left[1], 'x', ring(nx, -1))]
    concatenate x0 -> x2, other arithmetic: none -> 3.76 us  [the longest x1 2.46 us: shards(): all_inputs = jnp.concatenate([own[0], right[0], left[0], far_in])]
    all_gather x5 -> x3, blocking collectives: 69.7 us -> 66.6 us  [the longest x1 40.1 us: shards(): along_z = lax.all_gather(packed, 'z')]
  transfers between devices with their start and end apart: 10 -> 7, of which waited for: 7 -> 6; matrix products, arithmetic and copies ran while one was open for 6% -> 8% of each run, Pallas kernels for 0% -> 1%
where the time goes in v2:
time: 185 us; the launch traced here: 183 us
  blocking collectives  73.1 us (40%)
  waiting for transfers between devices  50.6 us (27%)
  starting transfers between devices  27.6 us (15%)
  other arithmetic  12.8 us (7%)
  local copies, waits for them, and re-layouts  7.87 us (4%)
  Pallas kernels  5.77 us (3%)
  matrix products  4.23 us (2%)
    all_gather x1, blocking collectives, shards(): along_z = lax.all_gather(packed, 'z')  40.1 us
    all_to_all x1, waiting for transfers between devices, shards(): lax.all_to_all(kept, 'z', 0, 0).astype(F32)  18.7 us
    all_to_all x1, waiting for transfers between devices, shards(): summed = jnp.sum(lax.all_to_all(summed, 'y', 0, 0), axis=0)  13.5 us
    all_gather x1, blocking collectives, shards(): both = lax.all_gather(jnp.stack([grad_gate_pre, grad_up_pre]), ('y', 'c'))  13.5 us
    all_gather x1, blocking collectives, shards(): all_kept = lax.all_gather(hidden_kept, ('y', 'c')).reshape(total, hidden)  13 us
    ppermute x1, waiting for transfers between devices, shards(): right = lax.ppermute(own, 'x', ring(nx, 1))  11.1 us
    all_to_all x1, starting transfers between devices, shards(): lax.all_to_all(kept, 'z', 0, 0).astype(F32)  6.65 us
    all_to_all x1, blocking collectives, shards(): summed = jnp.sum(lax.all_to_all(parts, 'c', 0, 0), axis=0)  6.55 us
  transfers between devices with their start and end apart: 7, of which 6 were waited for; matrix products, arithmetic and copies ran while one was open for 8% of the time, Pallas kernels for 1%

profile of v2, /device:TPU:6, one launch (start us, length us, event | category | flops | bytes accessed | tf_op | source)
XLA Modules:
  0.0 183.0 jit_solution(11673308471385086314)
XLA Ops:
  1.4 0.8 reshape.99
  2.2 40.1 %all-gather = bf16[3072,128]{1,0:T(8,128)(2,1)S(1)} all-gather(bf16[192,128]{1,0:T(8,128)(2,1)S(1)} %pad_maximum_fusion.3), channel_id=2, replica_groups=mesh['z'=16,'x'=4,'y'=4,'c'=2] {'z'}, dimensions={0}, use_global_device_ids=true | all-gather | bytes 835584 | tf_op jit(solution)/shard_map/all_gather | solution.py:145
  42.9 2.5 %collective-permute-start = (bf16[2,192,1024]{2,1,0:T(8,128)(2,1)S(1)}, bf16[2,192,1024]{2,1,0:T(8,128)(2,1)S(1)}, u32[]{:S(2)}, u32[]{:S(2)}) collective-permute-start(bf16[2,192,1024]{2,1,0:T(8,128)(2,1)S(1)} %constant_dynamic-update-slice_fusion.x_ref.c_ref), channel_id=1, source_target_pairs={{0,8},{8,16},{16,24},{24,0},{1,9},{9,17},{17,25},{25,1},{2,10},{10... | collective-permute-start | bytes 2359304 | tf_op jit(solution)/shard_map/ppermute | solution.py:149
  45.4 3.5 %collective-permute-start.2 = (bf16[2,192,1024]{2,1,0:T(8,128)(2,1)S(1)}, bf16[2,192,1024]{2,1,0:T(8,128)(2,1)S(1)}, u32[]{:S(2)}, u32[]{:S(2)}) collective-permute-start(bf16[2,192,1024]{2,1,0:T(8,128)(2,1)S(1)} %constant_dynamic-update-slice_fusion.x_ref.c_ref), channel_id=1, source_target_pairs={{0,24},{8,0},{16,8},{24,16},{1,25},{9,1},{17,9},{25,17},{2,26},{10... | collective-permute-start | bytes 2359304 | tf_op jit(solution)/shard_map/ppermute | solution.py:150
  48.9 11.1 %collective-permute-done.x_ref.c_ref = bf16[2,192,1024]{2,1,0:T(8,128)(2,1)S(1)} collective-permute-done((bf16[2,192,1024]{2,1,0:T(8,128)(2,1)S(1)}, bf16[2,192,1024]{2,1,0:T(8,128)(2,1)S(1)}, u32[]{:S(2)}, u32[]{:S(2)}) %collective-permute-start) | collective-permute-done | bytes 786464 | tf_op jit(solution)/shard_map/ppermute | solution.py:149
  59.9 0.8 slice_bitcast_fusion
  60.7 2.4 %collective-permute-start.1 = (bf16[192,1024]{1,0:T(8,128)(2,1)S(1)}, bf16[192,1024]{1,0:T(8,128)(2,1)S(1)}, u32[]{:S(2)}, u32[]{:S(2)}) collective-permute-start(bf16[192,1024]{1,0:T(8,128)(2,1)S(1)} %get-tuple-element.31), channel_id=1, source_target_pairs={{0,8},{8,16},{16,24},{24,0},{1,9},{9,17},{17,25},{25,1},{2,10},{10... | collective-permute-start | bytes 1179656 | tf_op jit(solution)/shard_map/ppermute | solution.py:151
  63.1 0.8 slice_bitcast_fusion.1
  63.9 3.4 %collective-permute-start.3 = (bf16[192,1024]{1,0:T(8,128)(2,1)S(1)}, bf16[192,1024]{1,0:T(8,128)(2,1)S(1)}, u32[]{:S(2)}, u32[]{:S(2)}) collective-permute-start(bf16[192,1024]{1,0:T(8,128)(2,1)S(1)} %get-tuple-element.33), channel_id=1, source_target_pairs={{0,24},{8,0},{16,8},{24,16},{1,25},{9,1},{17,9},{25,17},{2,26},{10... | collective-permute-start | bytes 1179656 | tf_op jit(solution)/shard_map/ppermute | solution.py:152
  69.1 1.3 collective-permute-done.1.x_ref
  70.4 4.4 %collective-permute-done.3.c_ref = bf16[192,1024]{1,0:T(8,128)(2,1)S(1)} collective-permute-done((bf16[192,1024]{1,0:T(8,128)(2,1)S(1)}, bf16[192,1024]{1,0:T(8,128)(2,1)S(1)}, u32[]{:S(2)}, u32[]{:S(2)}) %collective-permute-start.3) | collective-permute-done | bytes 393248 | tf_op jit(solution)/shard_map/ppermute | solution.py:152
  75.4 6.6 %all_to_all.20 = f32[2,4,3,96,256]{4,3,2,1,0:T(8,128)} all-to-all(f32[2,4,3,96,256]{4,3,2,1,0:T(8,128)S(1)} %forward_chunk.7), channel_id=1, replica_groups=mesh['z'=16,'x'=4,'y'=4,'c'=2] {'c'}, dimensions={0} | all-to-all | bytes 4718592 | tf_op jit(solution)/shard_map/all_to_all | solution.py:159
  81.9 3.0 %reduce_sum.60 = f32[4,3,96,256]{3,2,1,0:T(8,128)} reduce(f32[2,4,3,96,256]{4,3,2,1,0:T(8,128)} %all_to_all.20, f32[]{:T(128)} %constant.84.clone.1), dimensions={0}, to_apply=%region_0.0 | reduce | flops 294912 | bytes 3538948 | tf_op jit(solution)/shard_map/reduce_sum | solution.py:159
  84.9 4.6 %all-to-all-start.1 = ((f32[4,3,96,256]{3,2,1,0:T(8,128)}), f32[4,3,96,256]{3,2,1,0:T(8,128)}, u32[]{:S(2)}, u32[]{:S(2)}) async-start(f32[4,3,96,256]{3,2,1,0:T(8,128)} %reduce_sum.60), calls=%async_computation.1 | async-start | bytes 2359296 | tf_op jit(solution)/shard_map/all_to_all | solution.py:160
  90.2 2.7 %pad_add_fusion.x_index = s32[4]{0:T(128)S(1)} fusion(s32[1]{0:T(128)} %get-tuple-element.42, s32[1]{0:T(128)} %get-tuple-element.43, s32[1]{0:T(128)} %get-tuple-element.41, s32[1]{0:T(128)} %get-tuple-element.40), kind=kLoop, calls=%fused_computation.35 | loop fusion | flops 12 | bytes 32 | tf_op jit(solution)/shard_map/stack | solution.py:107
  92.9 13.5 %all-to-all-done.1 = f32[4,3,96,256]{3,2,1,0:T(8,128)} async-done(((f32[4,3,96,256]{3,2,1,0:T(8,128)}), f32[4,3,96,256]{3,2,1,0:T(8,128)}, u32[]{:S(2)}, u32[]{:S(2)}) %all-to-all-start.1) | async-done | bytes 1179680 | tf_op jit(solution)/shard_map/all_to_all | solution.py:160
  106.4 1.4 reduce_sum.61
  108.6 13.5 %all-gather.1 = bf16[16,96,256]{2,1,0:T(8,128)(2,1)S(1)} all-gather(bf16[2,96,256]{2,1,0:T(8,128)(2,1)S(1)} %pad_maximum_fusion.2), channel_id=3, replica_groups=mesh['z'=16,'x'=4,'y'=4,'c'=2] {'y','c'}, dimensions={0}, use_global_device_ids=true | all-gather | bytes 884736 | tf_op jit(solution)/shard_map/all_gather | solution.py:165
  122.0 3.6 %input_grad.1 = bf16[4,192,1024]{2,1,0:T(8,128)(2,1)} custom-call(s32[4]{0:T(128)S(1)} %pad_add_fusion.x_index, bf16[8,2,96,256]{3,2,1,0:T(8,128)(2,1)S(1)} %bitcast.39, bf16[1024,256]{1,0:T(8,128)(2,1)S(1)} %copy-done, bf16[1024,256]{1,0:T(8,128)(2,1)S(1)} %copy-done.1), custom_call_target="tpu_custom_call" | custom-call | flops 805306368 | bytes 3407872 | tf_op jit(solution)/shard_map/input_grad/pallas_call | solution.py:109
  125.8 4.6 %all-to-all-start.2 = ((bf16[4,192,1024]{2,1,0:T(8,128)(2,1)}), bf16[4,192,1024]{2,1,0:T(8,128)(2,1)}, u32[]{:S(2)}, u32[]{:S(2)}) async-start(bf16[4,192,1024]{2,1,0:T(8,128)(2,1)} %input_grad.1), calls=%async_computation.2 | async-start | bytes 3145728 | tf_op jit(solution)/shard_map/all_to_all | solution.py:169
  130.4 0.9 squeeze_stack_reshape.6
  131.6 2.5 %pad_maximum_fusion = bf16[768,1024]{1,0:T(8,128)(2,1)} fusion(bf16[192,1024]{1,0:T(8,128)(2,1)S(1)} %collective-permute-done.1.x_ref, bf16[192,1024]{1,0:T(8,128)(2,1)} %get-tuple-element.32, bf16[192,1024]{1,0:T(8,128)(2,1)S(1)} %copy-done.9, bf16[192,1024]{1,0:T(8,128)(2,1)} %squeeze_stack_reshape.6), kind=kLoop, calls=%fused_computation | loop fusion | flops 6291456 | bytes 3145728 | tf_op jit(solution)/shard_map/concatenate | solution.py:171
  134.0 1.3 pad_maximum_fusion.1
  135.3 13.0 %all-gather.2 = bf16[768,256]{1,0:T(8,128)(2,1)S(1)} all-gather(bf16[96,256]{1,0:T(8,128)(2,1)S(1)} %fusion.1), channel_id=4, replica_groups=mesh['z'=16,'x'=4,'y'=4,'c'=2] {'y','c'}, dimensions={0}, use_global_device_ids=true | all-gather | bytes 442368 | tf_op jit(solution)/shard_map/all_gather | solution.py:170
  148.3 1.7 all-to-all-done.2
  150.0 1.7 reduce_sum.64
  151.7 0.9 reshape.102
  152.6 6.6 %all-to-all-start.3 = ((bf16[16,96,128]{2,1,0:T(8,128)(2,1)}), bf16[16,96,128]{2,1,0:T(8,128)(2,1)S(1)}, u32[]{:S(2)}, u32[]{:S(2)}) async-start(bf16[16,96,128]{2,1,0:T(8,128)(2,1)} %reshape.102), calls=%async_computation.3 | async-start | bytes 786432 | tf_op jit(solution)/shard_map/all_to_all | solution.py:180
  159.3 1.4 convolution_convert_fusion.1
  160.7 1.4 convolution_convert_fusion.2
  162.2 1.4 convolution_convert_fusion
  163.6 18.7 %all-to-all-done.3 = bf16[16,96,128]{2,1,0:T(8,128)(2,1)S(1)} async-done(((bf16[16,96,128]{2,1,0:T(8,128)(2,1)}), bf16[16,96,128]{2,1,0:T(8,128)(2,1)S(1)}, u32[]{:S(2)}, u32[]{:S(2)}) %all-to-all-start.3) | async-done | bytes 393248 | tf_op jit(solution)/shard_map/all_to_all | solution.py:180
  (53 shorter events, 6.1 us)
Async XLA Ops:
  42.8 24.5 %copy-start = (bf16[1024,256]{1,0:T(8,128)(2,1)S(1)}, bf16[1024,256]{1,0:T(8,128)(2,1)}, u32[]{:S(2)}) copy-start(bf16[1024,256]{1,0:T(8,128)(2,1)} %wg_ref.9) | copy-start | bytes 1572868
  42.9 24.5 %copy-start.1 = (bf16[1024,256]{1,0:T(8,128)(2,1)S(1)}, bf16[1024,256]{1,0:T(8,128)(2,1)}, u32[]{:S(2)}) copy-start(bf16[1024,256]{1,0:T(8,128)(2,1)} %wu_ref.9) | copy-start | bytes 1572868
  42.9 24.5 %copy-start.2 = (bf16[256,1024]{1,0:T(8,128)(2,1)S(1)}, bf16[256,1024]{1,0:T(8,128)(2,1)}, u32[]{:S(2)}) copy-start(bf16[256,1024]{1,0:T(8,128)(2,1)} %wd_ref.7) | copy-start | bytes 1572868
  42.9 17.1 %collective-permute-start = (bf16[2,192,1024]{2,1,0:T(8,128)(2,1)S(1)}, bf16[2,192,1024]{2,1,0:T(8,128)(2,1)S(1)}, u32[]{:S(2)}, u32[]{:S(2)}) collective-permute-start(bf16[2,192,1024]{2,1,0:T(8,128)(2,1)S(1)} %constant_dynamic-update-slice_fusion.x_ref.c_ref), channel_id=1, source_target_pairs={{0,8},{8,16},{16,24},{24,0},{1,9},{9,17},{17,25},{25,1},{2,10},{10... | collective-permute-start | bytes 2359304 | tf_op jit(solution)/shard_map/ppermute | solution.py:149
  45.4 17.7 %collective-permute-start.2 = (bf16[2,192,1024]{2,1,0:T(8,128)(2,1)S(1)}, bf16[2,192,1024]{2,1,0:T(8,128)(2,1)S(1)}, u32[]{:S(2)}, u32[]{:S(2)}) collective-permute-start(bf16[2,192,1024]{2,1,0:T(8,128)(2,1)S(1)} %constant_dynamic-update-slice_fusion.x_ref.c_ref), channel_id=1, source_target_pairs={{0,24},{8,0},{16,8},{24,16},{1,25},{9,1},{17,9},{25,17},{2,26},{10... | collective-permute-start | bytes 2359304 | tf_op jit(solution)/shard_map/ppermute | solution.py:150
  60.7 7.2 %copy-start.8 = (bf16[192,1024]{1,0:T(8,128)(2,1)}, bf16[192,1024]{1,0:T(8,128)(2,1)S(1)}, u32[]{:S(2)}) copy-start(bf16[192,1024]{1,0:T(8,128)(2,1)S(1)} %get-tuple-element.31) | copy-start | bytes 1179652
  60.7 9.7 %collective-permute-start.1 = (bf16[192,1024]{1,0:T(8,128)(2,1)S(1)}, bf16[192,1024]{1,0:T(8,128)(2,1)S(1)}, u32[]{:S(2)}, u32[]{:S(2)}) collective-permute-start(bf16[192,1024]{1,0:T(8,128)(2,1)S(1)} %get-tuple-element.31), channel_id=1, source_target_pairs={{0,8},{8,16},{16,24},{24,0},{1,9},{9,17},{17,25},{25,1},{2,10},{10... | collective-permute-start | bytes 1179656 | tf_op jit(solution)/shard_map/ppermute | solution.py:151
  63.9 4.1 %copy-start.10 = (bf16[192,1024]{1,0:T(8,128)(2,1)}, bf16[192,1024]{1,0:T(8,128)(2,1)S(1)}, u32[]{:S(2)}) copy-start(bf16[192,1024]{1,0:T(8,128)(2,1)S(1)} %get-tuple-element.33) | copy-start | bytes 1179652
  63.9 10.9 %collective-permute-start.3 = (bf16[192,1024]{1,0:T(8,128)(2,1)S(1)}, bf16[192,1024]{1,0:T(8,128)(2,1)S(1)}, u32[]{:S(2)}, u32[]{:S(2)}) collective-permute-start(bf16[192,1024]{1,0:T(8,128)(2,1)S(1)} %get-tuple-element.33), channel_id=1, source_target_pairs={{0,24},{8,0},{16,8},{24,16},{1,25},{9,1},{17,9},{25,17},{2,26},{10... | collective-permute-start | bytes 1179656 | tf_op jit(solution)/shard_map/ppermute | solution.py:152
  84.9 4.6 %copy-start.12 = (s32[4]{0:T(128)S(1)}, s32[4]{0:T(128)}, u32[]{:S(2)}) copy-start(s32[4]{0:T(128)} %constant.94.clone) | copy-start | bytes 52
  84.9 7.9 %copy-start.13 = (s32[12,2]{0,1:T(2,128)S(1)}, s32[12,2]{0,1:T(2,128)}, u32[]{:S(2)}) copy-start(s32[12,2]{0,1:T(2,128)} %param.12) | copy-start | bytes 292
  84.9 21.5 %all-to-all-start.1 = ((f32[4,3,96,256]{3,2,1,0:T(8,128)}), f32[4,3,96,256]{3,2,1,0:T(8,128)}, u32[]{:S(2)}, u32[]{:S(2)}) async-start(f32[4,3,96,256]{3,2,1,0:T(8,128)} %reduce_sum.60), calls=%async_computation.1 | async-start | bytes 2359296 | tf_op jit(solution)/shard_map/all_to_all | solution.py:160
  107.8 0.7 copy-start.3
  122.0 3.7 %copy-start.4 = (f32[3,96,256]{2,1,0:T(8,128)S(1)}, f32[3,96,256]{2,1,0:T(8,128)}, u32[]{:S(2)}) copy-start(f32[3,96,256]{2,1,0:T(8,128)} %copy-done.3) | copy-start | bytes 884740
  125.8 24.1 %all-to-all-start.2 = ((bf16[4,192,1024]{2,1,0:T(8,128)(2,1)}), bf16[4,192,1024]{2,1,0:T(8,128)(2,1)}, u32[]{:S(2)}, u32[]{:S(2)}) async-start(bf16[4,192,1024]{2,1,0:T(8,128)(2,1)} %input_grad.1), calls=%async_computation.2 | async-start | bytes 3145728 | tf_op jit(solution)/shard_map/all_to_all | solution.py:169
  130.4 1.1 copy-start.9
  131.5 2.5 %copy-start.7 = (bf16[192,1024]{1,0:T(8,128)(2,1)S(1)}, bf16[192,1024]{1,0:T(8,128)(2,1)}, u32[]{:S(2)}) copy-start(bf16[192,1024]{1,0:T(8,128)(2,1)} %get-tuple-element.30) | copy-start | bytes 1179652
  131.6 2.5 %copy-start.11 = (bf16[192,1024]{1,0:T(8,128)(2,1)S(1)}, bf16[192,1024]{1,0:T(8,128)(2,1)}, u32[]{:S(2)}) copy-start(bf16[192,1024]{1,0:T(8,128)(2,1)} %copy-done.10) | copy-start | bytes 1179652
  151.7 7.6 %copy-start.5 = (bf16[768,1024]{1,0:T(8,128)(2,1)S(1)}, bf16[768,1024]{1,0:T(8,128)(2,1)}, u32[]{:S(2)}) copy-start(bf16[768,1024]{1,0:T(8,128)(2,1)} %pad_maximum_fusion) | copy-start | bytes 4718596
  152.6 29.7 %all-to-all-start.3 = ((bf16[16,96,128]{2,1,0:T(8,128)(2,1)}), bf16[16,96,128]{2,1,0:T(8,128)(2,1)S(1)}, u32[]{:S(2)}, u32[]{:S(2)}) async-start(bf16[16,96,128]{2,1,0:T(8,128)(2,1)} %reshape.102), calls=%async_computation.3 | async-start | bytes 786432 | tf_op jit(solution)/shard_map/all_to_all | solution.py:180
  160.7 1.4 copy-start.6

commit v3 on v2

v3 whole, which is shorter than its diff:
```python
import functools

import jax
import jax.numpy as jnp
from jax import lax
from jax.experimental import pallas as pl
from jax.experimental.pallas import tpu as pltpu
from jax.sharding import Mesh, PartitionSpec as P

F32, BF16, I16 = jnp.float32, jnp.bfloat16, jnp.int16
INNER = (((1,), (1,)), ((), ()))
PLAIN = (((1,), (0,)), ((), ()))
OUTER = (((0,), (0,)), ((), ()))
SUMS = 3
SCALES = 16
PARAMS = pltpu.CompilerParams(vmem_limit_bytes=32 << 20)


def ring(size, step):
    return [(i, (i + step) % size) for i in range(size)]


def dot(a, b, dims):
    return lax.dot_general(a, b, dims, preferred_element_type=F32)


def cost(flops, moved):
    return pl.CostEstimate(flops=flops, bytes_accessed=moved, transcendentals=0)


def row_is_lane(rows, lanes):
    shape = (rows, lanes)
    return lax.broadcasted_iota(jnp.int32, shape, 0) == lax.broadcasted_iota(jnp.int32, shape, 1)


def code(values):
    rows, lanes = values[0].shape
    diagonal = row_is_lane(rows, lanes)
    place = lax.broadcasted_iota(jnp.int32, (SCALES, lanes), 0)
    codes, tile = [], jnp.zeros((SCALES, lanes), F32)
    for k, v in enumerate(values):
        most = jnp.max(jnp.abs(v), axis=1, keepdims=True)
        exponent = jnp.ceil(jnp.log2(jnp.maximum(most, 1e-30)) + 0.01)
        codes.append(jnp.round(v * jnp.exp2(15.0 - exponent)).astype(jnp.int32).astype(I16))
        along = jnp.sum(jnp.where(diagonal, exponent, 0.0), axis=0, keepdims=True)
        tile = jnp.where(place == k, along, tile)
    return codes, tile.astype(jnp.int32).astype(I16)


def decode(block, rows):
    lanes = block.shape[1]
    diagonal = row_is_lane(rows, lanes)
    tile = jnp.exp2(block[SUMS * rows :].astype(jnp.int32).astype(F32) - 15.0)
    out = []
    for k in range(SUMS):
        scale = jnp.sum(jnp.where(diagonal, tile[k : k + 1], 0.0), axis=1, keepdims=True)
        out.append(block[k * rows : (k + 1) * rows].astype(jnp.int32).astype(F32) * scale)
    return out


def put(out_ref, index, values, rows):
    codes, tile = code(values)
    for k, c in enumerate(codes):
        out_ref[(*index, pl.ds(k * rows, rows))] = c
    out_ref[(*index, pl.ds(SUMS * rows, SCALES))] = tile


def unpack_kernel(packed_ref, out_ref):
    blocks = packed_ref.shape[0]
    width = out_ref.shape[2]
    half = width // 2
    for first in range(0, blocks, 2):
        pair = [packed_ref[first + i].astype(F32) for i in range(2)]
        for which in range(2):
            part = [p[which * 8 : which * 8 + 8] for p in pair]
            out_ref[which, first * 8 : first * 8 + 16] = jnp.concatenate(
                [p[:, :width] for p in part]
            ).astype(BF16)
    for first in range(0, blocks, 4):
        four = [packed_ref[first + i, :, width:].astype(F32) for i in range(4)]
        for which in range(2):
            part = [p[which * 8 : which * 8 + 8] for p in four]
            rows = jnp.concatenate(
                [
                    jnp.concatenate([p[:4] for p in part]),
                    jnp.concatenate([p[4:] for p in part]),
                ],
                axis=1,
            )
            out_ref[which, blocks * 8 + first * 4 : blocks * 8 + first * 4 + 16] = rows.astype(BF16)


def pack(a):
    half = a.shape[1] // 2
    return jnp.concatenate([a[:8], jnp.concatenate([a[8:, :half], a[8:, half:]])], axis=1)


def forward_kernel(rows, x_ref, c_ref, wg_ref, wu_ref, wd_ref, *rest):
    out_ref = rest[-1]
    x, c = x_ref[...], c_ref[...]
    values = [
        dot(x, wg_ref[...], PLAIN),
        dot(x, wu_ref[...], PLAIN),
        dot(c, wd_ref[...], INNER),
    ]
    for core in range(2):
        put(out_ref, (core,), [v[core * rows : (core + 1) * rows] for v in values], rows)


def forward(chunk, x, c, weights, held, chunks):
    tokens, width = x.shape[-2:]
    hidden = weights[0].shape[1]
    rows = tokens // 2

    def half(a, which):
        if a.ndim == 2:
            return pl.BlockSpec((tokens, width), lambda i: (0, 0))
        return pl.BlockSpec((None, tokens, width), lambda i: (which, 0, 0))

    whole = [pl.BlockSpec(w.shape, lambda i: (0, 0)) for w in weights]
    operands, specs, alias = [x, c, *weights], [half(x, 0), half(c, 1), *whole], {}
    if held is not None:
        operands.append(held)
        specs.append(pl.BlockSpec(memory_space=pl.ANY))
        alias = {5: 0}
    coded = SUMS * rows + SCALES
    return pl.pallas_call(
        functools.partial(forward_kernel, rows),
        out_shape=jax.ShapeDtypeStruct((2, chunks, coded, hidden), I16),
        grid=(1,),
        in_specs=specs,
        out_specs=pl.BlockSpec((2, None, coded, hidden), lambda i: (0, chunk, 0, 0)),
        input_output_aliases=alias,
        compiler_params=PARAMS,
        cost_estimate=cost(6 * tokens * width * hidden, 4 * tokens * width + 6 * width * hidden),
        name="forward_chunk",
    )(*operands)


def core_sum_kernel(rows, in_ref, out_ref):
    both = [decode(in_ref[i], rows) for i in range(2)]
    put(out_ref, (), [a + b for a, b in zip(*both)], rows)


def core_sum(arrived, rows):
    _, chunks, coded, hidden = arrived.shape
    return pl.pallas_call(
        functools.partial(core_sum_kernel, rows),
        out_shape=jax.ShapeDtypeStruct((chunks, coded, hidden), I16),
        grid=(chunks,),
        in_specs=[pl.BlockSpec((2, None, coded, hidden), lambda i: (0, i, 0, 0))],
        out_specs=pl.BlockSpec((None, coded, hidden), lambda i: (i, 0, 0)),
        compiler_params=PARAMS,
        cost_estimate=cost(0, 6 * chunks * coded * hidden),
        name="core_sum",
    )(arrived)


def pointwise_kernel(rows, in_ref, keep_ref, both_ref, kept_ref):
    parts = [decode(in_ref[i], rows) for i in range(in_ref.shape[0])]
    gate_pre, up_pre, grad_hidden = (sum(p[1:], p[0]) for p in zip(*parts))
    hidden = gate_pre.shape[1]
    sigmoid_gate = jax.nn.sigmoid(gate_pre)
    silu_gate = gate_pre * sigmoid_gate
    slope = sigmoid_gate * (1.0 + gate_pre * (1.0 - sigmoid_gate))
    both_ref[:, :hidden] = (grad_hidden * up_pre * slope).astype(BF16)
    both_ref[:, hidden:] = (grad_hidden * silu_gate).astype(BF16)
    kept_ref[...] = (silu_gate * up_pre * keep_ref[...]).astype(BF16)


def pointwise(arrived, keep_rows):
    rows, hidden = keep_rows.shape
    return pl.pallas_call(
        functools.partial(pointwise_kernel, rows),
        out_shape=(
            jax.ShapeDtypeStruct((rows, 2 * hidden), BF16),
            jax.ShapeDtypeStruct((rows, hidden), BF16),
        ),
        compiler_params=PARAMS,
        cost_estimate=cost(0, 2 * arrived.size),
        name="pointwise",
    )(arrived, keep_rows)


def keep_of_rows(keep_mask, rows, nz, nx, own_tokens, total):
    tiles, blocks = keep_mask.shape
    chunk = lax.axis_index("y")
    place = lax.axis_index("c") * rows + lax.broadcasted_iota(jnp.int32, (rows, 1), 0)
    rest = place - 8 * nz
    z = jnp.where(rest < 0, place // 8, rest // 4)
    inside = jnp.where(rest < 0, place % 8, 8 + rest % 4)
    shift = jnp.where(chunk == 1, -1, jnp.where(chunk == 2, 1, jnp.where(chunk == 3, 2, 0)))
    token = (z * nx + (lax.axis_index("x") + shift + nx) % nx) * own_tokens + inside
    tile = token // (total // tiles)
    chosen = tile == lax.broadcasted_iota(jnp.int32, (rows, tiles), 1)
    keep = [
        jnp.sum(jnp.where(chosen, keep_mask[:, b][None, :], 0), axis=1, keepdims=True)
        for b in range(blocks)
    ]
    return jnp.concatenate([jnp.broadcast_to(k, (rows, 128)) for k in keep], axis=1).astype(F32)


def input_grad_kernel(order, g_ref, w_ref, out_ref):
    g = g_ref[...].reshape(out_ref.shape[0], w_ref.shape[0])
    out_ref[...] = dot(g, w_ref[...], PLAIN).astype(out_ref.dtype)


def input_grad(both, weights, chunks):
    parts, rows, depth = both.shape
    width = weights.shape[1]
    tokens = parts * rows // chunks
    x = lax.axis_index("x")
    away = (jnp.arange(chunks) - x + chunks) % chunks
    order = jnp.where(away == 0, 0, jnp.where(away == 1, 2, jnp.where(away == 2, 3, 1)))
    return pl.pallas_call(
        input_grad_kernel,
        out_shape=jax.ShapeDtypeStruct((chunks, tokens, width), BF16),
        grid_spec=pltpu.PrefetchScalarGridSpec(
            num_scalar_prefetch=1,
            grid=(chunks,),
            in_specs=[
                pl.BlockSpec((parts // chunks, rows, depth), lambda d, order: (order[d], 0, 0)),
                pl.BlockSpec((depth, width), lambda d, order: (0, 0)),
            ],
            out_specs=pl.BlockSpec((None, tokens, width), lambda d, order: (d, 0, 0)),
        ),
        compiler_params=PARAMS,
        cost_estimate=cost(2 * chunks * tokens * width * depth, 2 * depth * width),
        name="input_grad",
    )(order.astype(jnp.int32), both, weights)


def x_sum_kernel(in_ref, out_ref):
    blocks = out_ref.shape[0]
    width = in_ref.shape[2]
    half = width // 2
    for first in range(0, blocks, 4):
        main = pl.ds(first * 8, 32)
        rest = pl.ds(blocks * 8 + first * 4, 16)
        main, rest = (
            sum((in_ref[i, rows].astype(F32) for i in range(1, in_ref.shape[0])), in_ref[0, rows].astype(F32))
            for rows in (main, rest)
        )
        for i in range(4):
            tail = rest[4 * i : 4 * i + 4]
            tail = jnp.concatenate([tail[:, :half], tail[:, half:]])
            block = jnp.concatenate([main[8 * i : 8 * i + 8], tail], axis=1)
            out_ref[first + i] = block.astype(BF16)


def x_sum(arrived, nz):
    width = arrived.shape[2]
    return pl.pallas_call(
        x_sum_kernel,
        out_shape=jax.ShapeDtypeStruct((nz, 8, 3 * width // 2), BF16),
        compiler_params=PARAMS,
        cost_estimate=cost(0, 2 * arrived.size),
        name="x_sum",
    )(arrived)


def z_sum_kernel(in_ref, out_ref):
    width = out_ref.shape[1]
    total = in_ref[0].astype(F32)
    for i in range(1, in_ref.shape[0]):
        total = total + in_ref[i].astype(F32)
    tail = jnp.concatenate([total[:4, width:], total[4:, width:]], axis=1)
    out_ref[...] = jnp.concatenate([total[:, :width], tail]).astype(BF16)


def z_sum(arrived, own_tokens, width):
    return pl.pallas_call(
        z_sum_kernel,
        out_shape=jax.ShapeDtypeStruct((own_tokens, width), BF16),
        compiler_params=PARAMS,
        cost_estimate=cost(0, 2 * arrived.size),
        name="z_sum",
    )(arrived)


def shards(inputs, cotangent, w_gate, w_up, w_down, keep_mask):
    own_tokens, width = inputs.shape
    hidden = w_gate.shape[1]
    nz, nx, nc = 16, 4, 2
    total = own_tokens * nz * nx
    tokens = own_tokens * nz
    rows = tokens // nc
    weights = (w_gate, w_up, w_down)

    packed = jnp.concatenate([pack(inputs), pack(cotangent)])
    along_z = lax.all_gather(packed, "z")
    own = pl.pallas_call(
        unpack_kernel,
        out_shape=jax.ShapeDtypeStruct((2, tokens, width), BF16),
        compiler_params=PARAMS,
        cost_estimate=cost(0, 8 * tokens * width),
        name="unpack",
    )(along_z)
    right = lax.ppermute(own, "x", ring(nx, 1))
    left = lax.ppermute(own, "x", ring(nx, -1))
    far_in = lax.ppermute(right[0], "x", ring(nx, 1))
    far_cot = lax.ppermute(left[1], "x", ring(nx, -1))
    own_late, w_gate_late, w_up_late = lax.optimization_barrier((own, w_gate, w_up))
    turned = jnp.concatenate([w_gate_late, w_up_late], axis=1).T

    parts = forward(0, own_late, own_late, weights, None, nx)
    parts = forward(1, right, right, weights, parts, nx)
    parts = forward(2, left, left, weights, parts, nx)
    parts = forward(3, far_in, far_cot, weights, parts, nx)

    summed = core_sum(lax.all_to_all(parts, "c", 0, 0), rows)
    keep_rows = keep_of_rows(keep_mask, rows, nz, nx, own_tokens, total)
    both, hidden_kept = pointwise(lax.all_to_all(summed, "y", 0, 0), keep_rows)
    both = lax.all_gather(both, ("y", "c"))

    result = input_grad(both, turned, nx)
    result, hidden_kept = lax.optimization_barrier((result, hidden_kept))
    arrived = lax.all_to_all(result, "x", 0, 0)
    all_kept = lax.all_gather(hidden_kept, ("y", "c")).reshape(total, hidden)
    all_inputs = jnp.concatenate([own[0], right[0], left[0], far_in])
    all_cotangent = jnp.concatenate([own[1], right[1], left[1], far_cot])
    arrived, all_kept, all_inputs, all_cotangent = lax.optimization_barrier(
        (arrived, all_kept, all_inputs, all_cotangent)
    )
    kept = x_sum(arrived, nz)
    kept, all_kept, all_inputs, all_cotangent, both = lax.optimization_barrier(
        (kept, all_kept, all_inputs, all_cotangent, both)
    )
    grad_input = z_sum(lax.all_to_all(kept, "z", 0, 0), own_tokens, width)

    both = both.reshape(total, 2 * hidden)
    grad_down = dot(all_kept, all_cotangent, OUTER).astype(BF16)
    grad_gate = dot(all_inputs, both[:, :hidden], OUTER).astype(BF16)
    grad_up = dot(all_inputs, both[:, hidden:], OUTER).astype(BF16)
    return grad_input, grad_gate, grad_up, grad_down


def solution(mesh):
    fine = Mesh(mesh.devices.reshape(16, 4, 4, 2), ("z", "x", "y", "c"))
    hid, mdl = ("z", "x"), ("y", "c")
    placed = (P(hid, mdl), P(hid, mdl), P(mdl, hid), P(mdl, hid), P(hid, mdl), P(None, hid))
    return jax.shard_map(
        shards,
        mesh=fine,
        in_specs=placed,
        out_specs=(P(hid, mdl), P(mdl, hid), P(mdl, hid), P(hid, mdl)),
        check_vma=False,
    )
```

time: 185 us -> 175 us (0.946)
  waiting for transfers between devices: 50.6 us -> 36.9 us
  Pallas kernels: 5.77 us -> 13.5 us
  other arithmetic: 12.8 us -> 6.02 us
  local copies, waits for them, and re-layouts: 7.87 us -> 11.6 us
    reduce_sum x4 -> x0, other arithmetic: 6.17 us -> none  [the longest x1 3 us: shards(): summed = jnp.sum(lax.all_to_all(parts, 'c', 0, 0), axis=0)]
    all_to_all x2, waiting for transfers between devices: 32.2 us -> 27.8 us  [the longest x1 18.4 us: shards(): grad_input = z_sum(lax.all_to_all(kept, 'z', 0, 0), own_tokens, width)]
    pallas_call x0 -> x5, Pallas kernels: none -> 4.25 us  [the longest x1 2.23 us: core_sum(): pl.pallas_call(functools.partial(core_sum_kernel, rows), out_shape=jax.Sh...]
    pallas_call x4, Pallas kernels: 2.18 us -> 5.97 us  [forward(): pl.pallas_call(functools.partial(forward_kernel, rows), out_shape=jax.Sha...]
    ppermute x1, waiting for transfers between devices: 11.1 us -> 7.7 us  [shards(): right = lax.ppermute(own, 'x', ring(nx, 1))]
    ppermute x1, waiting for transfers between devices: 4.4 us -> 1.11 us  [shards(): far_cot = lax.ppermute(left[1], 'x', ring(nx, -1))]
    reshape x4 -> x0, local copies, waits for them, and re-layouts: 3.15 us -> none  [the longest x1 0.91 us: shards(): jnp.sum(arrived.astype(F32), axis=0).astype(BF16).reshape(nz, flat, 128)]
    another operation x2 -> x0, other arithmetic: 2.67 us -> none  [the longest x1 2.66 us: input_grad(): order = jnp.stack([place[(d - x + chunks) % chunks] for d in range(chunks)])]
  transfers between devices with their start and end apart: 7 -> 7, of which waited for: 6 -> 5; matrix products, arithmetic and copies ran while one was open for 8% -> 10% of each run, Pallas kernels for 1% -> 2%
where the time goes in v3:
time: 175 us; the launch traced here: 174 us
  blocking collectives  71.4 us (41%)
  waiting for transfers between devices  36.9 us (21%)
  starting transfers between devices  27.4 us (16%)
  Pallas kernels  13.5 us (8%)
  local copies, waits for them, and re-layouts  11.6 us (7%)
  other arithmetic  6.02 us (3%)
  matrix products  5.77 us (3%)
    all_gather x1, blocking collectives, shards(): along_z = lax.all_gather(packed, 'z')  40.1 us
    all_to_all x1, waiting for transfers between devices, shards(): grad_input = z_sum(lax.all_to_all(kept, 'z', 0, 0), own_tokens, width)  18.4 us
    all_gather x1, blocking collectives, shards(): both = lax.all_gather(both, ('y', 'c'))  13.5 us
    all_gather x1, blocking collectives, shards(): all_kept = lax.all_gather(hidden_kept, ('y', 'c')).reshape(total, hidden)  13.1 us
    all_to_all x1, waiting for transfers between devices, shards(): both, hidden_kept = pointwise(lax.all_to_all(summed, 'y', 0, 0), keep_rows)  9.42 us
    ppermute x1, waiting for transfers between devices, shards(): right = lax.ppermute(own, 'x', ring(nx, 1))  7.7 us
    all_to_all x1, starting transfers between devices, shards(): grad_input = z_sum(lax.all_to_all(kept, 'z', 0, 0), own_tokens, width)  6.62 us
    pallas_call x4, Pallas kernels, forward(): pl.pallas_call(functools.partial(forward_kernel, rows), out_shape=jax.Sha...  5.97 us
  transfers between devices with their start and end apart: 7, of which 5 were waited for; matrix products, arithmetic and copies ran while one was open for 10% of the time, Pallas kernels for 2%

profile of v3, /device:TPU:6, one launch (start us, length us, event | category | flops | bytes accessed | tf_op | source)
XLA Modules:
  0.0 173.5 jit_solution(6253466405596034307)
XLA Ops:
  3.0 40.1 %all-gather = bf16[256,1536]{1,0:T(8,128)(2,1)S(1)} all-gather(bf16[16,1536]{1,0:T(8,128)(2,1)S(1)} %maximum_maximum_fusion), channel_id=2, replica_groups=mesh['z'=16,'x'=4,'y'=4,'c'=2] {'z'}, dimensions={0}, use_global_device_ids=true | all-gather | bytes 835584 | tf_op jit(solution)/shard_map/all_gather | solution.py:291
  43.2 2.4 %collective-permute-start = (bf16[2,192,1024]{2,1,0:T(8,128)(2,1)S(1)}, bf16[2,192,1024]{2,1,0:T(8,128)(2,1)}, u32[]{:S(2)}, u32[]{:S(2)}) collective-permute-start(bf16[2,192,1024]{2,1,0:T(8,128)(2,1)S(1)} %unpack.1.x_ref.c_ref), channel_id=1, source_target_pairs={{0,8},{8,16},{16,24},{24,0},{1,9},{9,17},{17,25},{25,1},{2,10},{10... | collective-permute-start | bytes 2359304 | tf_op jit(solution)/shard_map/ppermute | solution.py:299
  45.6 3.5 %collective-permute-start.2 = (bf16[2,192,1024]{2,1,0:T(8,128)(2,1)S(1)}, bf16[2,192,1024]{2,1,0:T(8,128)(2,1)}, u32[]{:S(2)}, u32[]{:S(2)}) collective-permute-start(bf16[2,192,1024]{2,1,0:T(8,128)(2,1)S(1)} %unpack.1.x_ref.c_ref), channel_id=1, source_target_pairs={{0,24},{8,0},{16,8},{24,16},{1,25},{9,1},{17,9},{25,17},{2,26},{10... | collective-permute-start | bytes 2359304 | tf_op jit(solution)/shard_map/ppermute | solution.py:300
  49.1 1.0 copy-done.2
  50.8 7.7 %collective-permute-done.x_ref.c_ref = bf16[2,192,1024]{2,1,0:T(8,128)(2,1)} collective-permute-done((bf16[2,192,1024]{2,1,0:T(8,128)(2,1)S(1)}, bf16[2,192,1024]{2,1,0:T(8,128)(2,1)}, u32[]{:S(2)}, u32[]{:S(2)}) %collective-permute-start) | collective-permute-done | bytes 786464 | tf_op jit(solution)/shard_map/ppermute | solution.py:299
  58.5 2.0 %slice_bitcast_fusion = (bf16[192,1024]{1,0:T(8,128)(2,1)}, bf16[192,1024]{1,0:T(8,128)(2,1)}) fusion(bf16[2,192,1024]{2,1,0:T(8,128)(2,1)} %collective-permute-done.x_ref.c_ref), kind=kLoop, calls=%fused_computation.8 | loop fusion | bytes 1572864 | tf_op jit(solution)/shard_map/squeeze | solution.py:321
  60.6 2.6 %collective-permute-start.1 = (bf16[192,1024]{1,0:T(8,128)(2,1)}, bf16[192,1024]{1,0:T(8,128)(2,1)S(1)}, u32[]{:S(2)}, u32[]{:S(2)}) collective-permute-start(bf16[192,1024]{1,0:T(8,128)(2,1)} %get-tuple-element.41), channel_id=1, source_target_pairs={{0,8},{8,16},{16,24},{24,0},{1,9},{9,17},{17,25},{25,1},{2,10},{10... | collective-permute-start | bytes 1179656 | tf_op jit(solution)/shard_map/ppermute | solution.py:301
  63.2 2.1 %slice_bitcast_fusion.2 = (bf16[192,1024]{1,0:T(8,128)(2,1)}, bf16[192,1024]{1,0:T(8,128)(2,1)}) fusion(bf16[2,192,1024]{2,1,0:T(8,128)(2,1)} %collective-permute-done.2.x_ref.c_ref), kind=kLoop, calls=%fused_computation.10 | loop fusion | bytes 1572864 | tf_op jit(solution)/shard_map/squeeze | solution.py:320
  65.2 3.4 %collective-permute-start.3 = (bf16[192,1024]{1,0:T(8,128)(2,1)}, bf16[192,1024]{1,0:T(8,128)(2,1)}, u32[]{:S(2)}, u32[]{:S(2)}) collective-permute-start(bf16[192,1024]{1,0:T(8,128)(2,1)} %get-tuple-element.43), channel_id=1, source_target_pairs={{0,24},{8,0},{16,8},{24,16},{1,25},{9,1},{17,9},{25,17},{2,26},{10... | collective-permute-start | bytes 1179656 | tf_op jit(solution)/shard_map/ppermute | solution.py:302
  68.6 1.0 copy.16
  69.6 1.0 copy.15
  70.6 1.0 copy-done.3
  71.7 1.8 %forward_chunk.5.rest_0_ = s16[2,4,304,256]{3,2,1,0:T(8,128)(2,1)S(1)} custom-call(bf16[2,192,1024]{2,1,0:T(8,128)(2,1)} %collective-permute-done.x_ref.c_ref, bf16[2,192,1024]{2,1,0:T(8,128)(2,1)} %collective-permute-done.x_ref.c_ref, bf16[1024,256]{1,0:T(8,128)(2,1)S(1)} %copy-done, ...), custom_call_target="tpu_custom_call", output_to_operand_aliasing={{}: (5, {})} | custom-call | flops 301989888 | bytes 2359296 | tf_op jit(solution)/shard_map/forward_chunk/pallas_call | solution.py:127
  73.5 1.8 %forward_chunk.6.rest_0_ = s16[2,4,304,256]{3,2,1,0:T(8,128)(2,1)S(1)} custom-call(bf16[2,192,1024]{2,1,0:T(8,128)(2,1)} %collective-permute-done.2.x_ref.c_ref, bf16[2,192,1024]{2,1,0:T(8,128)(2,1)} %collective-permute-done.2.x_ref.c_ref, bf16[1024,256]{1,0:T(8,128)(2,1)S(1)} %copy-done, ...), custom_call_target="tpu_custom_call", output_to_operand_aliasing={{}: (5, {})} | custom-call | flops 301989888 | bytes 2359296 | tf_op jit(solution)/shard_map/forward_chunk/pallas_call | solution.py:127
  75.3 1.1 collective-permute-done.3.c_ref
  76.4 1.7 forward_chunk.7
  78.1 4.7 %all_to_all.20.in_ref = s16[2,4,304,256]{3,2,1,0:T(8,128)(2,1)S(1)} all-to-all(s16[2,4,304,256]{3,2,1,0:T(8,128)(2,1)S(1)} %forward_chunk.7), channel_id=1, replica_groups=mesh['z'=16,'x'=4,'y'=4,'c'=2] {'c'}, dimensions={0} | all-to-all | bytes 2490368 | tf_op jit(solution)/shard_map/all_to_all | solution.py:311
  82.8 2.2 %core_sum.1 = s16[4,304,256]{2,1,0:T(8,128)(2,1)} custom-call(s16[2,4,304,256]{3,2,1,0:T(8,128)(2,1)S(1)} %all_to_all.20.in_ref), custom_call_target="tpu_custom_call" | custom-call | bytes 1867776 | tf_op jit(solution)/shard_map/core_sum/pallas_call | solution.py:147
  85.1 4.5 %all-to-all-start.1 = ((s16[4,304,256]{2,1,0:T(8,128)(2,1)}), s16[4,304,256]{2,1,0:T(8,128)(2,1)S(1)}, u32[]{:S(2)}, u32[]{:S(2)}) async-start(s16[4,304,256]{2,1,0:T(8,128)(2,1)} %core_sum.1), calls=%async_computation.1 | async-start | bytes 1245184 | tf_op jit(solution)/shard_map/all_to_all | solution.py:313
  89.8 1.1 maximum_bitcast_fusion.w_ref
  90.9 9.4 %all-to-all-done.1.in_ref = s16[4,304,256]{2,1,0:T(8,128)(2,1)S(1)} async-done(((s16[4,304,256]{2,1,0:T(8,128)(2,1)}), s16[4,304,256]{2,1,0:T(8,128)(2,1)S(1)}, u32[]{:S(2)}, u32[]{:S(2)}) %all-to-all-start.1) | async-done | bytes 622624 | tf_op jit(solution)/shard_map/all_to_all | solution.py:313
  100.6 13.5 %all-gather.1 = bf16[768,512]{1,0:T(8,128)(2,1)S(1)} all-gather(bf16[96,512]{1,0:T(8,128)(2,1)S(1)} %get-tuple-element.21), channel_id=3, replica_groups=mesh['z'=16,'x'=4,'y'=4,'c'=2] {'y','c'}, dimensions={0}, use_global_device_ids=true | all-gather | bytes 884736 | tf_op jit(solution)/shard_map/all_gather | solution.py:314
  114.1 3.2 %input_grad.1 = bf16[4,192,1024]{2,1,0:T(8,128)(2,1)} custom-call(s32[4]{0:T(128)S(1)} %compare_select_fusion.4.order, bf16[8,96,512]{2,1,0:T(8,128)(2,1)S(1)} %bitcast.26, bf16[512,1024]{1,0:T(8,128)(2,1)S(1)} %maximum_bitcast_fusion.w_ref), custom_call_target="tpu_custom_call" | custom-call | flops 805306368 | bytes 1048576 | tf_op jit(solution)/shard_map/input_grad/pallas_call | solution.py:215
  117.4 4.5 %all-to-all-start.2 = ((bf16[4,192,1024]{2,1,0:T(8,128)(2,1)}), bf16[4,192,1024]{2,1,0:T(8,128)(2,1)S(1)}, u32[]{:S(2)}, u32[]{:S(2)}) async-start(bf16[4,192,1024]{2,1,0:T(8,128)(2,1)} %input_grad.1), calls=%async_computation.2 | async-start | bytes 3145728 | tf_op jit(solution)/shard_map/all_to_all | solution.py:318
  122.9 2.3 %pad_maximum_fusion = bf16[768,1024]{1,0:T(8,128)(2,1)} fusion(bf16[192,1024]{1,0:T(8,128)(2,1)S(1)} %collective-permute-done.1.x_ref, bf16[192,1024]{1,0:T(8,128)(2,1)S(1)} %copy-done.10, bf16[192,1024]{1,0:T(8,128)(2,1)} %get-tuple-element.41, bf16[192,1024]{1,0:T(8,128)(2,1)S(1)} %get-tuple-element.39), kind=kLoop, calls=%fused_computation | loop fusion | flops 6291456 | bytes 3145728 | tf_op jit(solution)/shard_map/concatenate | solution.py:320
  125.2 2.4 %pad_maximum_fusion.1 = bf16[768,1024]{1,0:T(8,128)(2,1)} fusion(bf16[192,1024]{1,0:T(8,128)(2,1)} %collective-permute-done.3.c_ref, bf16[192,1024]{1,0:T(8,128)(2,1)} %get-tuple-element.43, bf16[192,1024]{1,0:T(8,128)(2,1)S(1)} %copy-done.9, bf16[192,1024]{1,0:T(8,128)(2,1)S(1)} %get-tuple-element.38), kind=kLoop, calls=%fused_computation.1 | loop fusion | flops 6291456 | bytes 3145728 | tf_op jit(solution)/shard_map/concatenate | solution.py:321
  127.6 13.1 %all-gather.2 = bf16[768,256]{1,0:T(8,128)(2,1)S(1)} all-gather(bf16[96,256]{1,0:T(8,128)(2,1)S(1)} %get-tuple-element.26), channel_id=4, replica_groups=mesh['z'=16,'x'=4,'y'=4,'c'=2] {'y','c'}, dimensions={0}, use_global_device_ids=true | all-gather | bytes 442368 | tf_op jit(solution)/shard_map/all_gather | solution.py:319
  142.0 6.6 %all-to-all-start.3 = ((bf16[16,8,1536]{2,1,0:T(8,128)(2,1)}), bf16[16,8,1536]{2,1,0:T(8,128)(2,1)S(1)}, u32[]{:S(2)}, u32[]{:S(2)}) async-start(bf16[16,8,1536]{2,1,0:T(8,128)(2,1)} %x_sum.1), calls=%async_computation.3 | async-start | bytes 786432 | tf_op jit(solution)/shard_map/all_to_all | solution.py:329
  148.7 3.0 %convolution_convert_fusion.2 = bf16[1024,256]{1,0:T(8,128)(2,1)} fusion(bf16[768,1024]{1,0:T(8,128)(2,1)} %pad_maximum_fusion, bf16[768,512]{1,0:T(8,128)(2,1)S(1)} %copy-done.5), kind=kOutput, calls=%fused_computation.4 | convolution fusion | flops 402915328 | bytes 2490368 | tf_op jit(solution)/shard_map/dot_general | solution.py:24
  151.6 1.4 convolution_convert_fusion.1
  153.1 1.4 convolution_convert_fusion
  154.5 18.4 %all-to-all-done.3.in_ref = bf16[16,8,1536]{2,1,0:T(8,128)(2,1)S(1)} async-done(((bf16[16,8,1536]{2,1,0:T(8,128)(2,1)}), bf16[16,8,1536]{2,1,0:T(8,128)(2,1)S(1)}, u32[]{:S(2)}, u32[]{:S(2)}) %all-to-all-start.3) | async-done | bytes 393248 | tf_op jit(solution)/shard_map/all_to_all | solution.py:329
  (42 shorter events, 6.7 us)
Async XLA Ops:
  0.6 48.4 %copy-start = (bf16[1024,256]{1,0:T(8,128)(2,1)S(1)}, bf16[1024,256]{1,0:T(8,128)(2,1)}, u32[]{:S(2)}) copy-start(bf16[1024,256]{1,0:T(8,128)(2,1)} %wg_ref.7) | copy-start | bytes 1572868
  0.6 48.4 %copy-start.1 = (bf16[1024,256]{1,0:T(8,128)(2,1)S(1)}, bf16[1024,256]{1,0:T(8,128)(2,1)}, u32[]{:S(2)}) copy-start(bf16[1024,256]{1,0:T(8,128)(2,1)} %wu_ref.7) | copy-start | bytes 1572868
  43.2 15.3 %collective-permute-start = (bf16[2,192,1024]{2,1,0:T(8,128)(2,1)S(1)}, bf16[2,192,1024]{2,1,0:T(8,128)(2,1)}, u32[]{:S(2)}, u32[]{:S(2)}) collective-permute-start(bf16[2,192,1024]{2,1,0:T(8,128)(2,1)S(1)} %unpack.1.x_ref.c_ref), channel_id=1, source_target_pairs={{0,8},{8,16},{16,24},{24,0},{1,9},{9,17},{17,25},{25,1},{2,10},{10... | collective-permute-start | bytes 2359304 | tf_op jit(solution)/shard_map/ppermute | solution.py:299
  45.6 17.6 %collective-permute-start.2 = (bf16[2,192,1024]{2,1,0:T(8,128)(2,1)S(1)}, bf16[2,192,1024]{2,1,0:T(8,128)(2,1)}, u32[]{:S(2)}, u32[]{:S(2)}) collective-permute-start(bf16[2,192,1024]{2,1,0:T(8,128)(2,1)S(1)} %unpack.1.x_ref.c_ref), channel_id=1, source_target_pairs={{0,24},{8,0},{16,8},{24,16},{1,25},{9,1},{17,9},{25,17},{2,26},{10... | collective-permute-start | bytes 2359304 | tf_op jit(solution)/shard_map/ppermute | solution.py:300
  49.1 1.0 copy-start.2
  60.6 10.1 %copy-start.11 = (s32[12,2]{0,1:T(2,128)S(1)}, s32[12,2]{0,1:T(2,128)}, u32[]{:S(2)}) copy-start(s32[12,2]{0,1:T(2,128)} %param.11) | copy-start | bytes 292
  60.6 14.7 %collective-permute-start.1 = (bf16[192,1024]{1,0:T(8,128)(2,1)}, bf16[192,1024]{1,0:T(8,128)(2,1)S(1)}, u32[]{:S(2)}, u32[]{:S(2)}) collective-permute-start(bf16[192,1024]{1,0:T(8,128)(2,1)} %get-tuple-element.41), channel_id=1, source_target_pairs={{0,8},{8,16},{16,24},{24,0},{1,9},{9,17},{17,25},{25,1},{2,10},{10... | collective-permute-start | bytes 1179656 | tf_op jit(solution)/shard_map/ppermute | solution.py:301
  65.2 11.2 %collective-permute-start.3 = (bf16[192,1024]{1,0:T(8,128)(2,1)}, bf16[192,1024]{1,0:T(8,128)(2,1)}, u32[]{:S(2)}, u32[]{:S(2)}) collective-permute-start(bf16[192,1024]{1,0:T(8,128)(2,1)} %get-tuple-element.43), channel_id=1, source_target_pairs={{0,24},{8,0},{16,8},{24,16},{1,25},{9,1},{17,9},{25,17},{2,26},{10... | collective-permute-start | bytes 1179656 | tf_op jit(solution)/shard_map/ppermute | solution.py:302
  70.6 1.0 copy-start.3
  82.8 7.0 %copy-start.6 = (bf16[1024,256]{0,1:T(8,128)(2,1)S(1)}, bf16[1024,256]{0,1:T(8,128)(2,1)}, u32[]{:S(2)}) copy-start(bf16[1024,256]{0,1:T(8,128)(2,1)} %copy.16) | copy-start | bytes 1572868
  85.1 15.3 %all-to-all-start.1 = ((s16[4,304,256]{2,1,0:T(8,128)(2,1)}), s16[4,304,256]{2,1,0:T(8,128)(2,1)S(1)}, u32[]{:S(2)}, u32[]{:S(2)}) async-start(s16[4,304,256]{2,1,0:T(8,128)(2,1)} %core_sum.1), calls=%async_computation.1 | async-start | bytes 1245184 | tf_op jit(solution)/shard_map/all_to_all | solution.py:313
  114.1 3.3 %copy-start.4 = (bf16[768,512]{1,0:T(8,128)(2,1)}, bf16[768,512]{1,0:T(8,128)(2,1)S(1)}, u32[]{:S(2)}) copy-start(bf16[768,512]{1,0:T(8,128)(2,1)S(1)} %all-gather.1) | copy-start | bytes 2359300
  117.4 23.7 %all-to-all-start.2 = ((bf16[4,192,1024]{2,1,0:T(8,128)(2,1)}), bf16[4,192,1024]{2,1,0:T(8,128)(2,1)S(1)}, u32[]{:S(2)}, u32[]{:S(2)}) async-start(bf16[4,192,1024]{2,1,0:T(8,128)(2,1)} %input_grad.1), calls=%async_computation.2 | async-start | bytes 3145728 | tf_op jit(solution)/shard_map/all_to_all | solution.py:318
  121.9 1.0 copy-start.10
  122.9 2.3 %copy-start.9 = (bf16[192,1024]{1,0:T(8,128)(2,1)S(1)}, bf16[192,1024]{1,0:T(8,128)(2,1)}, u32[]{:S(2)}) copy-start(bf16[192,1024]{1,0:T(8,128)(2,1)} %get-tuple-element.40) | copy-start | bytes 1179652
  127.6 21.0 %copy-start.5 = (bf16[768,512]{1,0:T(8,128)(2,1)S(1)}, bf16[768,512]{1,0:T(8,128)(2,1)}, u32[]{:S(2)}) copy-start(bf16[768,512]{1,0:T(8,128)(2,1)} %copy-done.4) | copy-start | bytes 2359300
  142.0 30.8 %all-to-all-start.3 = ((bf16[16,8,1536]{2,1,0:T(8,128)(2,1)}), bf16[16,8,1536]{2,1,0:T(8,128)(2,1)S(1)}, u32[]{:S(2)}, u32[]{:S(2)}) async-start(bf16[16,8,1536]{2,1,0:T(8,128)(2,1)} %x_sum.1), calls=%async_computation.3 | async-start | bytes 786432 | tf_op jit(solution)/shard_map/all_to_all | solution.py:329
  148.7 3.0 %copy-start.7 = (bf16[768,1024]{1,0:T(8,128)(2,1)S(1)}, bf16[768,1024]{1,0:T(8,128)(2,1)}, u32[]{:S(2)}) copy-start(bf16[768,1024]{1,0:T(8,128)(2,1)} %pad_maximum_fusion) | copy-start | bytes 4718596
  151.6 1.4 copy-start.8

commit v4 on v3

--- a/solution.py
+++ b/solution.py
@@ -13,7 +13,6 @@
 OUTER = (((0,), (0,)), ((), ()))
 SUMS = 3
 SCALES = 16
-PARAMS = pltpu.CompilerParams(vmem_limit_bytes=32 << 20)
 
 
 def ring(size, step):
@@ -22,6 +21,10 @@
 
 def dot(a, b, dims):
     return lax.dot_general(a, b, dims, preferred_element_type=F32)
+
+
+def params(mebibytes):
+    return pltpu.CompilerParams(vmem_limit_bytes=mebibytes << 20)
 
 
 def cost(flops, moved):
@@ -65,15 +68,15 @@
     out_ref[(*index, pl.ds(SUMS * rows, SCALES))] = tile
 
 
-def unpack_kernel(packed_ref, out_ref):
+def unpack_kernel(packed_ref, *out_refs):
     blocks = packed_ref.shape[0]
-    width = out_ref.shape[2]
+    width = out_refs[0].shape[1]
     half = width // 2
     for first in range(0, blocks, 2):
         pair = [packed_ref[first + i].astype(F32) for i in range(2)]
         for which in range(2):
             part = [p[which * 8 : which * 8 + 8] for p in pair]
-            out_ref[which, first * 8 : first * 8 + 16] = jnp.concatenate(
+            out_refs[which][first * 8 : first * 8 + 16] = jnp.concatenate(
                 [p[:, :width] for p in part]
             ).astype(BF16)
     for first in range(0, blocks, 4):
@@ -87,12 +90,29 @@
                 ],
                 axis=1,
             )
-            out_ref[which, blocks * 8 + first * 4 : blocks * 8 + first * 4 + 16] = rows.astype(BF16)
-
-
-def pack(a):
-    half = a.shape[1] // 2
-    return jnp.concatenate([a[:8], jnp.concatenate([a[8:, :half], a[8:, half:]])], axis=1)
+            place = blocks * 8 + first * 4
+            out_refs[which][place : place + 16] = rows.astype(BF16)
+
+
+def pack_kernel(*refs):
+    packed = []
+    for ref in refs[:-1]:
+        a = ref[...].astype(F32)
+        half = a.shape[1] // 2
+        tail = jnp.concatenate([a[8:, :half], a[8:, half:]])
+        packed.append(jnp.concatenate([a[:8], tail], axis=1))
+    refs[-1][...] = jnp.concatenate(packed).astype(BF16)
+
+
+def pack(*arrays):
+    width = arrays[0].shape[1]
+    return pl.pallas_call(
+        pack_kernel,
+        out_shape=jax.ShapeDtypeStruct((8 * len(arrays), 3 * width // 2), BF16),
+        cost_estimate=cost(0, 48 * len(arrays) * width),
+        compiler_params=params(2),
+        name="pack",
+    )(*arrays)
 
 
 def forward_kernel(rows, x_ref, c_ref, wg_ref, wu_ref, wd_ref, *rest):
@@ -112,13 +132,9 @@
     hidden = weights[0].shape[1]
     rows = tokens // 2
 
-    def half(a, which):
-        if a.ndim == 2:
-            return pl.BlockSpec((tokens, width), lambda i: (0, 0))
-        return pl.BlockSpec((None, tokens, width), lambda i: (which, 0, 0))
-
+    half = pl.BlockSpec((tokens, width), lambda i: (0, 0))
     whole = [pl.BlockSpec(w.shape, lambda i: (0, 0)) for w in weights]
-    operands, specs, alias = [x, c, *weights], [half(x, 0), half(c, 1), *whole], {}
+    operands, specs, alias = [x, c, *weights], [half, half, *whole], {}
     if held is not None:
         operands.append(held)
         specs.append(pl.BlockSpec(memory_space=pl.ANY))
@@ -131,27 +147,24 @@
         in_specs=specs,
         out_specs=pl.BlockSpec((2, None, coded, hidden), lambda i: (0, chunk, 0, 0)),
         input_output_aliases=alias,
-        compiler_params=PARAMS,
         cost_estimate=cost(6 * tokens * width * hidden, 4 * tokens * width + 6 * width * hidden),
+        compiler_params=params(9),
         name="forward_chunk",
     )(*operands)
 
 
 def core_sum_kernel(rows, in_ref, out_ref):
-    both = [decode(in_ref[i], rows) for i in range(2)]
-    put(out_ref, (), [a + b for a, b in zip(*both)], rows)
+    for chunk in range(in_ref.shape[1]):
+        both = [decode(in_ref[i, chunk], rows) for i in range(2)]
+        put(out_ref, (chunk,), [a + b for a, b in zip(*both)], rows)
 
 
 def core_sum(arrived, rows):
-    _, chunks, coded, hidden = arrived.shape
     return pl.pallas_call(
         functools.partial(core_sum_kernel, rows),
-        out_shape=jax.ShapeDtypeStruct((chunks, coded, hidden), I16),
-        grid=(chunks,),
-        in_specs=[pl.BlockSpec((2, None, coded, hidden), lambda i: (0, i, 0, 0))],
-        out_specs=pl.BlockSpec((None, coded, hidden), lambda i: (i, 0, 0)),
-        compiler_params=PARAMS,
-        cost_estimate=cost(0, 6 * chunks * coded * hidden),
+        out_shape=jax.ShapeDtypeStruct(arrived.shape[1:], I16),
+        cost_estimate=cost(0, 3 * arrived.size),
+        compiler_params=params(5),
         name="core_sum",
     )(arrived)
 
@@ -176,8 +189,8 @@
             jax.ShapeDtypeStruct((rows, 2 * hidden), BF16),
             jax.ShapeDtypeStruct((rows, hidden), BF16),
         ),
-        compiler_params=PARAMS,
         cost_estimate=cost(0, 2 * arrived.size),
+        compiler_params=params(4),
         name="pointwise",
     )(arrived, keep_rows)
 
@@ -200,34 +213,32 @@
     return jnp.concatenate([jnp.broadcast_to(k, (rows, 128)) for k in keep], axis=1).astype(F32)
 
 
-def input_grad_kernel(order, g_ref, w_ref, out_ref):
-    g = g_ref[...].reshape(out_ref.shape[0], w_ref.shape[0])
-    out_ref[...] = dot(g, w_ref[...], PLAIN).astype(out_ref.dtype)
-
-
-def input_grad(both, weights, chunks):
+def input_grad_kernel(chunks, g_ref, wg_ref, wu_ref, out_ref):
+    parts, rows, depth = g_ref.shape
+    width, hidden = wg_ref.shape
+    tokens = parts * rows // chunks
+    g = g_ref[...].reshape(parts * rows, depth)
+    x = lax.axis_index("x")
+    for first in range(0, width, 256):
+        columns = slice(first, first + 256)
+        product = dot(g[:, :hidden], wg_ref[columns], INNER)
+        product = (product + dot(g[:, hidden:], wu_ref[columns], INNER)).astype(BF16)
+        for k, away in enumerate((0, -1, 1, 2)):
+            owner = lax.rem(x + (away + chunks), chunks)
+            out_ref[owner, :, columns] = product[k * tokens : (k + 1) * tokens]
+
+
+def input_grad(both, w_gate, w_up, chunks):
     parts, rows, depth = both.shape
-    width = weights.shape[1]
+    width = w_gate.shape[0]
     tokens = parts * rows // chunks
-    x = lax.axis_index("x")
-    away = (jnp.arange(chunks) - x + chunks) % chunks
-    order = jnp.where(away == 0, 0, jnp.where(away == 1, 2, jnp.where(away == 2, 3, 1)))
-    return pl.pallas_call(
-        input_grad_kernel,
+    return pl.pallas_call(
+        functools.partial(input_grad_kernel, chunks),
         out_shape=jax.ShapeDtypeStruct((chunks, tokens, width), BF16),
-        grid_spec=pltpu.PrefetchScalarGridSpec(
-            num_scalar_prefetch=1,
-            grid=(chunks,),
-            in_specs=[
-                pl.BlockSpec((parts // chunks, rows, depth), lambda d, order: (order[d], 0, 0)),
-                pl.BlockSpec((depth, width), lambda d, order: (0, 0)),
-            ],
-            out_specs=pl.BlockSpec((None, tokens, width), lambda d, order: (d, 0, 0)),
-        ),
-        compiler_params=PARAMS,
+        compiler_params=params(8),
         cost_estimate=cost(2 * chunks * tokens * width * depth, 2 * depth * width),
         name="input_grad",
-    )(order.astype(jnp.int32), both, weights)
+    )(both, w_gate, w_up)
 
 
 def x_sum_kernel(in_ref, out_ref):
@@ -253,8 +264,8 @@
     return pl.pallas_call(
         x_sum_kernel,
         out_shape=jax.ShapeDtypeStruct((nz, 8, 3 * width // 2), BF16),
-        compiler_params=PARAMS,
         cost_estimate=cost(0, 2 * arrived.size),
+        compiler_params=params(5),
         name="x_sum",
     )(arrived)
 
@@ -272,8 +283,8 @@
     return pl.pallas_call(
         z_sum_kernel,
         out_shape=jax.ShapeDtypeStruct((own_tokens, width), BF16),
-        compiler_params=PARAMS,
         cost_estimate=cost(0, 2 * arrived.size),
+        compiler_params=params(3),
         name="z_sum",
     )(arrived)
 
@@ -287,47 +298,39 @@
     rows = tokens // nc
     weights = (w_gate, w_up, w_down)
 
-    packed = jnp.concatenate([pack(inputs), pack(cotangent)])
-    along_z = lax.all_gather(packed, "z")
-    own = pl.pallas_call(
+    along_z = lax.all_gather(pack(inputs, cotangent), "z")
+    own_in, own_cot = pl.pallas_call(
         unpack_kernel,
-        out_shape=jax.ShapeDtypeStruct((2, tokens, width), BF16),
-        compiler_params=PARAMS,
+        out_shape=(jax.ShapeDtypeStruct((tokens, width), BF16),) * 2,
         cost_estimate=cost(0, 8 * tokens * width),
+        compiler_params=params(6),
         name="unpack",
     )(along_z)
-    right = lax.ppermute(own, "x", ring(nx, 1))
-    left = lax.ppermute(own, "x", ring(nx, -1))
-    far_in = lax.ppermute(right[0], "x", ring(nx, 1))
-    far_cot = lax.ppermute(left[1], "x", ring(nx, -1))
-    own_late, w_gate_late, w_up_late = lax.optimization_barrier((own, w_gate, w_up))
-    turned = jnp.concatenate([w_gate_late, w_up_late], axis=1).T
-
-    parts = forward(0, own_late, own_late, weights, None, nx)
-    parts = forward(1, right, right, weights, parts, nx)
-    parts = forward(2, left, left, weights, parts, nx)
+    right_in = lax.ppermute(own_in, "x", ring(nx, 1))
+    left_cot = lax.ppermute(own_cot, "x", ring(nx, -1))
+    right_cot = lax.ppermute(own_cot, "x", ring(nx, 1))
+    left_in = lax.ppermute(own_in, "x", ring(nx, -1))
+    far_in = lax.ppermute(right_in, "x", ring(nx, 1))
+    far_cot = lax.ppermute(left_cot, "x", ring(nx, -1))
+    parts = forward(0, own_in, own_cot, weights, None, nx)
+    parts = forward(1, right_in, right_cot, weights, parts, nx)
+    parts = forward(2, left_in, left_cot, weights, parts, nx)
     parts = forward(3, far_in, far_cot, weights, parts, nx)
 
+    keep_rows = keep_of_rows(keep_mask, rows, nz, nx, own_tokens, total)
     summed = core_sum(lax.all_to_all(parts, "c", 0, 0), rows)
-    keep_rows = keep_of_rows(keep_mask, rows, nz, nx, own_tokens, total)
+    summed, keep_rows = lax.optimization_barrier((summed, keep_rows))
     both, hidden_kept = pointwise(lax.all_to_all(summed, "y", 0, 0), keep_rows)
     both = lax.all_gather(both, ("y", "c"))
 
-    result = input_grad(both, turned, nx)
-    result, hidden_kept = lax.optimization_barrier((result, hidden_kept))
-    arrived = lax.all_to_all(result, "x", 0, 0)
+    arrived = lax.all_to_all(input_grad(both, w_gate, w_up, nx), "x", 0, 0)
+    kept = x_sum(arrived, nz)
+    blocks = (own_in, right_in, left_in, far_in, own_cot, right_cot, left_cot, far_cot)
+    kept, hidden_kept, both, blocks = lax.optimization_barrier((kept, hidden_kept, both, blocks))
+    grad_input = z_sum(lax.all_to_all(kept, "z", 0, 0), own_tokens, width)
+
     all_kept = lax.all_gather(hidden_kept, ("y", "c")).reshape(total, hidden)
-    all_inputs = jnp.concatenate([own[0], right[0], left[0], far_in])
-    all_cotangent = jnp.concatenate([own[1], right[1], left[1], far_cot])
-    arrived, all_kept, all_inputs, all_cotangent = lax.optimization_barrier(
-        (arrived, all_kept, all_inputs, all_cotangent)
-    )
-    kept = x_sum(arrived, nz)
-    kept, all_kept, all_inputs, all_cotangent, both = lax.optimization_barrier(
-        (kept, all_kept, all_inputs, all_cotangent, both)
-    )
-    grad_input = z_sum(lax.all_to_all(kept, "z", 0, 0), own_tokens, width)
-
+    all_inputs, all_cotangent = jnp.concatenate(blocks[:nx]), jnp.concatenate(blocks[nx:])
     both = both.reshape(total, 2 * hidden)
     grad_down = dot(all_kept, all_cotangent, OUTER).astype(BF16)
     grad_gate = dot(all_inputs, both[:, :hidden], OUTER).astype(BF16)

time: 175 us -> 164 us (0.937)
  blocking collectives: 71.4 us -> 110 us
  waiting for transfers between devices: 36.9 us -> 7.96 us
  local copies, waits for them, and re-layouts: 11.6 us -> 1.92 us
  other arithmetic: 6.02 us -> 0.14 us
  Pallas kernels: 13.5 us -> 10.3 us
  starting transfers between devices: 27.4 us -> 25.4 us
    all_to_all x0 -> x2, blocking collectives: none -> 38.6 us  [the longest x1 23.5 us: shards(): arrived = lax.all_to_all(input_grad(both, w_gate, w_up, nx), 'x', 0, 0)]
    all_to_all x1, waiting for transfers between devices: 18.4 us -> 4.01 us  [shards(): grad_input = z_sum(lax.all_to_all(kept, 'z', 0, 0), own_tokens, width)]
    all_to_all x2 -> x0, waiting for transfers between devices: 9.74 us -> none  [the longest x1 9.42 us: shards(): both, hidden_kept = pointwise(lax.all_to_all(summed, 'y', 0, 0), keep_rows)]
    all_to_all x2 -> x0, starting transfers between devices: 8.97 us -> none  [the longest x1 4.5 us: shards(): arrived = lax.all_to_all(result, 'x', 0, 0)]
    ppermute x4 -> x6, starting transfers between devices: 11.8 us -> 18.7 us  [the longest x1 4.32 us: shards(): right_cot = lax.ppermute(own_cot, 'x', ring(nx, 1))]
    ppermute x4 -> x6, waiting for transfers between devices: 8.81 us -> 3.94 us  [the longest x1 1.9 us: shards(): far_cot = lax.ppermute(left_cot, 'x', ring(nx, -1))]
    concatenate x3 -> x0, other arithmetic: 4.76 us -> none  [the longest x1 2.4 us: shards(): all_cotangent = jnp.concatenate([own[1], right[1], left[1], far_cot])]
    squeeze x3 -> x0, local copies, waits for them, and re-layouts: 4.14 us -> none  [the longest x2 2.09 us: shards(): all_cotangent = jnp.concatenate([own[1], right[1], left[1], far_cot])]
  transfers between devices with their start and end apart: 7 -> 7, of which waited for: 5 -> 4; matrix products, arithmetic and copies ran while one was open for 10% -> 4% of each run, Pallas kernels for 2% -> 3%
where the time goes in v4:
time: 164 us; the launch traced here: 162 us
  blocking collectives  110 us (67%)
  starting transfers between devices  25.4 us (15%)
  Pallas kernels  10.3 us (6%)
  waiting for transfers between devices  7.96 us (5%)
  matrix products  5.47 us (3%)
  local copies, waits for them, and re-layouts  1.92 us (1%)
    all_gather x1, blocking collectives, shards(): along_z = lax.all_gather(pack(inputs, cotangent), 'z')  40.3 us
    all_to_all x1, blocking collectives, shards(): arrived = lax.all_to_all(input_grad(both, w_gate, w_up, nx), 'x', 0, 0)  23.5 us
    all_to_all x1, blocking collectives, shards(): both, hidden_kept = pointwise(lax.all_to_all(summed, 'y', 0, 0), keep_rows)  15.1 us
    all_gather x1, blocking collectives, shards(): both = lax.all_gather(both, ('y', 'c'))  13.5 us
    all_gather x1, blocking collectives, shards(): all_kept = lax.all_gather(hidden_kept, ('y', 'c')).reshape(total, hidden)  13 us
    all_to_all x1, starting transfers between devices, shards(): grad_input = z_sum(lax.all_to_all(kept, 'z', 0, 0), own_tokens, width)  6.65 us
    pallas_call x4, Pallas kernels, forward(): pl.pallas_call(functools.partial(forward_kernel, rows), out_shape=jax.Sha...  5.75 us
    dot_general x3, matrix products, dot(): return lax.dot_general(a, b, dims, preferred_element_type=F32)  5.47 us
  transfers between devices with their start and end apart: 7, of which 4 were waited for; matrix products, arithmetic and copies ran while one was open for 4% of the time, Pallas kernels for 3%

profile of v4, /device:TPU:6, one launch (start us, length us, event | category | flops | bytes accessed | tf_op | source)
XLA Modules:
  0.0 162.1 jit_solution(8706029129999483889)
XLA Ops:
  0.7 0.8 copy-done.5
  1.5 0.8 copy-done.6
  2.3 40.3 %all-gather = bf16[256,1536]{1,0:T(8,128)(2,1)S(1)} all-gather(bf16[16,1536]{1,0:T(8,128)(2,1)S(1)} %pack.1), channel_id=2, replica_groups=mesh['z'=16,'x'=4,'y'=4,'c'=2] {'z'}, dimensions={0}, use_global_device_ids=true | all-gather | bytes 835584 | tf_op jit(solution)/shard_map/all_gather | solution.py:301
  42.5 0.8 unpack.1
  43.3 2.4 %collective-permute-start = (bf16[192,1024]{1,0:T(8,128)(2,1)S(1)}, bf16[192,1024]{1,0:T(8,128)(2,1)S(1)}, u32[]{:S(2)}, u32[]{:S(2)}) collective-permute-start(bf16[192,1024]{1,0:T(8,128)(2,1)S(1)} %get-tuple-element.28.x_ref), channel_id=1, source_target_pairs={{0,8},{8,16},{16,24},{24,0},{1,9},{9,17},{17,25},{25,1},{2,10},{10... | collective-permute-start | bytes 1179656 | tf_op jit(solution)/shard_map/ppermute | solution.py:309
  45.7 3.5 %collective-permute-start.2 = (bf16[192,1024]{1,0:T(8,128)(2,1)}, bf16[192,1024]{1,0:T(8,128)(2,1)}, u32[]{:S(2)}, u32[]{:S(2)}) collective-permute-start(bf16[192,1024]{1,0:T(8,128)(2,1)} %get-tuple-element.34.c_ref), channel_id=1, source_target_pairs={{0,24},{8,0},{16,8},{24,16},{1,25},{9,1},{17,9},{25,17},{2,26},{10... | collective-permute-start | bytes 1179656 | tf_op jit(solution)/shard_map/ppermute | solution.py:310
  49.2 2.7 %collective-permute-start.4 = (bf16[192,1024]{1,0:T(8,128)(2,1)S(1)}, bf16[192,1024]{1,0:T(8,128)(2,1)S(1)}, u32[]{:S(2)}, u32[]{:S(2)}) collective-permute-start(bf16[192,1024]{1,0:T(8,128)(2,1)S(1)} %get-tuple-element.28.x_ref), channel_id=1, source_target_pairs={{0,24},{8,0},{16,8},{24,16},{1,25},{9,1},{17,9},{25,17},{2,26},{10... | collective-permute-start | bytes 1179656 | tf_op jit(solution)/shard_map/ppermute | solution.py:312
  51.9 4.3 %collective-permute-start.5 = (bf16[192,1024]{1,0:T(8,128)(2,1)}, bf16[192,1024]{1,0:T(8,128)(2,1)}, u32[]{:S(2)}, u32[]{:S(2)}) collective-permute-start(bf16[192,1024]{1,0:T(8,128)(2,1)} %get-tuple-element.34.c_ref), channel_id=1, source_target_pairs={{0,8},{8,16},{16,24},{24,0},{1,9},{9,17},{17,25},{25,1},{2,10},{10... | collective-permute-start | bytes 1179656 | tf_op jit(solution)/shard_map/ppermute | solution.py:311
  56.3 1.7 %forward_chunk.4.rest_0_ = s16[2,4,304,256]{3,2,1,0:T(8,128)(2,1)S(1)} custom-call(bf16[192,1024]{1,0:T(8,128)(2,1)S(1)} %get-tuple-element.28.x_ref, bf16[192,1024]{1,0:T(8,128)(2,1)} %get-tuple-element.34.c_ref, bf16[1024,256]{1,0:T(8,128)(2,1)S(1)} %copy-done, bf16[1024,256]{1,0:T(8,128)(2,1)S(1)} %copy-done.1, bf16[256,1024]{1,0:T(8,128)(2,1)S(1)} %copy-done.2), custom_call_target="tpu_custom_call" | custom-call | flops 301989888 | bytes 2359296 | tf_op jit(solution)/shard_map/forward_chunk/pallas_call | solution.py:143
  58.0 2.4 %collective-permute-start.1 = (bf16[192,1024]{1,0:T(8,128)(2,1)S(1)}, bf16[192,1024]{1,0:T(8,128)(2,1)S(1)}, u32[]{:S(2)}, u32[]{:S(2)}) collective-permute-start(bf16[192,1024]{1,0:T(8,128)(2,1)S(1)} %collective-permute-done.x_ref), channel_id=1, source_target_pairs={{0,8},{8,16},{16,24},{24,0},{1,9},{9,17},{17,25},{25,1},{2,10},{10... | collective-permute-start | bytes 1179656 | tf_op jit(solution)/shard_map/ppermute | solution.py:313
  60.4 3.5 %collective-permute-start.3 = (bf16[192,1024]{1,0:T(8,128)(2,1)}, bf16[192,1024]{1,0:T(8,128)(2,1)S(1)}, u32[]{:S(2)}, u32[]{:S(2)}) collective-permute-start(bf16[192,1024]{1,0:T(8,128)(2,1)} %collective-permute-done.2.c_ref), channel_id=1, source_target_pairs={{0,24},{8,0},{16,8},{24,16},{1,25},{9,1},{17,9},{25,17},{2,26},{10... | collective-permute-start | bytes 1179656 | tf_op jit(solution)/shard_map/ppermute | solution.py:314
  64.2 1.3 collective-permute-done.5.c_ref
  65.5 1.7 %forward_chunk.5.rest_0_ = s16[2,4,304,256]{3,2,1,0:T(8,128)(2,1)S(1)} custom-call(bf16[192,1024]{1,0:T(8,128)(2,1)S(1)} %collective-permute-done.x_ref, bf16[192,1024]{1,0:T(8,128)(2,1)} %collective-permute-done.5.c_ref, bf16[1024,256]{1,0:T(8,128)(2,1)S(1)} %copy-done, bf16[1024,256]{1,0:T(8,128)(2,1)S(1)} %copy-done.1, ...), custom_call_target="tpu_custom_call", output_to_operand_aliasing={{}: (5, {})} | custom-call | flops 301989888 | bytes 2359296 | tf_op jit(solution)/shard_map/forward_chunk/pallas_call | solution.py:143
  67.2 1.7 %forward_chunk.6.rest_0_ = s16[2,4,304,256]{3,2,1,0:T(8,128)(2,1)S(1)} custom-call(bf16[192,1024]{1,0:T(8,128)(2,1)S(1)} %collective-permute-done.4.x_ref, bf16[192,1024]{1,0:T(8,128)(2,1)} %collective-permute-done.2.c_ref, bf16[1024,256]{1,0:T(8,128)(2,1)S(1)} %copy-done, bf16[1024,256]{1,0:T(8,128)(2,1)S(1)} %copy-done.1, ...), custom_call_target="tpu_custom_call", output_to_operand_aliasing={{}: (5, {})} | custom-call | flops 301989888 | bytes 2359296 | tf_op jit(solution)/shard_map/forward_chunk/pallas_call | solution.py:143
  68.9 0.7 collective-permute-done.1.x_ref
  69.6 1.9 %collective-permute-done.3.c_ref = bf16[192,1024]{1,0:T(8,128)(2,1)S(1)} collective-permute-done((bf16[192,1024]{1,0:T(8,128)(2,1)}, bf16[192,1024]{1,0:T(8,128)(2,1)S(1)}, u32[]{:S(2)}, u32[]{:S(2)}) %collective-permute-start.3) | collective-permute-done | bytes 393248 | tf_op jit(solution)/shard_map/ppermute | solution.py:314
  71.5 0.7 forward_chunk.7
  72.3 4.7 %all_to_all.20.in_ref = s16[2,4,304,256]{3,2,1,0:T(8,128)(2,1)S(1)} all-to-all(s16[2,4,304,256]{3,2,1,0:T(8,128)(2,1)S(1)} %forward_chunk.7), channel_id=1, replica_groups=mesh['z'=16,'x'=4,'y'=4,'c'=2] {'c'}, dimensions={0} | all-to-all | bytes 2490368 | tf_op jit(solution)/shard_map/all_to_all | solution.py:321
  77.0 0.8 core_sum.1
  77.8 15.1 %all_to_all.21.in_ref = s16[4,304,256]{2,1,0:T(8,128)(2,1)S(1)} all-to-all(s16[4,304,256]{2,1,0:T(8,128)(2,1)S(1)} %core_sum.1), channel_id=1, replica_groups=mesh['z'=16,'x'=4,'y'=4,'c'=2] {'y'}, dimensions={0} | all-to-all | bytes 1245184 | tf_op jit(solution)/shard_map/all_to_all | solution.py:323
  92.9 0.3 pointwise.1
  93.2 13.5 %all-gather.1 = bf16[768,512]{1,0:T(8,128)(2,1)S(1)} all-gather(bf16[96,512]{1,0:T(8,128)(2,1)S(1)} %get-tuple-element.25), channel_id=3, replica_groups=mesh['z'=16,'x'=4,'y'=4,'c'=2] {'y','c'}, dimensions={0}, use_global_device_ids=true | all-gather | bytes 884736 | tf_op jit(solution)/shard_map/all_gather | solution.py:324
  106.7 1.0 input_grad.1
  107.7 23.5 %all_to_all.22.in_ref = bf16[4,192,1024]{2,1,0:T(8,128)(2,1)S(1)} all-to-all(bf16[4,192,1024]{2,1,0:T(8,128)(2,1)S(1)} %input_grad.1), channel_id=1, replica_groups=mesh['z'=16,'x'=4,'y'=4,'c'=2] {'x'}, dimensions={0} | all-to-all | bytes 3145728 | tf_op jit(solution)/shard_map/all_to_all | solution.py:326
  131.2 1.0 x_sum.1
  132.1 6.6 %all-to-all-start.3 = ((bf16[16,8,1536]{2,1,0:T(8,128)(2,1)}), bf16[16,8,1536]{2,1,0:T(8,128)(2,1)S(1)}, u32[]{:S(2)}, u32[]{:S(2)}) async-start(bf16[16,8,1536]{2,1,0:T(8,128)(2,1)} %x_sum.1), calls=%async_computation.3 | async-start | bytes 786432 | tf_op jit(solution)/shard_map/all_to_all | solution.py:330
  138.9 13.0 %all-gather.2 = bf16[768,256]{1,0:T(8,128)(2,1)S(1)} all-gather(bf16[96,256]{1,0:T(8,128)(2,1)S(1)} %get-tuple-element.33), channel_id=4, replica_groups=mesh['z'=16,'x'=4,'y'=4,'c'=2] {'y','c'}, dimensions={0}, use_global_device_ids=true | all-gather | bytes 442368 | tf_op jit(solution)/shard_map/all_gather | solution.py:332
  151.9 1.4 convolution_convert_fusion
  153.3 1.4 convolution_convert_fusion.1
  154.8 2.6 %fusion.8 = bf16[256,1024]{1,0:T(8,128)(2,1)} fusion(bf16[768,256]{1,0:T(8,128)(2,1)S(1)} %all-gather.2, bf16[192,1024]{1,0:T(8,128)(2,1)S(1)} %copy-done.4, bf16[192,1024]{1,0:T(8,128)(2,1)} %collective-permute-done.2.c_ref, bf16[192,1024]{1,0:T(8,128)(2,1)} %collective-permute-done.5.c_ref, bf16[192,1024]{1,0:T(8,128)(2,1)} %get-tuple-element.34.c_ref), kind=kOutput, calls=%fused_computation.8 | convolution fusion | flops 409206784 | bytes 2490368 | tf_op jit(solution)/shard_map/dot_general | solution.py:23
  157.4 4.0 %all-to-all-done.3.in_ref = bf16[16,8,1536]{2,1,0:T(8,128)(2,1)S(1)} async-done(((bf16[16,8,1536]{2,1,0:T(8,128)(2,1)}), bf16[16,8,1536]{2,1,0:T(8,128)(2,1)S(1)}, u32[]{:S(2)}, u32[]{:S(2)}) %all-to-all-start.3) | async-done | bytes 393248 | tf_op jit(solution)/shard_map/all_to_all | solution.py:330
  161.4 0.7 z_sum.1
  (28 shorter events, 0.5 us)
Async XLA Ops:
  0.6 55.7 %copy-start.1 = (bf16[1024,256]{1,0:T(8,128)(2,1)S(1)}, bf16[1024,256]{1,0:T(8,128)(2,1)}, u32[]{:S(2)}) copy-start(bf16[1024,256]{1,0:T(8,128)(2,1)} %wu_ref.9) | copy-start | bytes 1572868
  0.6 55.7 %copy-start = (bf16[1024,256]{1,0:T(8,128)(2,1)S(1)}, bf16[1024,256]{1,0:T(8,128)(2,1)}, u32[]{:S(2)}) copy-start(bf16[1024,256]{1,0:T(8,128)(2,1)} %wg_ref.9) | copy-start | bytes 1572868
  0.7 0.8 copy-start.5
  1.5 0.8 copy-start.6
  2.3 54.0 %copy-start.7 = (s32[12,2]{0,1:T(2,128)S(1)}, s32[12,2]{0,1:T(2,128)}, u32[]{:S(2)}) copy-start(s32[12,2]{0,1:T(2,128)} %param.11) | copy-start | bytes 292
  2.3 54.1 %copy-start.2 = (bf16[256,1024]{1,0:T(8,128)(2,1)S(1)}, bf16[256,1024]{1,0:T(8,128)(2,1)}, u32[]{:S(2)}) copy-start(bf16[256,1024]{1,0:T(8,128)(2,1)} %wd_ref.7) | copy-start | bytes 1572868
  43.3 14.7 %collective-permute-start = (bf16[192,1024]{1,0:T(8,128)(2,1)S(1)}, bf16[192,1024]{1,0:T(8,128)(2,1)S(1)}, u32[]{:S(2)}, u32[]{:S(2)}) collective-permute-start(bf16[192,1024]{1,0:T(8,128)(2,1)S(1)} %get-tuple-element.28.x_ref), channel_id=1, source_target_pairs={{0,8},{8,16},{16,24},{24,0},{1,9},{9,17},{17,25},{25,1},{2,10},{10... | collective-permute-start | bytes 1179656 | tf_op jit(solution)/shard_map/ppermute | solution.py:309
  45.7 14.7 %collective-permute-start.2 = (bf16[192,1024]{1,0:T(8,128)(2,1)}, bf16[192,1024]{1,0:T(8,128)(2,1)}, u32[]{:S(2)}, u32[]{:S(2)}) collective-permute-start(bf16[192,1024]{1,0:T(8,128)(2,1)} %get-tuple-element.34.c_ref), channel_id=1, source_target_pairs={{0,24},{8,0},{16,8},{24,16},{1,25},{9,1},{17,9},{25,17},{2,26},{10... | collective-permute-start | bytes 1179656 | tf_op jit(solution)/shard_map/ppermute | solution.py:310
  49.2 18.0 %collective-permute-start.4 = (bf16[192,1024]{1,0:T(8,128)(2,1)S(1)}, bf16[192,1024]{1,0:T(8,128)(2,1)S(1)}, u32[]{:S(2)}, u32[]{:S(2)}) collective-permute-start(bf16[192,1024]{1,0:T(8,128)(2,1)S(1)} %get-tuple-element.28.x_ref), channel_id=1, source_target_pairs={{0,24},{8,0},{16,8},{24,16},{1,25},{9,1},{17,9},{25,17},{2,26},{10... | collective-permute-start | bytes 1179656 | tf_op jit(solution)/shard_map/ppermute | solution.py:312
  51.9 13.6 %collective-permute-start.5 = (bf16[192,1024]{1,0:T(8,128)(2,1)}, bf16[192,1024]{1,0:T(8,128)(2,1)}, u32[]{:S(2)}, u32[]{:S(2)}) collective-permute-start(bf16[192,1024]{1,0:T(8,128)(2,1)} %get-tuple-element.34.c_ref), channel_id=1, source_target_pairs={{0,8},{8,16},{16,24},{24,0},{1,9},{9,17},{17,25},{25,1},{2,10},{10... | collective-permute-start | bytes 1179656 | tf_op jit(solution)/shard_map/ppermute | solution.py:311
  58.0 11.6 %collective-permute-start.1 = (bf16[192,1024]{1,0:T(8,128)(2,1)S(1)}, bf16[192,1024]{1,0:T(8,128)(2,1)S(1)}, u32[]{:S(2)}, u32[]{:S(2)}) collective-permute-start(bf16[192,1024]{1,0:T(8,128)(2,1)S(1)} %collective-permute-done.x_ref), channel_id=1, source_target_pairs={{0,8},{8,16},{16,24},{24,0},{1,9},{9,17},{17,25},{25,1},{2,10},{10... | collective-permute-start | bytes 1179656 | tf_op jit(solution)/shard_map/ppermute | solution.py:313
  60.4 11.1 %collective-permute-start.3 = (bf16[192,1024]{1,0:T(8,128)(2,1)}, bf16[192,1024]{1,0:T(8,128)(2,1)S(1)}, u32[]{:S(2)}, u32[]{:S(2)}) collective-permute-start(bf16[192,1024]{1,0:T(8,128)(2,1)} %collective-permute-done.2.c_ref), channel_id=1, source_target_pairs={{0,24},{8,0},{16,8},{24,16},{1,25},{9,1},{17,9},{25,17},{2,26},{10... | collective-permute-start | bytes 1179656 | tf_op jit(solution)/shard_map/ppermute | solution.py:314
  71.5 0.7 copy-start.3
  132.1 29.3 %all-to-all-start.3 = ((bf16[16,8,1536]{2,1,0:T(8,128)(2,1)}), bf16[16,8,1536]{2,1,0:T(8,128)(2,1)S(1)}, u32[]{:S(2)}, u32[]{:S(2)}) async-start(bf16[16,8,1536]{2,1,0:T(8,128)(2,1)} %x_sum.1), calls=%async_computation.3 | async-start | bytes 786432 | tf_op jit(solution)/shard_map/all_to_all | solution.py:330
  153.3 1.4 copy-start.4

commit v5 on v4

--- a/solution.py
+++ b/solution.py
@@ -69,29 +69,23 @@
 
 
 def unpack_kernel(packed_ref, *out_refs):
-    blocks = packed_ref.shape[0]
+    blocks = packed_ref.shape[0] // 2
     width = out_refs[0].shape[1]
-    half = width // 2
-    for first in range(0, blocks, 2):
-        pair = [packed_ref[first + i].astype(F32) for i in range(2)]
-        for which in range(2):
-            part = [p[which * 8 : which * 8 + 8] for p in pair]
-            out_refs[which][first * 8 : first * 8 + 16] = jnp.concatenate(
-                [p[:, :width] for p in part]
-            ).astype(BF16)
-    for first in range(0, blocks, 4):
-        four = [packed_ref[first + i, :, width:].astype(F32) for i in range(4)]
-        for which in range(2):
-            part = [p[which * 8 : which * 8 + 8] for p in four]
-            rows = jnp.concatenate(
-                [
-                    jnp.concatenate([p[:4] for p in part]),
-                    jnp.concatenate([p[4:] for p in part]),
-                ],
-                axis=1,
-            )
-            place = blocks * 8 + first * 4
-            out_refs[which][place : place + 16] = rows.astype(BF16)
+    for odd in range(2):
+        base = odd * 12 * blocks
+        for first in range(0, blocks, 2):
+            pair = [packed_ref[2 * (first + i) + odd].astype(F32) for i in range(2)]
+            for which in range(2):
+                rows = jnp.concatenate([p[which * 8 : which * 8 + 8, :width] for p in pair])
+                place = base + first * 8
+                out_refs[which][place : place + 16] = rows.astype(BF16)
+        for first in range(0, blocks, 4):
+            four = [packed_ref[2 * (first + i) + odd, :, width:].astype(F32) for i in range(4)]
+            for which in range(2):
+                part = [p[which * 8 : which * 8 + 8] for p in four]
+                halves = [jnp.concatenate([p[h : h + 4] for p in part]) for h in (0, 4)]
+                place = base + 8 * blocks + first * 4
+                out_refs[which][place : place + 16] = jnp.concatenate(halves, axis=1).astype(BF16)
 
 
 def pack_kernel(*refs):
@@ -195,12 +189,13 @@
     )(arrived, keep_rows)
 
 
-def keep_of_rows(keep_mask, rows, nz, nx, own_tokens, total):
+def keep_of_rows(keep_mask, rows, nx, own_tokens, total):
     tiles, blocks = keep_mask.shape
     chunk = lax.axis_index("y")
-    place = lax.axis_index("c") * rows + lax.broadcasted_iota(jnp.int32, (rows, 1), 0)
-    rest = place - 8 * nz
-    z = jnp.where(rest < 0, place // 8, rest // 4)
+    place = lax.broadcasted_iota(jnp.int32, (rows, 1), 0)
+    blocks_of_8 = rows // own_tokens * 8
+    rest = place - blocks_of_8
+    z = 2 * jnp.where(rest < 0, place // 8, rest // 4) + lax.axis_index("c")
     inside = jnp.where(rest < 0, place % 8, 8 + rest % 4)
     shift = jnp.where(chunk == 1, -1, jnp.where(chunk == 2, 1, jnp.where(chunk == 3, 2, 0)))
     token = (z * nx + (lax.axis_index("x") + shift + nx) % nx) * own_tokens + inside
@@ -216,7 +211,7 @@
 def input_grad_kernel(chunks, g_ref, wg_ref, wu_ref, out_ref):
     parts, rows, depth = g_ref.shape
     width, hidden = wg_ref.shape
-    tokens = parts * rows // chunks
+    tokens = parts * rows // (2 * chunks)
     g = g_ref[...].reshape(parts * rows, depth)
     x = lax.axis_index("x")
     for first in range(0, width, 256):
@@ -225,18 +220,20 @@
         product = (product + dot(g[:, hidden:], wu_ref[columns], INNER)).astype(BF16)
         for k, away in enumerate((0, -1, 1, 2)):
             owner = lax.rem(x + (away + chunks), chunks)
-            out_ref[owner, :, columns] = product[k * tokens : (k + 1) * tokens]
+            for odd in range(2):
+                place = (2 * k + odd) * tokens
+                out_ref[odd * chunks + owner, :, columns] = product[place : place + tokens]
 
 
 def input_grad(both, w_gate, w_up, chunks):
     parts, rows, depth = both.shape
     width = w_gate.shape[0]
-    tokens = parts * rows // chunks
+    tokens = parts * rows // (2 * chunks)
     return pl.pallas_call(
         functools.partial(input_grad_kernel, chunks),
-        out_shape=jax.ShapeDtypeStruct((chunks, tokens, width), BF16),
+        out_shape=jax.ShapeDtypeStruct((2 * chunks, tokens, width), BF16),
         compiler_params=params(8),
-        cost_estimate=cost(2 * chunks * tokens * width * depth, 2 * depth * width),
+        cost_estimate=cost(4 * chunks * tokens * width * depth, 2 * depth * width),
         name="input_grad",
     )(both, w_gate, w_up)
 
@@ -259,11 +256,11 @@
             out_ref[first + i] = block.astype(BF16)
 
 
-def x_sum(arrived, nz):
+def x_sum(arrived, blocks):
     width = arrived.shape[2]
     return pl.pallas_call(
         x_sum_kernel,
-        out_shape=jax.ShapeDtypeStruct((nz, 8, 3 * width // 2), BF16),
+        out_shape=jax.ShapeDtypeStruct((blocks, 8, 3 * width // 2), BF16),
         cost_estimate=cost(0, 2 * arrived.size),
         compiler_params=params(5),
         name="x_sum",
@@ -298,7 +295,7 @@
     rows = tokens // nc
     weights = (w_gate, w_up, w_down)
 
-    along_z = lax.all_gather(pack(inputs, cotangent), "z")
+    along_z = lax.all_gather(pack(inputs, cotangent), ("zq", "zb"))
     own_in, own_cot = pl.pallas_call(
         unpack_kernel,
         out_shape=(jax.ShapeDtypeStruct((tokens, width), BF16),) * 2,
@@ -317,30 +314,35 @@
     parts = forward(2, left_in, left_cot, weights, parts, nx)
     parts = forward(3, far_in, far_cot, weights, parts, nx)
 
-    keep_rows = keep_of_rows(keep_mask, rows, nz, nx, own_tokens, total)
+    keep_rows = keep_of_rows(keep_mask, rows, nx, own_tokens, total)
     summed = core_sum(lax.all_to_all(parts, "c", 0, 0), rows)
     summed, keep_rows = lax.optimization_barrier((summed, keep_rows))
     both, hidden_kept = pointwise(lax.all_to_all(summed, "y", 0, 0), keep_rows)
     both = lax.all_gather(both, ("y", "c"))
 
-    arrived = lax.all_to_all(input_grad(both, w_gate, w_up, nx), "x", 0, 0)
-    kept = x_sum(arrived, nz)
-    blocks = (own_in, right_in, left_in, far_in, own_cot, right_cot, left_cot, far_cot)
-    kept, hidden_kept, both, blocks = lax.optimization_barrier((kept, hidden_kept, both, blocks))
-    grad_input = z_sum(lax.all_to_all(kept, "z", 0, 0), own_tokens, width)
-
+    result = input_grad(both, w_gate, w_up, nx)
+    xs, cs = (own_in, right_in, left_in, far_in), (own_cot, right_cot, left_cot, far_cot)
+    result, hidden_kept, both, xs = lax.optimization_barrier((result, hidden_kept, both, xs))
+    arrived = lax.all_to_all(result, ("zb", "x"), 0, 0)
     all_kept = lax.all_gather(hidden_kept, ("y", "c")).reshape(total, hidden)
-    all_inputs, all_cotangent = jnp.concatenate(blocks[:nx]), jnp.concatenate(blocks[nx:])
     both = both.reshape(total, 2 * hidden)
-    grad_down = dot(all_kept, all_cotangent, OUTER).astype(BF16)
+    all_inputs = jnp.concatenate(xs)
     grad_gate = dot(all_inputs, both[:, :hidden], OUTER).astype(BF16)
     grad_up = dot(all_inputs, both[:, hidden:], OUTER).astype(BF16)
+    arrived, all_kept, grad_gate, grad_up = lax.optimization_barrier(
+        (arrived, all_kept, grad_gate, grad_up)
+    )
+
+    kept = x_sum(arrived, nz // 2)
+    kept, all_kept, cs = lax.optimization_barrier((kept, all_kept, cs))
+    grad_down = dot(all_kept, jnp.concatenate(cs), OUTER).astype(BF16)
+    grad_input = z_sum(lax.all_to_all(kept, "zq", 0, 0), own_tokens, width)
     return grad_input, grad_gate, grad_up, grad_down
 
 
 def solution(mesh):
-    fine = Mesh(mesh.devices.reshape(16, 4, 4, 2), ("z", "x", "y", "c"))
-    hid, mdl = ("z", "x"), ("y", "c")
+    fine = Mesh(mesh.devices.reshape(8, 2, 4, 4, 2), ("zq", "zb", "x", "y", "c"))
+    hid, mdl = ("zq", "zb", "x"), ("y", "c")
     placed = (P(hid, mdl), P(hid, mdl), P(mdl, hid), P(mdl, hid), P(hid, mdl), P(None, hid))
     return jax.shard_map(
         shards,

time: 164 us -> 160 us (0.976)
  blocking collectives: 110 us -> 86.5 us
  waiting for transfers between devices: 7.96 us -> 25 us
  starting transfers between devices: 25.4 us -> 29 us
    all_to_all x1 -> x0, blocking collectives: 23.5 us -> none  [shards(): arrived = lax.all_to_all(input_grad(both, w_gate, w_up, nx), 'x', 0, 0)]
    all_to_all x1 -> x2, waiting for transfers between devices: 4.01 us -> 18.8 us  [the longest x1 16 us: shards(): grad_input = z_sum(lax.all_to_all(kept, 'zq', 0, 0), own_tokens, width)]
    all_to_all x1 -> x2, starting transfers between devices: 6.65 us -> 11.4 us  [the longest x1 6.84 us: shards(): grad_input = z_sum(lax.all_to_all(kept, 'zq', 0, 0), own_tokens, width)]
    ppermute x1, waiting for transfers between devices: 0.01 us -> 2.69 us  [shards(): left_in = lax.ppermute(own_in, 'x', ring(nx, -1))]
    ppermute x1, starting transfers between devices: 2.39 us -> 4.07 us  [shards(): far_in = lax.ppermute(right_in, 'x', ring(nx, 1))]
  transfers between devices with their start and end apart: 7 -> 8, of which waited for: 4 -> 5; matrix products, arithmetic and copies ran while one was open for 4% -> 4% of each run, Pallas kernels for 3% -> 3%
where the time goes in v5:
time: 160 us; the launch traced here: 159 us
  blocking collectives  86.5 us (54%)
  starting transfers between devices  29 us (18%)
  waiting for transfers between devices  25 us (16%)
  Pallas kernels  9.66 us (6%)
  matrix products  5.36 us (3%)
  local copies, waits for them, and re-layouts  2.82 us (2%)
    all_gather x1, blocking collectives, shards(): along_z = lax.all_gather(pack(inputs, cotangent), ('zq', 'zb'))  40.3 us
    all_to_all x1, waiting for transfers between devices, shards(): grad_input = z_sum(lax.all_to_all(kept, 'zq', 0, 0), own_tokens, width)  16 us
    all_to_all x1, blocking collectives, shards(): both, hidden_kept = pointwise(lax.all_to_all(summed, 'y', 0, 0), keep_rows)  15.1 us
    all_gather x1, blocking collectives, shards(): both = lax.all_gather(both, ('y', 'c'))  13.5 us
    all_gather x1, blocking collectives, shards(): all_kept = lax.all_gather(hidden_kept, ('y', 'c')).reshape(total, hidden)  13 us
    all_to_all x1, starting transfers between devices, shards(): grad_input = z_sum(lax.all_to_all(kept, 'zq', 0, 0), own_tokens, width)  6.84 us
    dot_general x3, matrix products, dot(): return lax.dot_general(a, b, dims, preferred_element_type=F32)  5.36 us
    pallas_call x4, Pallas kernels, forward(): pl.pallas_call(functools.partial(forward_kernel, rows), out_shape=jax.Sha...  4.75 us
  transfers between devices with their start and end apart: 8, of which 5 were waited for; matrix products, arithmetic and copies ran while one was open for 4% of the time, Pallas kernels for 3%

profile of v5, /device:TPU:6, one launch (start us, length us, event | category | flops | bytes accessed | tf_op | source)
XLA Modules:
  0.0 159.5 jit_solution(13408313939360303424)
XLA Ops:
  0.7 0.8 copy-done.11
  1.5 0.8 copy-done.12
  2.3 40.3 %all-gather = bf16[256,1536]{1,0:T(8,128)(2,1)S(1)} all-gather(bf16[16,1536]{1,0:T(8,128)(2,1)S(1)} %pack.1), channel_id=2, replica_groups=mesh['zq'=8,'zb'=2,'x'=4,'y'=4,'c'=2] {'zq','zb'}, dimensions={0}, use_global_device_ids=true | all-gather | bytes 835584 | tf_op jit(solution)/shard_map/all_gather | solution.py:298
  42.6 2.4 %collective-permute-start = (bf16[192,1024]{1,0:T(8,128)(2,1)S(1)}, bf16[192,1024]{1,0:T(8,128)(2,1)S(1)}, u32[]{:S(2)}, u32[]{:S(2)}) collective-permute-start(bf16[192,1024]{1,0:T(8,128)(2,1)S(1)} %get-tuple-element.35.x_ref), channel_id=1, source_target_pairs={{0,8},{8,16},{16,24},{24,0},{1,9},{9,17},{17,25},{25,1},{2,10},{10... | collective-permute-start | bytes 1179656 | tf_op jit(solution)/shard_map/ppermute | solution.py:306
  45.0 3.5 %collective-permute-start.2 = (bf16[192,1024]{1,0:T(8,128)(2,1)S(1)}, bf16[192,1024]{1,0:T(8,128)(2,1)}, u32[]{:S(2)}, u32[]{:S(2)}) collective-permute-start(bf16[192,1024]{1,0:T(8,128)(2,1)S(1)} %get-tuple-element.46.c_ref), channel_id=1, source_target_pairs={{0,24},{8,0},{16,8},{24,16},{1,25},{9,1},{17,9},{25,17},{2,26},{10... | collective-permute-start | bytes 1179656 | tf_op jit(solution)/shard_map/ppermute | solution.py:307
  48.5 3.6 %collective-permute-start.5 = (bf16[192,1024]{1,0:T(8,128)(2,1)S(1)}, bf16[192,1024]{1,0:T(8,128)(2,1)}, u32[]{:S(2)}, u32[]{:S(2)}) collective-permute-start(bf16[192,1024]{1,0:T(8,128)(2,1)S(1)} %get-tuple-element.46.c_ref), channel_id=1, source_target_pairs={{0,8},{8,16},{16,24},{24,0},{1,9},{9,17},{17,25},{25,1},{2,10},{10... | collective-permute-start | bytes 1179656 | tf_op jit(solution)/shard_map/ppermute | solution.py:308
  52.1 2.2 %collective-permute-start.4 = (bf16[192,1024]{1,0:T(8,128)(2,1)S(1)}, bf16[192,1024]{1,0:T(8,128)(2,1)S(1)}, u32[]{:S(2)}, u32[]{:S(2)}) collective-permute-start(bf16[192,1024]{1,0:T(8,128)(2,1)S(1)} %get-tuple-element.35.x_ref), channel_id=1, source_target_pairs={{0,24},{8,0},{16,8},{24,16},{1,25},{9,1},{17,9},{25,17},{2,26},{10... | collective-permute-start | bytes 1179656 | tf_op jit(solution)/shard_map/ppermute | solution.py:309
  54.4 0.7 forward_chunk.4.rest_0_
  55.1 0.7 collective-permute-done.x_ref
  55.9 4.1 %collective-permute-start.1 = (bf16[192,1024]{1,0:T(8,128)(2,1)S(1)}, bf16[192,1024]{1,0:T(8,128)(2,1)S(1)}, u32[]{:S(2)}, u32[]{:S(2)}) collective-permute-start(bf16[192,1024]{1,0:T(8,128)(2,1)S(1)} %collective-permute-done.x_ref), channel_id=1, source_target_pairs={{0,8},{8,16},{16,24},{24,0},{1,9},{9,17},{17,25},{25,1},{2,10},{10... | collective-permute-start | bytes 1179656 | tf_op jit(solution)/shard_map/ppermute | solution.py:310
  60.0 1.9 %collective-permute-start.3 = (bf16[192,1024]{1,0:T(8,128)(2,1)}, bf16[192,1024]{1,0:T(8,128)(2,1)S(1)}, u32[]{:S(2)}, u32[]{:S(2)}) collective-permute-start(bf16[192,1024]{1,0:T(8,128)(2,1)} %collective-permute-done.2.c_ref), channel_id=1, source_target_pairs={{0,24},{8,0},{16,8},{24,16},{1,25},{9,1},{17,9},{25,17},{2,26},{10... | collective-permute-start | bytes 1179656 | tf_op jit(solution)/shard_map/ppermute | solution.py:311
  62.2 1.7 %forward_chunk.5.rest_0_ = s16[2,4,304,256]{3,2,1,0:T(8,128)(2,1)S(1)} custom-call(bf16[192,1024]{1,0:T(8,128)(2,1)S(1)} %collective-permute-done.x_ref, bf16[192,1024]{1,0:T(8,128)(2,1)} %collective-permute-done.5.c_ref, bf16[1024,256]{1,0:T(8,128)(2,1)S(1)} %copy-done, bf16[1024,256]{1,0:T(8,128)(2,1)S(1)} %copy-done.1, ...), custom_call_target="tpu_custom_call", output_to_operand_aliasing={{}: (5, {})} | custom-call | flops 301989888 | bytes 2359296 | tf_op jit(solution)/shard_map/forward_chunk/pallas_call | solution.py:137
  63.9 2.7 %collective-permute-done.4.x_ref = bf16[192,1024]{1,0:T(8,128)(2,1)S(1)} collective-permute-done((bf16[192,1024]{1,0:T(8,128)(2,1)S(1)}, bf16[192,1024]{1,0:T(8,128)(2,1)S(1)}, u32[]{:S(2)}, u32[]{:S(2)}) %collective-permute-start.4) | collective-permute-done | bytes 393248 | tf_op jit(solution)/shard_map/ppermute | solution.py:309
  66.6 1.7 %forward_chunk.6.rest_0_ = s16[2,4,304,256]{3,2,1,0:T(8,128)(2,1)S(1)} custom-call(bf16[192,1024]{1,0:T(8,128)(2,1)S(1)} %collective-permute-done.4.x_ref, bf16[192,1024]{1,0:T(8,128)(2,1)} %collective-permute-done.2.c_ref, bf16[1024,256]{1,0:T(8,128)(2,1)S(1)} %copy-done, bf16[1024,256]{1,0:T(8,128)(2,1)S(1)} %copy-done.1, ...), custom_call_target="tpu_custom_call", output_to_operand_aliasing={{}: (5, {})} | custom-call | flops 301989888 | bytes 2359296 | tf_op jit(solution)/shard_map/forward_chunk/pallas_call | solution.py:137
  68.3 2.8 %collective-permute-done.3.c_ref = bf16[192,1024]{1,0:T(8,128)(2,1)S(1)} collective-permute-done((bf16[192,1024]{1,0:T(8,128)(2,1)}, bf16[192,1024]{1,0:T(8,128)(2,1)S(1)}, u32[]{:S(2)}, u32[]{:S(2)}) %collective-permute-start.3) | collective-permute-done | bytes 393248 | tf_op jit(solution)/shard_map/ppermute | solution.py:311
  71.1 0.7 forward_chunk.7
  71.8 4.7 %all_to_all.20.in_ref = s16[2,4,304,256]{3,2,1,0:T(8,128)(2,1)S(1)} all-to-all(s16[2,4,304,256]{3,2,1,0:T(8,128)(2,1)S(1)} %forward_chunk.7), channel_id=1, replica_groups=mesh['zq'=8,'zb'=2,'x'=4,'y'=4,'c'=2] {'c'}, dimensions={0} | all-to-all | bytes 2490368 | tf_op jit(solution)/shard_map/all_to_all | solution.py:318
  76.5 0.8 core_sum.1
  77.4 15.1 %all_to_all.21.in_ref = s16[4,304,256]{2,1,0:T(8,128)(2,1)S(1)} all-to-all(s16[4,304,256]{2,1,0:T(8,128)(2,1)S(1)} %core_sum.1), channel_id=1, replica_groups=mesh['zq'=8,'zb'=2,'x'=4,'y'=4,'c'=2] {'y'}, dimensions={0} | all-to-all | bytes 1245184 | tf_op jit(solution)/shard_map/all_to_all | solution.py:320
  92.8 13.5 %all-gather.1 = bf16[768,512]{1,0:T(8,128)(2,1)S(1)} all-gather(bf16[96,512]{1,0:T(8,128)(2,1)S(1)} %get-tuple-element.31), channel_id=3, replica_groups=mesh['zq'=8,'zb'=2,'x'=4,'y'=4,'c'=2] {'y','c'}, dimensions={0}, use_global_device_ids=true | all-gather | bytes 884736 | tf_op jit(solution)/shard_map/all_gather | solution.py:321
  106.2 2.2 %input_grad.1 = bf16[8,96,1024]{2,1,0:T(8,128)(2,1)} custom-call(bf16[8,96,512]{2,1,0:T(8,128)(2,1)S(1)} %bitcast.11, bf16[1024,256]{1,0:T(8,128)(2,1)S(1)} %copy-done, bf16[1024,256]{1,0:T(8,128)(2,1)S(1)} %copy-done.1), custom_call_target="tpu_custom_call" | custom-call | flops 805306368 | bytes 1048576 | tf_op jit(solution)/shard_map/input_grad/pallas_call | solution.py:232
  108.4 4.5 %all-to-all-start.2 = ((bf16[8,96,1024]{2,1,0:T(8,128)(2,1)}), bf16[8,96,1024]{2,1,0:T(8,128)(2,1)S(1)}, u32[]{:S(2)}, u32[]{:S(2)}) async-start(bf16[8,96,1024]{2,1,0:T(8,128)(2,1)} %input_grad.1), calls=%async_computation.2 | async-start | bytes 3145728 | tf_op jit(solution)/shard_map/all_to_all | solution.py:326
  113.0 0.9 copy-done.4
  114.0 13.0 %all-gather.2 = bf16[768,256]{1,0:T(8,128)(2,1)S(1)} all-gather(bf16[96,256]{1,0:T(8,128)(2,1)S(1)} %copy-done.10), channel_id=4, replica_groups=mesh['zq'=8,'zb'=2,'x'=4,'y'=4,'c'=2] {'y','c'}, dimensions={0}, use_global_device_ids=true | all-gather | bytes 442368 | tf_op jit(solution)/shard_map/all_gather | solution.py:327
  126.9 1.4 convolution_convert_fusion
  128.4 1.4 convolution_convert_fusion.1
  129.8 2.7 %all-to-all-done.2.in_ref = bf16[8,96,1024]{2,1,0:T(8,128)(2,1)S(1)} async-done(((bf16[8,96,1024]{2,1,0:T(8,128)(2,1)}), bf16[8,96,1024]{2,1,0:T(8,128)(2,1)S(1)}, u32[]{:S(2)}, u32[]{:S(2)}) %all-to-all-start.2) | async-done | bytes 1572896 | tf_op jit(solution)/shard_map/all_to_all | solution.py:326
  132.5 0.9 x_sum.1
  133.4 6.8 %all-to-all-start.3 = ((bf16[8,8,1536]{2,1,0:T(8,128)(2,1)}), bf16[8,8,1536]{2,1,0:T(8,128)(2,1)S(1)}, u32[]{:S(2)}, u32[]{:S(2)}) async-start(bf16[8,8,1536]{2,1,0:T(8,128)(2,1)} %x_sum.1), calls=%async_computation.3 | async-start | bytes 393216 | tf_op jit(solution)/shard_map/all_to_all | solution.py:339
  140.3 2.5 %fusion.8 = bf16[256,1024]{1,0:T(8,128)(2,1)} fusion(bf16[768,256]{1,0:T(8,128)(2,1)S(1)} %all-gather.2, bf16[192,1024]{1,0:T(8,128)(2,1)S(1)} %copy-done.8, bf16[192,1024]{1,0:T(8,128)(2,1)} %collective-permute-done.2.c_ref, bf16[192,1024]{1,0:T(8,128)(2,1)} %collective-permute-done.5.c_ref, bf16[192,1024]{1,0:T(8,128)(2,1)S(1)} %copy-done.6), kind=kOutput, calls=%fused_computation.8 | convolution fusion | flops 409206784 | bytes 2490368 | tf_op jit(solution)/shard_map/dot_general | solution.py:23
  142.8 16.0 %all-to-all-done.3.in_ref = bf16[8,8,1536]{2,1,0:T(8,128)(2,1)S(1)} async-done(((bf16[8,8,1536]{2,1,0:T(8,128)(2,1)}), bf16[8,8,1536]{2,1,0:T(8,128)(2,1)S(1)}, u32[]{:S(2)}, u32[]{:S(2)}) %all-to-all-start.3) | async-done | bytes 196640 | tf_op jit(solution)/shard_map/all_to_all | solution.py:339
  158.8 0.6 z_sum.1
  (41 shorter events, 0.9 us)
Async XLA Ops:
  0.6 53.8 %copy-start.2 = (bf16[256,1024]{1,0:T(8,128)(2,1)S(1)}, bf16[256,1024]{1,0:T(8,128)(2,1)}, u32[]{:S(2)}) copy-start(bf16[256,1024]{1,0:T(8,128)(2,1)} %wd_ref.7) | copy-start | bytes 1572868
  0.6 53.8 %copy-start = (bf16[1024,256]{1,0:T(8,128)(2,1)S(1)}, bf16[1024,256]{1,0:T(8,128)(2,1)}, u32[]{:S(2)}) copy-start(bf16[1024,256]{1,0:T(8,128)(2,1)} %wg_ref.9) | copy-start | bytes 1572868
  0.7 0.8 copy-start.11
  1.5 0.8 copy-start.12
  2.3 52.1 %copy-start.13 = (s32[12,2]{0,1:T(2,128)S(1)}, s32[12,2]{0,1:T(2,128)}, u32[]{:S(2)}) copy-start(s32[12,2]{0,1:T(2,128)} %param.11) | copy-start | bytes 292
  2.3 52.2 %copy-start.1 = (bf16[1024,256]{1,0:T(8,128)(2,1)S(1)}, bf16[1024,256]{1,0:T(8,128)(2,1)}, u32[]{:S(2)}) copy-start(bf16[1024,256]{1,0:T(8,128)(2,1)} %wu_ref.9) | copy-start | bytes 1572868
  42.6 12.5 %copy-start.5 = (bf16[192,1024]{1,0:T(8,128)(2,1)}, bf16[192,1024]{1,0:T(8,128)(2,1)S(1)}, u32[]{:S(2)}) copy-start(bf16[192,1024]{1,0:T(8,128)(2,1)S(1)} %get-tuple-element.46.c_ref) | copy-start | bytes 1179652
  42.6 13.2 %collective-permute-start = (bf16[192,1024]{1,0:T(8,128)(2,1)S(1)}, bf16[192,1024]{1,0:T(8,128)(2,1)S(1)}, u32[]{:S(2)}, u32[]{:S(2)}) collective-permute-start(bf16[192,1024]{1,0:T(8,128)(2,1)S(1)} %get-tuple-element.35.x_ref), channel_id=1, source_target_pairs={{0,8},{8,16},{16,24},{24,0},{1,9},{9,17},{17,25},{25,1},{2,10},{10... | collective-permute-start | bytes 1179656 | tf_op jit(solution)/shard_map/ppermute | solution.py:306
  45.0 14.9 %collective-permute-start.2 = (bf16[192,1024]{1,0:T(8,128)(2,1)S(1)}, bf16[192,1024]{1,0:T(8,128)(2,1)}, u32[]{:S(2)}, u32[]{:S(2)}) collective-permute-start(bf16[192,1024]{1,0:T(8,128)(2,1)S(1)} %get-tuple-element.46.c_ref), channel_id=1, source_target_pairs={{0,24},{8,0},{16,8},{24,16},{1,25},{9,1},{17,9},{25,17},{2,26},{10... | collective-permute-start | bytes 1179656 | tf_op jit(solution)/shard_map/ppermute | solution.py:307
  48.5 13.7 %collective-permute-start.5 = (bf16[192,1024]{1,0:T(8,128)(2,1)S(1)}, bf16[192,1024]{1,0:T(8,128)(2,1)}, u32[]{:S(2)}, u32[]{:S(2)}) collective-permute-start(bf16[192,1024]{1,0:T(8,128)(2,1)S(1)} %get-tuple-element.46.c_ref), channel_id=1, source_target_pairs={{0,8},{8,16},{16,24},{24,0},{1,9},{9,17},{17,25},{25,1},{2,10},{10... | collective-permute-start | bytes 1179656 | tf_op jit(solution)/shard_map/ppermute | solution.py:308
  52.1 14.5 %collective-permute-start.4 = (bf16[192,1024]{1,0:T(8,128)(2,1)S(1)}, bf16[192,1024]{1,0:T(8,128)(2,1)S(1)}, u32[]{:S(2)}, u32[]{:S(2)}) collective-permute-start(bf16[192,1024]{1,0:T(8,128)(2,1)S(1)} %get-tuple-element.35.x_ref), channel_id=1, source_target_pairs={{0,24},{8,0},{16,8},{24,16},{1,25},{9,1},{17,9},{25,17},{2,26},{10... | collective-permute-start | bytes 1179656 | tf_op jit(solution)/shard_map/ppermute | solution.py:309
  55.9 12.4 %collective-permute-start.1 = (bf16[192,1024]{1,0:T(8,128)(2,1)S(1)}, bf16[192,1024]{1,0:T(8,128)(2,1)S(1)}, u32[]{:S(2)}, u32[]{:S(2)}) collective-permute-start(bf16[192,1024]{1,0:T(8,128)(2,1)S(1)} %collective-permute-done.x_ref), channel_id=1, source_target_pairs={{0,8},{8,16},{16,24},{24,0},{1,9},{9,17},{17,25},{25,1},{2,10},{10... | collective-permute-start | bytes 1179656 | tf_op jit(solution)/shard_map/ppermute | solution.py:310
  60.0 11.1 %collective-permute-start.3 = (bf16[192,1024]{1,0:T(8,128)(2,1)}, bf16[192,1024]{1,0:T(8,128)(2,1)S(1)}, u32[]{:S(2)}, u32[]{:S(2)}) collective-permute-start(bf16[192,1024]{1,0:T(8,128)(2,1)} %collective-permute-done.2.c_ref), channel_id=1, source_target_pairs={{0,24},{8,0},{16,8},{24,16},{1,25},{9,1},{17,9},{25,17},{2,26},{10... | collective-permute-start | bytes 1179656 | tf_op jit(solution)/shard_map/ppermute | solution.py:311
  68.3 3.5 %copy-start.3 = (bf16[192,1024]{1,0:T(8,128)(2,1)}, bf16[192,1024]{1,0:T(8,128)(2,1)S(1)}, u32[]{:S(2)}) copy-start(bf16[192,1024]{1,0:T(8,128)(2,1)S(1)} %collective-permute-done.1.x_ref) | copy-start | bytes 1179652
  71.1 0.7 copy-start.7
  92.7 15.7 %copy-start.9 = (bf16[96,256]{1,0:T(8,128)(2,1)}, bf16[96,256]{1,0:T(8,128)(2,1)S(1)}, u32[]{:S(2)}) copy-start(bf16[96,256]{1,0:T(8,128)(2,1)S(1)} %get-tuple-element.34) | copy-start | bytes 147460
  108.4 24.1 %all-to-all-start.2 = ((bf16[8,96,1024]{2,1,0:T(8,128)(2,1)}), bf16[8,96,1024]{2,1,0:T(8,128)(2,1)S(1)}, u32[]{:S(2)}, u32[]{:S(2)}) async-start(bf16[8,96,1024]{2,1,0:T(8,128)(2,1)} %input_grad.1), calls=%async_computation.2 | async-start | bytes 3145728 | tf_op jit(solution)/shard_map/all_to_all | solution.py:326
  112.9 1.0 copy-start.4
  112.9 1.0 copy-start.10
  129.8 10.5 %copy-start.6 = (bf16[192,1024]{1,0:T(8,128)(2,1)S(1)}, bf16[192,1024]{1,0:T(8,128)(2,1)}, u32[]{:S(2)}) copy-start(bf16[192,1024]{1,0:T(8,128)(2,1)} %copy-done.5) | copy-start | bytes 1179652
  129.8 10.5 %copy-start.8 = (bf16[192,1024]{1,0:T(8,128)(2,1)S(1)}, bf16[192,1024]{1,0:T(8,128)(2,1)}, u32[]{:S(2)}) copy-start(bf16[192,1024]{1,0:T(8,128)(2,1)} %copy-done.7) | copy-start | bytes 1179652
  133.4 25.4 %all-to-all-start.3 = ((bf16[8,8,1536]{2,1,0:T(8,128)(2,1)}), bf16[8,8,1536]{2,1,0:T(8,128)(2,1)S(1)}, u32[]{:S(2)}, u32[]{:S(2)}) async-start(bf16[8,8,1536]{2,1,0:T(8,128)(2,1)} %x_sum.1), calls=%async_computation.3 | async-start | bytes 393216 | tf_op jit(solution)/shard_map/all_to_all | solution.py:339

commit v6 on v5

v6 whole, which is shorter than its diff:
```python
import functools

import jax
import jax.numpy as jnp
from jax import lax
from jax.experimental import pallas as pl
from jax.experimental.pallas import tpu as pltpu
from jax.sharding import Mesh, PartitionSpec as P

F32, BF16, I16 = jnp.float32, jnp.bfloat16, jnp.int16
INNER = (((1,), (1,)), ((), ()))
PLAIN = (((1,), (0,)), ((), ()))
OUTER = (((0,), (0,)), ((), ()))
SUMS = 6
SCALES = 16


def ring(size, step):
    return [(i, (i + step) % size) for i in range(size)]


def dot(a, b, dims):
    return lax.dot_general(a, b, dims, preferred_element_type=F32)


def params(mebibytes):
    return pltpu.CompilerParams(vmem_limit_bytes=mebibytes << 20)


def cost(flops, moved):
    return pl.CostEstimate(flops=flops, bytes_accessed=moved, transcendentals=0)


def row_is_lane(rows, lanes):
    shape = (rows, lanes)
    return lax.broadcasted_iota(jnp.int32, shape, 0) == lax.broadcasted_iota(jnp.int32, shape, 1)


def code(values):
    rows, lanes = values[0].shape
    diagonal = row_is_lane(rows, lanes)
    place = lax.broadcasted_iota(jnp.int32, (SCALES, lanes), 0)
    codes, tile = [], jnp.zeros((SCALES, lanes), F32)
    for k, v in enumerate(values):
        most = jnp.max(jnp.abs(v), axis=1, keepdims=True)
        exponent = jnp.ceil(jnp.log2(jnp.maximum(most, 1e-30)) + 0.01)
        codes.append(jnp.round(v * jnp.exp2(15.0 - exponent)).astype(jnp.int32).astype(I16))
        along = jnp.sum(jnp.where(diagonal, exponent, 0.0), axis=0, keepdims=True)
        tile = jnp.where(place == k, along, tile)
    return codes, tile.astype(jnp.int32).astype(I16)


def decode(block, rows):
    lanes = block.shape[1]
    diagonal = row_is_lane(rows, lanes)
    tile = jnp.exp2(block[SUMS * rows :].astype(jnp.int32).astype(F32) - 15.0)
    out = []
    for k in range(SUMS):
        scale = jnp.sum(jnp.where(diagonal, tile[k : k + 1], 0.0), axis=1, keepdims=True)
        out.append(block[k * rows : (k + 1) * rows].astype(jnp.int32).astype(F32) * scale)
    return out


def put(out_ref, index, values, rows):
    codes, tile = code(values)
    for k, c in enumerate(codes):
        out_ref[(*index, pl.ds(k * rows, rows))] = c
    out_ref[(*index, pl.ds(SUMS * rows, SCALES))] = tile


def unpack_kernel(packed_ref, out_ref):
    blocks = packed_ref.shape[0] // 2
    width = out_ref.shape[2]
    for odd in range(2):
        base = odd * 12 * blocks
        for first in range(0, blocks, 2):
            pair = [packed_ref[2 * (first + i) + odd].astype(F32) for i in range(2)]
            for which in range(2):
                rows = jnp.concatenate([p[which * 8 : which * 8 + 8, :width] for p in pair])
                place = base + first * 8
                out_ref[which, place : place + 16] = rows.astype(BF16)
        for first in range(0, blocks, 4):
            four = [packed_ref[2 * (first + i) + odd, :, width:].astype(F32) for i in range(4)]
            for which in range(2):
                part = [p[which * 8 : which * 8 + 8] for p in four]
                halves = [jnp.concatenate([p[h : h + 4] for p in part]) for h in (0, 4)]
                place = base + 8 * blocks + first * 4
                out_ref[which, place : place + 16] = jnp.concatenate(halves, axis=1).astype(BF16)


def pack_kernel(*refs):
    packed = []
    for ref in refs[:-1]:
        a = ref[...].astype(F32)
        half = a.shape[1] // 2
        tail = jnp.concatenate([a[8:, :half], a[8:, half:]])
        packed.append(jnp.concatenate([a[:8], tail], axis=1))
    refs[-1][...] = jnp.concatenate(packed).astype(BF16)


def pack(*arrays):
    width = arrays[0].shape[1]
    return pl.pallas_call(
        pack_kernel,
        out_shape=jax.ShapeDtypeStruct((8 * len(arrays), 3 * width // 2), BF16),
        cost_estimate=cost(0, 48 * len(arrays) * width),
        compiler_params=params(2),
        name="pack",
    )(*arrays)


def stack_kernel(wg_ref, wu_ref, wd_ref, out_ref, sems):
    hidden, width = wd_ref.shape
    copies = [(wg_ref, out_ref.at[0]), (wu_ref, out_ref.at[1])]
    for first in range(0, width, hidden):
        part = pl.ds(first, hidden)
        copies.append((wd_ref.at[:, part], out_ref.at[2, part]))
    copies = [pltpu.make_async_copy(a, b, sems.at[i]) for i, (a, b) in enumerate(copies)]
    for c in copies:
        c.start()
    for c in copies:
        c.wait()


def stack_weights(w_gate, w_up, w_down):
    width, hidden = w_gate.shape
    spec = pl.BlockSpec(memory_space=pl.ANY)
    return pl.pallas_call(
        stack_kernel,
        out_shape=jax.ShapeDtypeStruct((3, width, hidden), BF16),
        in_specs=[spec] * 3,
        out_specs=spec,
        scratch_shapes=[pltpu.SemaphoreType.DMA((2 + width // hidden,))],
        compiler_params=params(1),
        cost_estimate=cost(0, 12 * width * hidden),
        name="stack_weights",
    )(w_gate, w_up, w_down)


def forward_kernel(rows, tokens_ref, *refs):
    out_ref = refs[-1]
    x, c = tokens_ref[0], tokens_ref[1]
    values = []
    wg_ref, wu_ref, wd_ref, pair_ref = refs[:4]
    hidden, width = wd_ref.shape
    values += [dot(x, w_ref[...], PLAIN) for w_ref in (wg_ref, wu_ref)]
    values.append(dot(c, wd_ref[...], INNER))
    values += [dot(x, pair_ref[i], PLAIN) for i in range(2)]
    blocks = [slice(first, first + hidden) for first in range(0, width, hidden)]
    products = [dot(c[:, b], pair_ref[2, b], INNER) for b in blocks]
    values.append(sum(products[1:], products[0]))
    cores, chunks = out_ref.shape[:2]
    for chunk in range(chunks):
        for core in range(cores):
            place = (chunk * cores + core) * rows
            put(out_ref, (core, chunk), [v[place : place + rows] for v in values], rows)


def forward(half, tokens, weights, held, rows, cores, chunks):
    hidden = weights[0].shape[1]
    coded = SUMS * rows + SCALES
    specs = [pl.BlockSpec(a.shape, lambda i, n=a.ndim: (0,) * n) for a in (tokens, *weights)]
    operands, alias = [tokens, *weights], {}
    if held is not None:
        operands.append(held)
        specs.append(pl.BlockSpec(memory_space=pl.ANY))
        alias = {5: 0}
    return pl.pallas_call(
        functools.partial(forward_kernel, rows),
        out_shape=jax.ShapeDtypeStruct((cores, chunks, coded, hidden), I16),
        grid=(1,),
        in_specs=specs,
        out_specs=pl.BlockSpec((cores, chunks // 2, coded, hidden), lambda i: (0, half, 0, 0)),
        input_output_aliases=alias,
        compiler_params=params(16),
        cost_estimate=cost(6 * tokens.size * hidden, 2 * tokens.size + 12 * weights[0].size),
        name="forward",
    )(*operands)


def core_sum_kernel(rows, in_ref, out_ref):
    for chunk in range(in_ref.shape[1]):
        both = [decode(in_ref[i, chunk], rows) for i in range(2)]
        put(out_ref, (chunk,), [a + b for a, b in zip(*both)], rows)


def core_sum(arrived, rows):
    return pl.pallas_call(
        functools.partial(core_sum_kernel, rows),
        out_shape=jax.ShapeDtypeStruct(arrived.shape[1:], I16),
        cost_estimate=cost(0, 3 * arrived.size),
        compiler_params=params(5),
        name="core_sum",
    )(arrived)


def pointwise_kernel(rows, in_ref, both_ref, *kept_refs):
    parts = [decode(in_ref[i], rows) for i in range(in_ref.shape[0])]
    sums = [sum(p[1:], p[0]) for p in zip(*parts)]
    hidden = sums[0].shape[1]
    for which, kept_ref in enumerate(kept_refs):
        gate_pre, up_pre, grad_hidden = sums[3 * which : 3 * which + 3]
        sigmoid_gate = jax.nn.sigmoid(gate_pre)
        silu_gate = gate_pre * sigmoid_gate
        slope = sigmoid_gate * (1.0 + gate_pre * (1.0 - sigmoid_gate))
        first = 2 * which * hidden
        both_ref[:, first : first + hidden] = (grad_hidden * up_pre * slope).astype(BF16)
        both_ref[:, first + hidden : first + 2 * hidden] = (grad_hidden * silu_gate).astype(BF16)
        kept_ref[...] = (silu_gate * up_pre).astype(BF16)


def pointwise(arrived, rows):
    hidden = arrived.shape[2]
    one = jax.ShapeDtypeStruct((rows, hidden), BF16)
    return pl.pallas_call(
        functools.partial(pointwise_kernel, rows),
        out_shape=(jax.ShapeDtypeStruct((rows, 4 * hidden), BF16), one, one),
        compiler_params=params(4),
        cost_estimate=cost(0, 2 * arrived.size),
        name="pointwise",
    )(arrived)


def pieces(refs, which, columns):
    return jnp.concatenate([r[which, :, columns] for r in refs])


def gate_up_kernel(both_ref, pair_ref, *refs):
    *tokens, gate_ref, up_ref = refs
    parts, rows, depth = both_ref.shape
    hidden = gate_ref.shape[1]
    grads = both_ref[:, :, : depth // 2].reshape(parts * rows, depth // 2)
    grads = jnp.concatenate([grads, pair_ref[...]])
    for first in range(0, gate_ref.shape[0], 256):
        columns = slice(first, first + 256)
        total = dot(pieces(tokens, 0, columns), grads, OUTER).astype(BF16)
        gate_ref[columns] = total[:, :hidden]
        up_ref[columns] = total[:, hidden:]


def gate_up_grads(both, pair, tokens):
    width, hidden = tokens[0].shape[2], pair.shape[1] // 2
    return pl.pallas_call(
        gate_up_kernel,
        out_shape=(jax.ShapeDtypeStruct((width, hidden), BF16),) * 2,
        compiler_params=params(10),
        cost_estimate=cost(16 * pair.size * width, 8 * tokens[0].size),
        name="gate_up_grads",
    )(both, pair, *tokens)


def down_kernel(kept_ref, keep_ref, *refs):
    *tokens, out_ref = refs
    rows = kept_ref.shape[1] // 2
    kept = [
        kept_ref[:, i * rows : (i + 1) * rows].reshape(keep_ref.shape[1:]) * keep_ref[i]
        for i in range(2)
    ]
    kept = jnp.concatenate(kept)
    for first in range(0, out_ref.shape[1], 256):
        columns = slice(first, first + 256)
        out_ref[:, columns] = dot(kept, pieces(tokens, 1, columns), OUTER).astype(BF16)


def down_grad(kept, keep, tokens):
    width, hidden = tokens[0].shape[2], kept.shape[2]
    return pl.pallas_call(
        down_kernel,
        out_shape=jax.ShapeDtypeStruct((hidden, width), BF16),
        compiler_params=params(9),
        cost_estimate=cost(2 * kept.size * width, 8 * tokens[0].size),
        name="down_grad",
    )(kept, keep, *tokens)


def keep_of_tokens(keep_mask, x, tokens, nx, own_tokens, total):
    tiles, blocks = keep_mask.shape
    row = lax.broadcasted_iota(jnp.int32, (tokens, 1), 0)
    per_kind = tokens // 4
    place, eights = row % per_kind, per_kind // own_tokens * 8
    rest = place - eights
    z = 2 * jnp.where(rest < 0, place // 8, rest // 4) + row // per_kind % 2
    inside = jnp.where(rest < 0, place % 8, 8 + rest % 4)
    other = row // (2 * per_kind)
    from_x = x + other * (1 - 2 * (x % 2))
    tile = ((z * nx + from_x) * own_tokens + inside) // (total // tiles)
    chosen = tile == lax.broadcasted_iota(jnp.int32, (tokens, tiles), 1)
    keep = [
        jnp.sum(jnp.where(chosen, keep_mask[:, b][None, :], 0), axis=1, keepdims=True)
        for b in range(blocks)
    ]
    return jnp.concatenate([jnp.broadcast_to(k, (tokens, 128)) for k in keep], axis=1).astype(BF16)


def input_grad_kernel(g_ref, wg_ref, wu_ref, pair_ref, out_ref):
    chunks, rows, width = out_ref.shape
    hidden = wg_ref.shape[1]
    xl = lax.axis_index("xl")
    g = g_ref[...].reshape(chunks * rows, 4 * hidden)
    for first in range(0, width, 256):
        columns = slice(first, first + 256)
        places = (wg_ref[columns], wu_ref[columns], pair_ref[0, columns], pair_ref[1, columns])
        product = dot(g[:, :hidden], places[0], INNER)
        for i, w in enumerate(places[1:], 1):
            product = product + dot(g[:, i * hidden : (i + 1) * hidden], w, INNER)
        product = product.astype(BF16)
        for k in range(2):
            owner = lax.rem(xl + k, 2)
            for odd in range(2):
                place = (2 * k + odd) * rows
                out_ref[2 * odd + owner, :, columns] = product[place : place + rows]


def input_grad(both, weights, chunks):
    parts, rows, depth = both.shape
    width = weights[0].shape[0]
    tokens = parts * rows
    return pl.pallas_call(
        input_grad_kernel,
        out_shape=jax.ShapeDtypeStruct((chunks, tokens // chunks, width), BF16),
        compiler_params=params(10),
        cost_estimate=cost(2 * tokens * width * depth, 2 * depth * width),
        name="input_grad",
    )(both, *weights)


def x_sum_kernel(in_ref, out_ref):
    blocks = out_ref.shape[0]
    width = in_ref.shape[2]
    half = width // 2
    for first in range(0, blocks, 4):
        main = pl.ds(first * 8, 32)
        rest = pl.ds(blocks * 8 + first * 4, 16)
        main, rest = (
            sum((in_ref[i, rows].astype(F32) for i in range(1, in_ref.shape[0])), in_ref[0, rows].astype(F32))
            for rows in (main, rest)
        )
        for i in range(4):
            tail = rest[4 * i : 4 * i + 4]
            tail = jnp.concatenate([tail[:, :half], tail[:, half:]])
            block = jnp.concatenate([main[8 * i : 8 * i + 8], tail], axis=1)
            out_ref[first + i] = block.astype(BF16)


def x_sum(arrived, blocks):
    width = arrived.shape[2]
    return pl.pallas_call(
        x_sum_kernel,
        out_shape=jax.ShapeDtypeStruct((blocks, 8, 3 * width // 2), BF16),
        cost_estimate=cost(0, 2 * arrived.size),
        compiler_params=params(5),
        name="x_sum",
    )(arrived)


def z_sum_kernel(in_ref, out_ref):
    width = out_ref.shape[1]
    total = in_ref[0].astype(F32)
    for i in range(1, in_ref.shape[0]):
        total = total + in_ref[i].astype(F32)
    tail = jnp.concatenate([total[:4, width:], total[4:, width:]], axis=1)
    out_ref[...] = jnp.concatenate([total[:, :width], tail]).astype(BF16)


def z_sum(arrived, own_tokens, width):
    return pl.pallas_call(
        z_sum_kernel,
        out_shape=jax.ShapeDtypeStruct((own_tokens, width), BF16),
        cost_estimate=cost(0, 2 * arrived.size),
        compiler_params=params(3),
        name="z_sum",
    )(arrived)


def shards(inputs, cotangent, w_gate, w_up, w_down, keep_mask):
    own_tokens, width = inputs.shape
    hidden = w_gate.shape[1]
    nz, nx, ny, nc = 16, 4, 4, 2
    total = own_tokens * nz * nx
    tokens = total // 2
    rows = tokens // (ny * nc)

    def to_partner(a):
        return lax.ppermute(a, ("xh", "xl"), [(0, 3), (3, 0), (1, 2), (2, 1)])

    w_2 = to_partner(stack_weights(w_gate, w_up, w_down))
    along_z = lax.all_gather(pack(inputs, cotangent), ("zq", "zb"))
    own = pl.pallas_call(
        unpack_kernel,
        out_shape=jax.ShapeDtypeStruct((2, tokens // 2, width), BF16),
        cost_estimate=cost(0, 4 * tokens * width),
        compiler_params=params(6),
        name="unpack",
    )(along_z)
    other = lax.ppermute(own, "xl", ring(2, 1))
    weights = (w_gate, w_up, w_down, w_2)

    parts = forward(0, own, weights, None, rows, nc, ny)
    parts = forward(1, other, weights, parts, rows, nc, ny)
    summed = core_sum(lax.all_to_all(parts, "c", 0, 0), rows)
    own_2 = to_partner(own)
    summed, own_2, other_late = lax.optimization_barrier((summed, own_2, other))
    other_2 = to_partner(other_late)
    both, kept, kept_2 = pointwise(lax.all_to_all(summed, "y", 0, 0), rows)
    both = lax.all_gather(both, ("y", "c"))
    both, other_2 = lax.optimization_barrier((both, other_2))

    result = input_grad(both, (w_gate, w_up, w_2), nx)
    result, both, kept, kept_2 = lax.optimization_barrier((result, both, kept, kept_2))
    arrived = lax.all_to_all(result, ("zb", "xl"), 0, 0)
    both_2 = to_partner(both.reshape(tokens, 4 * hidden)[:, 2 * hidden :])
    kept = jnp.concatenate([kept, to_partner(kept_2)])
    x = lax.axis_index(("xh", "xl"))
    keep = jnp.stack(
        [
            keep_of_tokens(keep_mask, at, tokens, nx, own_tokens, total)
            for at in (x, nx - 1 - x)
        ]
    )
    arrived, kept, keep = lax.optimization_barrier((arrived, kept, keep))

    grad_sum = x_sum(arrived, nz // 2)
    grad_sum, kept = lax.optimization_barrier((grad_sum, kept))
    grad_input = z_sum(lax.all_to_all(grad_sum, "zq", 0, 0), own_tokens, width)
    kept = lax.all_gather(kept, ("y", "c"))
    places = (own, other, own_2, other_2)
    grad_gate, grad_up = gate_up_grads(both, both_2, places)
    grad_down = down_grad(kept, keep, places)
    return grad_input, grad_gate, grad_up, grad_down


def solution(mesh):
    fine = Mesh(mesh.devices.reshape(8, 2, 2, 2, 4, 2), ("zq", "zb", "xh", "xl", "y", "c"))
    hid, mdl = ("zq", "zb", "xh", "xl"), ("y", "c")
    placed = (P(hid, mdl), P(hid, mdl), P(mdl, hid), P(mdl, hid), P(hid, mdl), P(None, hid))
    return jax.shard_map(
        shards,
        mesh=fine,
        in_specs=placed,
        out_specs=(P(hid, mdl), P(mdl, hid), P(mdl, hid), P(hid, mdl)),
        check_vma=False,
    )
```

time: 160 us -> 152 us (0.950)
  the two profiles are of different devices: /device:TPU:6 before, /device:TPU:1 now
where the time goes in v6:
time: 152 us
  blocking collectives  75 us (49%)
  starting transfers between devices  32.7 us (22%)
  waiting for transfers between devices  18.6 us (12%)
  Pallas kernels  13.9 us (9%)
  local copies, waits for them, and re-layouts  8.81 us (6%)
  other arithmetic  1.56 us (1%)
    all_gather x1, blocking collectives, shards(): along_z = lax.all_gather(pack(inputs, cotangent), ('zq', 'zb'))  34.9 us
    ppermute x5, starting transfers between devices, to_partner(): return lax.ppermute(a, ('xh', 'xl'), [(0, 3), (3, 0), (1, 2), (2, 1)])  16.5 us
    all_gather x1, blocking collectives, shards(): both = lax.all_gather(both, ('y', 'c'))  14.7 us
    all_gather x1, blocking collectives, shards(): kept = lax.all_gather(kept, ('y', 'c'))  13.9 us
    all_to_all x1, blocking collectives, shards(): summed = core_sum(lax.all_to_all(parts, 'c', 0, 0), rows)  11.4 us
    ppermute x1, waiting for transfers between devices, shards(): other = lax.ppermute(own, 'xl', ring(2, 1))  9.3 us
    all_to_all x1, waiting for transfers between devices, shards(): both, kept, kept_2 = pointwise(lax.all_to_all(summed, 'y', 0, 0), rows)  7.8 us
    unnamed x40, local copies, waits for them, and re-layouts  7.58 us
  transfers between devices with their start and end apart: 9, of which 3 were waited for; matrix products, arithmetic and copies ran while one was open for 2% of the time, Pallas kernels for 7%

profile of v6, /device:TPU:1, one launch (start us, length us, event | category | flops | bytes accessed | tf_op | source)
XLA Modules:
  0.0 151.6 jit_solution(15275246163330895351)
XLA Ops:
  0.6 1.0 copy-done
  1.7 1.0 copy-done.2
  2.7 1.0 copy-done.6
  4.0 5.3 %collective-permute-start.1 = (bf16[3,1024,256]{2,1,0:T(8,128)(2,1)S(1)}, bf16[3,1024,256]{2,1,0:T(8,128)(2,1)S(1)}, u32[]{:S(2)}, u32[]{:S(2)}) collective-permute-start(bf16[3,1024,256]{2,1,0:T(8,128)(2,1)S(1)} %stack_weights.1), channel_id=1, source_target_pairs={{0,24},{24,0},{8,16},{16,8},{1,25},{25,1},{9,17},{17,9},{2,26},{26... | collective-permute-start | bytes 4718600 | tf_op jit(solution)/shard_map/ppermute | solution.py:384
  9.4 34.9 %all-gather = bf16[256,1536]{1,0:T(8,128)(2,1)S(1)} all-gather(bf16[16,1536]{1,0:T(8,128)(2,1)S(1)} %pack.1), channel_id=2, replica_groups=mesh['zq'=8,'zb'=2,'xh'=2,'xl'=2,'y'=4,'c'=2] {'zq','zb'}, dimensions={0}, use_global_device_ids=true | all-gather | bytes 835584 | tf_op jit(solution)/shard_map/all_gather | solution.py:387
  44.4 1.9 %collective-permute-start = (bf16[2,192,1024]{2,1,0:T(8,128)(2,1)S(1)}, bf16[2,192,1024]{2,1,0:T(8,128)(2,1)S(1)}, u32[]{:S(2)}, u32[]{:S(2)}) collective-permute-start(bf16[2,192,1024]{2,1,0:T(8,128)(2,1)S(1)} %unpack.1.tokens_ref.refs_0_), channel_id=1, source_target_pairs={{0,8},{8,0},{1,9},{9,1},{2,10},{10,2},{3,11},{11,3},{4,12},{12,4},... | collective-permute-start | bytes 2359304 | tf_op jit(solution)/shard_map/ppermute | solution.py:395
  46.4 2.4 %collective-permute-start.2 = (bf16[2,192,1024]{2,1,0:T(8,128)(2,1)S(1)}, bf16[2,192,1024]{2,1,0:T(8,128)(2,1)S(1)}, u32[]{:S(2)}, u32[]{:S(2)}) collective-permute-start(bf16[2,192,1024]{2,1,0:T(8,128)(2,1)S(1)} %unpack.1.tokens_ref.refs_0_), channel_id=1, source_target_pairs={{0,24},{24,0},{8,16},{16,8},{1,25},{25,1},{9,17},{17,9},{2,26},{26... | collective-permute-start | bytes 2359304 | tf_op jit(solution)/shard_map/ppermute | solution.py:384
  48.8 1.2 forward.2.refs_4_
  50.0 9.3 %collective-permute-done.tokens_ref.refs_1_ = bf16[2,192,1024]{2,1,0:T(8,128)(2,1)S(1)} collective-permute-done((bf16[2,192,1024]{2,1,0:T(8,128)(2,1)S(1)}, bf16[2,192,1024]{2,1,0:T(8,128)(2,1)S(1)}, u32[]{:S(2)}, u32[]{:S(2)}) %collective-permute-start) | collective-permute-done | bytes 786464 | tf_op jit(solution)/shard_map/ppermute | solution.py:395
  59.3 1.2 forward.3
  60.5 11.4 %all_to_all.20.in_ref = s16[2,4,304,256]{3,2,1,0:T(8,128)(2,1)S(1)} all-to-all(s16[2,4,304,256]{3,2,1,0:T(8,128)(2,1)S(1)} %forward.3), channel_id=1, replica_groups=mesh['zq'=8,'zb'=2,'xh'=2,'xl'=2,'y'=4,'c'=2] {'c'}, dimensions={0} | all-to-all | bytes 2490368 | tf_op jit(solution)/shard_map/all_to_all | solution.py:400
  71.8 0.8 core_sum.1
  72.7 0.8 copy-done.11
  73.5 0.9 copy-done.13
  74.4 4.3 %all-to-all-start.1 = ((s16[4,304,256]{2,1,0:T(8,128)(2,1)}), s16[4,304,256]{2,1,0:T(8,128)(2,1)}, u32[]{:S(2)}, u32[]{:S(2)}) async-start(s16[4,304,256]{2,1,0:T(8,128)(2,1)} %copy-done.11), calls=%async_computation.1 | async-start | bytes 1245184 | tf_op jit(solution)/shard_map/all_to_all | solution.py:404
  78.7 2.3 %collective-permute-start.3 = (bf16[2,192,1024]{2,1,0:T(8,128)(2,1)}, bf16[2,192,1024]{2,1,0:T(8,128)(2,1)}, u32[]{:S(2)}, u32[]{:S(2)}) collective-permute-start(bf16[2,192,1024]{2,1,0:T(8,128)(2,1)} %copy-done.9), channel_id=1, source_target_pairs={{0,24},{24,0},{8,16},{16,8},{1,25},{25,1},{9,17},{17,9},{2,26},{26... | collective-permute-start | bytes 2359304 | tf_op jit(solution)/shard_map/ppermute | solution.py:384
  81.0 7.8 %all-to-all-done.1.in_ref = s16[4,304,256]{2,1,0:T(8,128)(2,1)} async-done(((s16[4,304,256]{2,1,0:T(8,128)(2,1)}), s16[4,304,256]{2,1,0:T(8,128)(2,1)}, u32[]{:S(2)}, u32[]{:S(2)}) %all-to-all-start.1) | async-done | bytes 622624 | tf_op jit(solution)/shard_map/all_to_all | solution.py:404
  88.8 1.9 %pointwise.1 = (bf16[48,1024]{1,0:T(8,128)(2,1)S(1)}, bf16[48,256]{1,0:T(8,128)(2,1)S(1)}, bf16[48,256]{1,0:T(8,128)(2,1)}) custom-call(s16[4,304,256]{2,1,0:T(8,128)(2,1)} %all-to-all-done.1.in_ref), custom_call_target="tpu_custom_call" | custom-call | bytes 622592 | tf_op jit(solution)/shard_map/pointwise/pallas_call | solution.py:215
  90.7 14.7 %all-gather.1 = bf16[384,1024]{1,0:T(8,128)(2,1)S(1)} all-gather(bf16[48,1024]{1,0:T(8,128)(2,1)S(1)} %get-tuple-element.24), channel_id=3, replica_groups=mesh['zq'=8,'zb'=2,'xh'=2,'xl'=2,'y'=4,'c'=2] {'y','c'}, dimensions={0}, use_global_device_ids=true | all-gather | bytes 884736 | tf_op jit(solution)/shard_map/all_gather | solution.py:405
  105.5 1.0 input_grad.1
  106.5 0.9 copy-done.8
  107.4 3.6 %all-to-all-start.2 = ((bf16[4,96,1024]{2,1,0:T(8,128)(2,1)}), bf16[4,96,1024]{2,1,0:T(8,128)(2,1)S(1)}, u32[]{:S(2)}, u32[]{:S(2)}) async-start(bf16[4,96,1024]{2,1,0:T(8,128)(2,1)} %copy-done.8), calls=%async_computation.2 | async-start | bytes 1572864 | tf_op jit(solution)/shard_map/all_to_all | solution.py:410
  111.3 2.3 %collective-permute-start.4 = (bf16[48,256]{1,0:T(8,128)(2,1)}, bf16[48,256]{1,0:T(8,128)(2,1)S(1)}, u32[]{:S(2)}, u32[]{:S(2)}) collective-permute-start(bf16[48,256]{1,0:T(8,128)(2,1)} %get-tuple-element.31), channel_id=1, source_target_pairs={{0,24},{24,0},{8,16},{16,8},{1,25},{25,1},{9,17},{17,9},{2,26},{26... | collective-permute-start | bytes 73736 | tf_op jit(solution)/shard_map/ppermute | solution.py:384
  114.3 4.2 %collective-permute-start.5 = (bf16[384,512]{1,0:T(8,128)(2,1)}, bf16[384,512]{1,0:T(8,128)(2,1)}, u32[]{:S(2)}, u32[]{:S(2)}) collective-permute-start(bf16[384,512]{1,0:T(8,128)(2,1)} %slice.14), channel_id=1, source_target_pairs={{0,24},{24,0},{8,16},{16,8},{1,25},{25,1},{9,17},{17,9},{2,26},{26... | collective-permute-start | bytes 1179656 | tf_op jit(solution)/shard_map/ppermute | solution.py:384
  119.1 1.4 pad_maximum_fusion
  120.5 1.5 all-to-all-done.2.in_ref
  122.7 6.4 %all-to-all-start.3 = ((bf16[8,8,1536]{2,1,0:T(8,128)(2,1)}), bf16[8,8,1536]{2,1,0:T(8,128)(2,1)}, u32[]{:S(2)}, u32[]{:S(2)}) async-start(bf16[8,8,1536]{2,1,0:T(8,128)(2,1)} %copy-done.12), calls=%async_computation.3 | async-start | bytes 393216 | tf_op jit(solution)/shard_map/all_to_all | solution.py:424
  129.1 1.1 copy-done.14
  130.3 3.3 %gate_up_grads.1 = (bf16[1024,256]{1,0:T(8,128)(2,1)}, bf16[1024,256]{1,0:T(8,128)(2,1)}) custom-call(bf16[8,48,1024]{2,1,0:T(8,128)(2,1)S(1)} %bitcast.9, bf16[384,512]{1,0:T(8,128)(2,1)} %collective-permute-done.5.pair_ref, bf16[2,192,1024]{2,1,0:T(8,128)(2,1)S(1)} %unpack.1.tokens_ref.refs_0_, bf16[2,192,1024]{2,1,0:T(8,128)(2,1)S(1)} %copy-done.10, ...), custom_call_target="tpu_custom_call" | custom-call | flops 3221225472 | bytes 3145728 | tf_op jit(solution)/shard_map/gate_up_grads/pallas_call | solution.py:243
  133.5 13.9 %all-gather.2 = bf16[768,256]{1,0:T(8,128)(2,1)S(1)} all-gather(bf16[96,256]{1,0:T(8,128)(2,1)S(1)} %copy-done.18), channel_id=4, replica_groups=mesh['zq'=8,'zb'=2,'xh'=2,'xl'=2,'y'=4,'c'=2] {'y','c'}, dimensions={0}, use_global_device_ids=true | all-gather | bytes 442368 | tf_op jit(solution)/shard_map/all_gather | solution.py:425
  147.5 2.5 %down_grad.1 = bf16[256,1024]{1,0:T(8,128)(2,1)} custom-call(bf16[8,96,256]{2,1,0:T(8,128)(2,1)S(1)} %bitcast.11, bf16[2,384,256]{2,1,0:T(8,128)(2,1)S(1)} %maximum_maximum_fusion.keep_ref, bf16[2,192,1024]{2,1,0:T(8,128)(2,1)S(1)} %unpack.1.tokens_ref.refs_0_, bf16[2,192,1024]{2,1,0:T(8,128)(2,1)S(1)} %copy-done.10, bf16[2,192,1024]{2,1,0:T(8,128)(2,1)S(1)} %copy-done.14, ...), custom_call_target="tpu_custom_call" | custom-call | flops 402653184 | bytes 3145728 | tf_op jit(solution)/shard_map/down_grad/pallas_call | solution.py:267
  150.0 1.6 %z_sum.1 = bf16[12,1024]{1,0:T(8,128)(2,1)} custom-call(bf16[8,8,1536]{2,1,0:T(8,128)(2,1)} %all-to-all-done.3.in_ref), custom_call_target="tpu_custom_call" | custom-call | bytes 196608 | tf_op jit(solution)/shard_map/z_sum/pallas_call | solution.py:366
  (56 shorter events, 2.6 us)
Async XLA Ops:
  0.6 1.0 copy-start
  1.7 1.0 copy-start.2
  2.7 1.0 copy-start.6
  3.8 5.6 %copy-start.15 = (bf16[12,1024]{1,0:T(8,128)(2,1)S(1)}, bf16[12,1024]{1,0:T(8,128)(2,1)}, u32[]{:S(2)}) copy-start(bf16[12,1024]{1,0:T(8,128)(2,1)} %refs_0_.3) | copy-start | bytes 73732
  3.8 5.6 %copy-start.16 = (bf16[12,1024]{1,0:T(8,128)(2,1)S(1)}, bf16[12,1024]{1,0:T(8,128)(2,1)}, u32[]{:S(2)}) copy-start(bf16[12,1024]{1,0:T(8,128)(2,1)} %refs_1_.3) | copy-start | bytes 73732
  4.0 44.8 %copy-start.1 = (bf16[1024,256]{1,0:T(8,128)(2,1)S(1)}, bf16[1024,256]{1,0:T(8,128)(2,1)}, u32[]{:S(2)}) copy-start(bf16[1024,256]{1,0:T(8,128)(2,1)} %wg_ref.3) | copy-start | bytes 1572868
  4.0 44.8 %copy-start.3 = (bf16[1024,256]{1,0:T(8,128)(2,1)S(1)}, bf16[1024,256]{1,0:T(8,128)(2,1)}, u32[]{:S(2)}) copy-start(bf16[1024,256]{1,0:T(8,128)(2,1)} %wu_ref.3) | copy-start | bytes 1572868
  4.0 44.8 %copy-start.7 = (bf16[256,1024]{1,0:T(8,128)(2,1)S(1)}, bf16[256,1024]{1,0:T(8,128)(2,1)}, u32[]{:S(2)}) copy-start(bf16[256,1024]{1,0:T(8,128)(2,1)} %refs_2_.3) | copy-start | bytes 1572868
  4.0 44.8 %collective-permute-start.1 = (bf16[3,1024,256]{2,1,0:T(8,128)(2,1)S(1)}, bf16[3,1024,256]{2,1,0:T(8,128)(2,1)S(1)}, u32[]{:S(2)}, u32[]{:S(2)}) collective-permute-start(bf16[3,1024,256]{2,1,0:T(8,128)(2,1)S(1)} %stack_weights.1), channel_id=1, source_target_pairs={{0,24},{24,0},{8,16},{16,8},{1,25},{25,1},{9,17},{17,9},{2,26},{26... | collective-permute-start | bytes 4718600 | tf_op jit(solution)/shard_map/ppermute | solution.py:384
  44.4 14.8 %collective-permute-start = (bf16[2,192,1024]{2,1,0:T(8,128)(2,1)S(1)}, bf16[2,192,1024]{2,1,0:T(8,128)(2,1)S(1)}, u32[]{:S(2)}, u32[]{:S(2)}) collective-permute-start(bf16[2,192,1024]{2,1,0:T(8,128)(2,1)S(1)} %unpack.1.tokens_ref.refs_0_), channel_id=1, source_target_pairs={{0,8},{8,0},{1,9},{9,1},{2,10},{10,2},{3,11},{11,3},{4,12},{12,4},... | collective-permute-start | bytes 2359304 | tf_op jit(solution)/shard_map/ppermute | solution.py:395
  46.4 27.2 %collective-permute-start.2 = (bf16[2,192,1024]{2,1,0:T(8,128)(2,1)S(1)}, bf16[2,192,1024]{2,1,0:T(8,128)(2,1)S(1)}, u32[]{:S(2)}, u32[]{:S(2)}) collective-permute-start(bf16[2,192,1024]{2,1,0:T(8,128)(2,1)S(1)} %unpack.1.tokens_ref.refs_0_), channel_id=1, source_target_pairs={{0,24},{24,0},{8,16},{16,8},{1,25},{25,1},{9,17},{17,9},{2,26},{26... | collective-permute-start | bytes 2359304 | tf_op jit(solution)/shard_map/ppermute | solution.py:384
  59.3 1.2 copy-start.9
  72.7 0.8 copy-start.11
  73.5 0.9 copy-start.13
  74.4 14.4 %all-to-all-start.1 = ((s16[4,304,256]{2,1,0:T(8,128)(2,1)}), s16[4,304,256]{2,1,0:T(8,128)(2,1)}, u32[]{:S(2)}, u32[]{:S(2)}) async-start(s16[4,304,256]{2,1,0:T(8,128)(2,1)} %copy-done.11), calls=%async_computation.1 | async-start | bytes 1245184 | tf_op jit(solution)/shard_map/all_to_all | solution.py:404
  78.7 26.7 %collective-permute-start.3 = (bf16[2,192,1024]{2,1,0:T(8,128)(2,1)}, bf16[2,192,1024]{2,1,0:T(8,128)(2,1)}, u32[]{:S(2)}, u32[]{:S(2)}) collective-permute-start(bf16[2,192,1024]{2,1,0:T(8,128)(2,1)} %copy-done.9), channel_id=1, source_target_pairs={{0,24},{24,0},{8,16},{16,8},{1,25},{25,1},{9,17},{17,9},{2,26},{26... | collective-permute-start | bytes 2359304 | tf_op jit(solution)/shard_map/ppermute | solution.py:384
  90.7 14.7 %copy-start.17 = (bf16[48,256]{1,0:T(8,128)(2,1)}, bf16[48,256]{1,0:T(8,128)(2,1)S(1)}, u32[]{:S(2)}) copy-start(bf16[48,256]{1,0:T(8,128)(2,1)S(1)} %get-tuple-element.30) | copy-start | bytes 73732
  105.5 1.0 copy-start.4
  106.5 0.9 copy-start.8
  106.5 4.6 %copy-start.19 = (s32[12,2]{0,1:T(2,128)S(1)}, s32[12,2]{0,1:T(2,128)}, u32[]{:S(2)}) copy-start(s32[12,2]{0,1:T(2,128)} %param.11) | copy-start | bytes 292
  107.4 6.2 %copy-start.5 = (bf16[384,1024]{1,0:T(8,128)(2,1)S(1)}, bf16[384,1024]{1,0:T(8,128)(2,1)}, u32[]{:S(2)}) copy-start(bf16[384,1024]{1,0:T(8,128)(2,1)} %copy-done.4) | copy-start | bytes 2359300
  107.4 14.5 %all-to-all-start.2 = ((bf16[4,96,1024]{2,1,0:T(8,128)(2,1)}), bf16[4,96,1024]{2,1,0:T(8,128)(2,1)S(1)}, u32[]{:S(2)}, u32[]{:S(2)}) async-start(bf16[4,96,1024]{2,1,0:T(8,128)(2,1)} %copy-done.8), calls=%async_computation.2 | async-start | bytes 1572864 | tf_op jit(solution)/shard_map/all_to_all | solution.py:410
  111.3 7.8 %collective-permute-start.4 = (bf16[48,256]{1,0:T(8,128)(2,1)}, bf16[48,256]{1,0:T(8,128)(2,1)S(1)}, u32[]{:S(2)}, u32[]{:S(2)}) collective-permute-start(bf16[48,256]{1,0:T(8,128)(2,1)} %get-tuple-element.31), channel_id=1, source_target_pairs={{0,24},{24,0},{8,16},{16,8},{1,25},{25,1},{9,17},{17,9},{2,26},{26... | collective-permute-start | bytes 73736 | tf_op jit(solution)/shard_map/ppermute | solution.py:384
  114.3 14.8 %collective-permute-start.5 = (bf16[384,512]{1,0:T(8,128)(2,1)}, bf16[384,512]{1,0:T(8,128)(2,1)}, u32[]{:S(2)}, u32[]{:S(2)}) collective-permute-start(bf16[384,512]{1,0:T(8,128)(2,1)} %slice.14), channel_id=1, source_target_pairs={{0,24},{24,0},{8,16},{16,8},{1,25},{25,1},{9,17},{17,9},{2,26},{26... | collective-permute-start | bytes 1179656 | tf_op jit(solution)/shard_map/ppermute | solution.py:384
  118.8 10.3 %copy-start.10 = (bf16[2,192,1024]{2,1,0:T(8,128)(2,1)S(1)}, bf16[2,192,1024]{2,1,0:T(8,128)(2,1)}, u32[]{:S(2)}) copy-start(bf16[2,192,1024]{2,1,0:T(8,128)(2,1)} %copy-done.9) | copy-start | bytes 2359300
  122.0 0.7 copy-start.12
  122.7 27.3 %all-to-all-start.3 = ((bf16[8,8,1536]{2,1,0:T(8,128)(2,1)}), bf16[8,8,1536]{2,1,0:T(8,128)(2,1)}, u32[]{:S(2)}, u32[]{:S(2)}) async-start(bf16[8,8,1536]{2,1,0:T(8,128)(2,1)} %copy-done.12), calls=%async_computation.3 | async-start | bytes 393216 | tf_op jit(solution)/shard_map/all_to_all | solution.py:424
  129.1 1.1 copy-start.14
  130.3 3.3 %copy-start.18 = (bf16[96,256]{1,0:T(8,128)(2,1)S(1)}, bf16[96,256]{1,0:T(8,128)(2,1)}, u32[]{:S(2)}) copy-start(bf16[96,256]{1,0:T(8,128)(2,1)} %pad_maximum_fusion) | copy-start | bytes 147460

commit v7 on v6

--- a/solution.py
+++ b/solution.py
@@ -12,6 +12,7 @@
 PLAIN = (((1,), (0,)), ((), ()))
 OUTER = (((0,), (0,)), ((), ()))
 SUMS = 6
+SIDES = 3
 SCALES = 16
 
 
@@ -34,6 +35,15 @@
 def row_is_lane(rows, lanes):
     shape = (rows, lanes)
     return lax.broadcasted_iota(jnp.int32, shape, 0) == lax.broadcasted_iota(jnp.int32, shape, 1)
+
+
+def exponent_of(values):
+    most = jnp.max(jnp.abs(values), axis=1, keepdims=True)
+    return jnp.ceil(jnp.log2(jnp.maximum(most, 1e-30)) + 0.01)
+
+
+def integers(values, exponent):
+    return jnp.round(values * jnp.exp2(15.0 - exponent)).astype(jnp.int32).astype(I16)
 
 
 def code(values):
@@ -42,9 +52,8 @@
     place = lax.broadcasted_iota(jnp.int32, (SCALES, lanes), 0)
     codes, tile = [], jnp.zeros((SCALES, lanes), F32)
     for k, v in enumerate(values):
-        most = jnp.max(jnp.abs(v), axis=1, keepdims=True)
-        exponent = jnp.ceil(jnp.log2(jnp.maximum(most, 1e-30)) + 0.01)
-        codes.append(jnp.round(v * jnp.exp2(15.0 - exponent)).astype(jnp.int32).astype(I16))
+        exponent = exponent_of(v)
+        codes.append(integers(v, exponent))
         along = jnp.sum(jnp.where(diagonal, exponent, 0.0), axis=0, keepdims=True)
         tile = jnp.where(place == k, along, tile)
     return codes, tile.astype(jnp.int32).astype(I16)
@@ -109,17 +118,26 @@
     )(*arrays)
 
 
-def stack_kernel(wg_ref, wu_ref, wd_ref, out_ref, sems):
+def stack_kernel(wg_ref, wu_ref, wd_ref, out_ref, held, sems):
     hidden, width = wd_ref.shape
-    copies = [(wg_ref, out_ref.at[0]), (wu_ref, out_ref.at[1])]
+    copies = []
     for first in range(0, width, hidden):
         part = pl.ds(first, hidden)
-        copies.append((wd_ref.at[:, part], out_ref.at[2, part]))
-    copies = [pltpu.make_async_copy(a, b, sems.at[i]) for i, (a, b) in enumerate(copies)]
-    for c in copies:
-        c.start()
-    for c in copies:
-        c.wait()
+        for k, source in enumerate((wg_ref.at[part], wu_ref.at[part], wd_ref.at[:, part])):
+            place, sem = held.at[k, part], sems.at[len(copies)]
+            copies.append(
+                (
+                    pltpu.make_async_copy(source, place, sem),
+                    pltpu.make_async_copy(place, out_ref.at[k, part], sem),
+                )
+            )
+    for into, _ in copies:
+        into.start()
+    for into, out in copies:
+        into.wait()
+        out.start()
+    for _, out in copies:
+        out.wait()
 
 
 def stack_weights(w_gate, w_up, w_down):
@@ -130,8 +148,11 @@
         out_shape=jax.ShapeDtypeStruct((3, width, hidden), BF16),
         in_specs=[spec] * 3,
         out_specs=spec,
-        scratch_shapes=[pltpu.SemaphoreType.DMA((2 + width // hidden,))],
-        compiler_params=params(1),
+        scratch_shapes=[
+            pltpu.VMEM((3, width, hidden), BF16),
+            pltpu.SemaphoreType.DMA((3 * (width // hidden),)),
+        ],
+        compiler_params=params(56),
         cost_estimate=cost(0, 12 * width * hidden),
         name="stack_weights",
     )(w_gate, w_up, w_down)
@@ -194,27 +215,33 @@
     )(arrived)
 
 
-def pointwise_kernel(rows, in_ref, both_ref, *kept_refs):
+def pointwise_kernel(rows, in_ref, out_ref):
     parts = [decode(in_ref[i], rows) for i in range(in_ref.shape[0])]
     sums = [sum(p[1:], p[0]) for p in zip(*parts)]
     hidden = sums[0].shape[1]
-    for which, kept_ref in enumerate(kept_refs):
+    grads, kept = [], []
+    for which in range(2):
         gate_pre, up_pre, grad_hidden = sums[3 * which : 3 * which + 3]
         sigmoid_gate = jax.nn.sigmoid(gate_pre)
         silu_gate = gate_pre * sigmoid_gate
         slope = sigmoid_gate * (1.0 + gate_pre * (1.0 - sigmoid_gate))
-        first = 2 * which * hidden
-        both_ref[:, first : first + hidden] = (grad_hidden * up_pre * slope).astype(BF16)
-        both_ref[:, first + hidden : first + 2 * hidden] = (grad_hidden * silu_gate).astype(BF16)
-        kept_ref[...] = (silu_gate * up_pre).astype(BF16)
+        grads += [grad_hidden * up_pre * slope, grad_hidden * silu_gate]
+        kept.append(silu_gate * up_pre)
+    lane = lax.broadcasted_iota(jnp.int32, (rows, 128), 1)
+    exponents = jnp.zeros((rows, 128), F32)
+    for k, v in enumerate(grads + kept):
+        v = v.astype(BF16).astype(F32)
+        exponent = exponent_of(v)
+        exponents = jnp.where(lane == k, exponent, exponents)
+        out_ref[:, k * hidden : (k + 1) * hidden] = integers(v, exponent)
+    out_ref[:, SUMS * hidden :] = exponents.astype(jnp.int32).astype(I16)
 
 
 def pointwise(arrived, rows):
     hidden = arrived.shape[2]
-    one = jax.ShapeDtypeStruct((rows, hidden), BF16)
     return pl.pallas_call(
         functools.partial(pointwise_kernel, rows),
-        out_shape=(jax.ShapeDtypeStruct((rows, 4 * hidden), BF16), one, one),
+        out_shape=jax.ShapeDtypeStruct((rows, SUMS * hidden + 128), I16),
         compiler_params=params(4),
         cost_estimate=cost(0, 2 * arrived.size),
         name="pointwise",
@@ -225,12 +252,10 @@
     return jnp.concatenate([r[which, :, columns] for r in refs])
 
 
-def gate_up_kernel(both_ref, pair_ref, *refs):
+def gate_up_kernel(own_ref, pair_ref, *refs):
     *tokens, gate_ref, up_ref = refs
-    parts, rows, depth = both_ref.shape
     hidden = gate_ref.shape[1]
-    grads = both_ref[:, :, : depth // 2].reshape(parts * rows, depth // 2)
-    grads = jnp.concatenate([grads, pair_ref[...]])
+    grads = jnp.concatenate([own_ref[:, : 2 * hidden], pair_ref[:, : 2 * hidden]])
     for first in range(0, gate_ref.shape[0], 256):
         columns = slice(first, first + 256)
         total = dot(pieces(tokens, 0, columns), grads, OUTER).astype(BF16)
@@ -238,39 +263,36 @@
         up_ref[columns] = total[:, hidden:]
 
 
-def gate_up_grads(both, pair, tokens):
-    width, hidden = tokens[0].shape[2], pair.shape[1] // 2
+def gate_up_grads(own, pair, tokens):
+    width, hidden = tokens[0].shape[2], own.shape[1] // SIDES
     return pl.pallas_call(
         gate_up_kernel,
         out_shape=(jax.ShapeDtypeStruct((width, hidden), BF16),) * 2,
         compiler_params=params(10),
-        cost_estimate=cost(16 * pair.size * width, 8 * tokens[0].size),
+        cost_estimate=cost(8 * own.shape[0] * hidden * width, 8 * tokens[0].size),
         name="gate_up_grads",
-    )(both, pair, *tokens)
-
-
-def down_kernel(kept_ref, keep_ref, *refs):
+    )(own, pair, *tokens)
+
+
+def down_kernel(own_ref, pair_ref, keep_ref, *refs):
     *tokens, out_ref = refs
-    rows = kept_ref.shape[1] // 2
-    kept = [
-        kept_ref[:, i * rows : (i + 1) * rows].reshape(keep_ref.shape[1:]) * keep_ref[i]
-        for i in range(2)
-    ]
+    hidden = out_ref.shape[0]
+    kept = [ref[:, 2 * hidden :] * keep_ref[i] for i, ref in enumerate((own_ref, pair_ref))]
     kept = jnp.concatenate(kept)
     for first in range(0, out_ref.shape[1], 256):
         columns = slice(first, first + 256)
         out_ref[:, columns] = dot(kept, pieces(tokens, 1, columns), OUTER).astype(BF16)
 
 
-def down_grad(kept, keep, tokens):
-    width, hidden = tokens[0].shape[2], kept.shape[2]
+def down_grad(own, pair, keep, tokens):
+    width, hidden = tokens[0].shape[2], own.shape[1] // SIDES
     return pl.pallas_call(
         down_kernel,
         out_shape=jax.ShapeDtypeStruct((hidden, width), BF16),
         compiler_params=params(9),
-        cost_estimate=cost(2 * kept.size * width, 8 * tokens[0].size),
+        cost_estimate=cost(4 * own.shape[0] * hidden * width, 8 * tokens[0].size),
         name="down_grad",
-    )(kept, keep, *tokens)
+    )(own, pair, keep, *tokens)
 
 
 def keep_of_tokens(keep_mask, x, tokens, nx, own_tokens, total):
@@ -292,17 +314,46 @@
     return jnp.concatenate([jnp.broadcast_to(k, (tokens, 128)) for k in keep], axis=1).astype(BF16)
 
 
+def gathered_values(coded_ref, hidden, wanted):
+    coded = coded_ref[...].reshape(coded_ref.shape[0] * coded_ref.shape[1], coded_ref.shape[2])
+    scales = jnp.exp2(coded[:, SUMS * hidden :].astype(jnp.int32).astype(F32) - 15.0)
+    values = []
+    for k in wanted:
+        v = coded[:, k * hidden : (k + 1) * hidden].astype(jnp.int32).astype(F32)
+        values.append((v * scales[:, k : k + 1]).astype(BF16))
+    return values
+
+
+def sides_kernel(coded_ref, *side_refs):
+    for which, side_ref in enumerate(side_refs):
+        hidden = side_ref.shape[1] // SIDES
+        values = gathered_values(coded_ref, hidden, (2 * which, 2 * which + 1, 4 + which))
+        for i, v in enumerate(values):
+            side_ref[:, i * hidden : (i + 1) * hidden] = v
+
+
+def sides(coded, hidden):
+    side = jax.ShapeDtypeStruct((coded.shape[0] * coded.shape[1], SIDES * hidden), BF16)
+    return pl.pallas_call(
+        sides_kernel,
+        out_shape=(side, side),
+        compiler_params=params(8),
+        cost_estimate=cost(0, 4 * coded.size),
+        name="sides",
+    )(coded)
+
+
 def input_grad_kernel(g_ref, wg_ref, wu_ref, pair_ref, out_ref):
     chunks, rows, width = out_ref.shape
     hidden = wg_ref.shape[1]
     xl = lax.axis_index("xl")
-    g = g_ref[...].reshape(chunks * rows, 4 * hidden)
+    g = gathered_values(g_ref, hidden, range(4))
     for first in range(0, width, 256):
         columns = slice(first, first + 256)
         places = (wg_ref[columns], wu_ref[columns], pair_ref[0, columns], pair_ref[1, columns])
-        product = dot(g[:, :hidden], places[0], INNER)
-        for i, w in enumerate(places[1:], 1):
-            product = product + dot(g[:, i * hidden : (i + 1) * hidden], w, INNER)
+        product = dot(g[0], places[0], INNER)
+        for v, w in zip(g[1:], places[1:]):
+            product = product + dot(v, w, INNER)
         product = product.astype(BF16)
         for k in range(2):
             owner = lax.rem(xl + k, 2)
@@ -311,17 +362,16 @@
                 out_ref[2 * odd + owner, :, columns] = product[place : place + rows]
 
 
-def input_grad(both, weights, chunks):
-    parts, rows, depth = both.shape
-    width = weights[0].shape[0]
-    tokens = parts * rows
+def input_grad(coded, weights, chunks):
+    width, hidden = weights[0].shape
+    tokens = coded.shape[0] * coded.shape[1]
     return pl.pallas_call(
         input_grad_kernel,
         out_shape=jax.ShapeDtypeStruct((chunks, tokens // chunks, width), BF16),
-        compiler_params=params(10),
-        cost_estimate=cost(2 * tokens * width * depth, 2 * depth * width),
+        compiler_params=params(12),
+        cost_estimate=cost(8 * tokens * width * hidden, 2 * coded.size),
         name="input_grad",
-    )(both, *weights)
+    )(coded, *weights)
 
 
 def x_sum_kernel(in_ref, out_ref):
@@ -401,15 +451,14 @@
     own_2 = to_partner(own)
     summed, own_2, other_late = lax.optimization_barrier((summed, own_2, other))
     other_2 = to_partner(other_late)
-    both, kept, kept_2 = pointwise(lax.all_to_all(summed, "y", 0, 0), rows)
-    both = lax.all_gather(both, ("y", "c"))
-    both, other_2 = lax.optimization_barrier((both, other_2))
-
-    result = input_grad(both, (w_gate, w_up, w_2), nx)
-    result, both, kept, kept_2 = lax.optimization_barrier((result, both, kept, kept_2))
+    coded = lax.all_gather(pointwise(lax.all_to_all(summed, "y", 0, 0), rows), ("y", "c"))
+    coded, other_2 = lax.optimization_barrier((coded, other_2))
+
+    result = input_grad(coded, (w_gate, w_up, w_2), nx)
+    result, coded = lax.optimization_barrier((result, coded))
     arrived = lax.all_to_all(result, ("zb", "xl"), 0, 0)
-    both_2 = to_partner(both.reshape(tokens, 4 * hidden)[:, 2 * hidden :])
-    kept = jnp.concatenate([kept, to_partner(kept_2)])
+    mine, pair = sides(coded, hidden)
+    pair = to_partner(pair)
     x = lax.axis_index(("xh", "xl"))
     keep = jnp.stack(
         [
@@ -417,15 +466,13 @@
             for at in (x, nx - 1 - x)
         ]
     )
-    arrived, kept, keep = lax.optimization_barrier((arrived, kept, keep))
+    arrived, keep = lax.optimization_barrier((arrived, keep))
 
     grad_sum = x_sum(arrived, nz // 2)
-    grad_sum, kept = lax.optimization_barrier((grad_sum, kept))
     grad_input = z_sum(lax.all_to_all(grad_sum, "zq", 0, 0), own_tokens, width)
-    kept = lax.all_gather(kept, ("y", "c"))
     places = (own, other, own_2, other_2)
-    grad_gate, grad_up = gate_up_grads(both, both_2, places)
-    grad_down = down_grad(kept, keep, places)
+    grad_gate, grad_up = gate_up_grads(mine, pair, places)
+    grad_down = down_grad(mine, pair, keep, places)
     return grad_input, grad_gate, grad_up, grad_down
 
 

time: 152 us -> 149 us (0.980)
  the two profiles are of different devices: /device:TPU:1 before, /device:TPU:2 now
where the time goes in v7:
time: 149 us; the launch traced here: 148 us
  blocking collectives  59.3 us (40%)
  waiting for transfers between devices  34.1 us (23%)
  starting transfers between devices  29.3 us (20%)
  Pallas kernels  16.1 us (11%)
  local copies, waits for them, and re-layouts  8.06 us (5%)
    all_gather x1, blocking collectives, shards(): along_z = lax.all_gather(pack(inputs, cotangent), ('zq', 'zb'))  40.3 us
    all_gather x1, blocking collectives, shards(): lax.all_gather(pointwise(lax.all_to_all(summed, 'y', 0, 0), rows), ('y',...  14.3 us
    ppermute x4, starting transfers between devices, to_partner(): return lax.ppermute(a, ('xh', 'xl'), [(0, 3), (3, 0), (1, 2), (2, 1)])  9.4 us
    ppermute x1, waiting for transfers between devices, shards(): other = lax.ppermute(own, 'xl', ring(2, 1))  9.14 us
    all_to_all x1, waiting for transfers between devices, shards(): lax.all_to_all(summed, 'y', 0, 0)  9.02 us
    all_to_all x1, waiting for transfers between devices, shards(): grad_input = z_sum(lax.all_to_all(grad_sum, 'zq', 0, 0), own_tokens, width)  8.21 us
    unnamed x36, local copies, waits for them, and re-layouts  7.6 us
    all_to_all x1, starting transfers between devices, shards(): grad_input = z_sum(lax.all_to_all(grad_sum, 'zq', 0, 0), own_tokens, width)  6.5 us
  transfers between devices with their start and end apart: 8, of which 5 were waited for; matrix products, arithmetic and copies ran while one was open for 0% of the time, Pallas kernels for 8%

profile of v7, /device:TPU:2, one launch (start us, length us, event | category | flops | bytes accessed | tf_op | source)
XLA Modules:
  0.0 147.9 jit_solution(6630371129964279358)
XLA Ops:
  0.7 2.3 %stack_weights.1 = bf16[3,1024,256]{2,1,0:T(8,128)(2,1)} custom-call(bf16[1024,256]{1,0:T(8,128)(2,1)} %wg_ref.3, bf16[1024,256]{1,0:T(8,128)(2,1)} %wu_ref.3, bf16[256,1024]{1,0:T(8,128)(2,1)} %refs_2_.3), custom_call_target="tpu_custom_call" | custom-call | bytes 3145728 | tf_op jit(solution)/shard_map/stack_weights/pallas_call | solution.py:146
  3.0 3.5 %collective-permute-start.1 = (bf16[3,1024,256]{2,1,0:T(8,128)(2,1)}, bf16[3,1024,256]{2,1,0:T(8,128)(2,1)S(1)}, u32[]{:S(2)}, u32[]{:S(2)}) collective-permute-start(bf16[3,1024,256]{2,1,0:T(8,128)(2,1)} %stack_weights.1), channel_id=1, source_target_pairs={{0,24},{24,0},{8,16},{16,8},{1,25},{25,1},{9,17},{17,9},{2,26},{26... | collective-permute-start | bytes 4718600 | tf_op jit(solution)/shard_map/ppermute | solution.py:434
  6.5 40.3 %all-gather = bf16[256,1536]{1,0:T(8,128)(2,1)S(1)} all-gather(bf16[16,1536]{1,0:T(8,128)(2,1)S(1)} %pack.1), channel_id=2, replica_groups=mesh['zq'=8,'zb'=2,'xh'=2,'xl'=2,'y'=4,'c'=2] {'zq','zb'}, dimensions={0}, use_global_device_ids=true | all-gather | bytes 835584 | tf_op jit(solution)/shard_map/all_gather | solution.py:437
  46.9 3.5 %collective-permute-start = (bf16[2,192,1024]{2,1,0:T(8,128)(2,1)S(1)}, bf16[2,192,1024]{2,1,0:T(8,128)(2,1)S(1)}, u32[]{:S(2)}, u32[]{:S(2)}) collective-permute-start(bf16[2,192,1024]{2,1,0:T(8,128)(2,1)S(1)} %unpack.1.tokens_ref.refs_0_), channel_id=1, source_target_pairs={{0,8},{8,0},{1,9},{9,1},{2,10},{10,2},{3,11},{11,3},{4,12},{12,4},... | collective-permute-start | bytes 2359304 | tf_op jit(solution)/shard_map/ppermute | solution.py:445
  50.4 1.9 %collective-permute-start.2 = (bf16[2,192,1024]{2,1,0:T(8,128)(2,1)S(1)}, bf16[2,192,1024]{2,1,0:T(8,128)(2,1)S(1)}, u32[]{:S(2)}, u32[]{:S(2)}) collective-permute-start(bf16[2,192,1024]{2,1,0:T(8,128)(2,1)S(1)} %unpack.1.tokens_ref.refs_0_), channel_id=1, source_target_pairs={{0,24},{24,0},{8,16},{16,8},{1,25},{25,1},{9,17},{17,9},{2,26},{26... | collective-permute-start | bytes 2359304 | tf_op jit(solution)/shard_map/ppermute | solution.py:434
  52.4 1.2 forward.2.refs_4_
  53.5 9.1 %collective-permute-done.tokens_ref.refs_1_ = bf16[2,192,1024]{2,1,0:T(8,128)(2,1)S(1)} collective-permute-done((bf16[2,192,1024]{2,1,0:T(8,128)(2,1)S(1)}, bf16[2,192,1024]{2,1,0:T(8,128)(2,1)S(1)}, u32[]{:S(2)}, u32[]{:S(2)}) %collective-permute-start) | collective-permute-done | bytes 786464 | tf_op jit(solution)/shard_map/ppermute | solution.py:445
  62.7 1.2 forward.3
  63.9 4.7 %all_to_all.20.in_ref = s16[2,4,304,256]{3,2,1,0:T(8,128)(2,1)S(1)} all-to-all(s16[2,4,304,256]{3,2,1,0:T(8,128)(2,1)S(1)} %forward.3), channel_id=1, replica_groups=mesh['zq'=8,'zb'=2,'xh'=2,'xl'=2,'y'=4,'c'=2] {'c'}, dimensions={0} | all-to-all | bytes 2490368 | tf_op jit(solution)/shard_map/all_to_all | solution.py:450
  68.6 0.8 core_sum.1
  69.5 0.8 copy-done.10
  70.3 0.9 copy-done.8
  71.2 4.6 %all-to-all-start.1 = ((s16[4,304,256]{2,1,0:T(8,128)(2,1)}), s16[4,304,256]{2,1,0:T(8,128)(2,1)}, u32[]{:S(2)}, u32[]{:S(2)}) async-start(s16[4,304,256]{2,1,0:T(8,128)(2,1)} %copy-done.10), calls=%async_computation.1 | async-start | bytes 1245184 | tf_op jit(solution)/shard_map/all_to_all | solution.py:454
  75.8 1.9 %collective-permute-start.3 = (bf16[2,192,1024]{2,1,0:T(8,128)(2,1)}, bf16[2,192,1024]{2,1,0:T(8,128)(2,1)}, u32[]{:S(2)}, u32[]{:S(2)}) collective-permute-start(bf16[2,192,1024]{2,1,0:T(8,128)(2,1)} %copy-done.4), channel_id=1, source_target_pairs={{0,24},{24,0},{8,16},{16,8},{1,25},{25,1},{9,17},{17,9},{2,26},{26... | collective-permute-start | bytes 2359304 | tf_op jit(solution)/shard_map/ppermute | solution.py:434
  77.7 9.0 %all-to-all-done.1.in_ref = s16[4,304,256]{2,1,0:T(8,128)(2,1)} async-done(((s16[4,304,256]{2,1,0:T(8,128)(2,1)}), s16[4,304,256]{2,1,0:T(8,128)(2,1)}, u32[]{:S(2)}, u32[]{:S(2)}) %all-to-all-start.1) | async-done | bytes 622624 | tf_op jit(solution)/shard_map/all_to_all | solution.py:454
  86.7 1.5 %pointwise.1 = s16[48,1664]{1,0:T(8,128)(2,1)S(1)} custom-call(s16[4,304,256]{2,1,0:T(8,128)(2,1)} %all-to-all-done.1.in_ref), custom_call_target="tpu_custom_call" | custom-call | bytes 622592 | tf_op jit(solution)/shard_map/pointwise/pallas_call | solution.py:242
  88.2 14.3 %all-gather.3 = s16[384,1664]{1,0:T(8,128)(2,1)S(1)} all-gather(s16[48,1664]{1,0:T(8,128)(2,1)S(1)} %pointwise.1), channel_id=3, replica_groups=mesh['zq'=8,'zb'=2,'xh'=2,'xl'=2,'y'=4,'c'=2] {'y','c'}, dimensions={0}, use_global_device_ids=true | all-gather | bytes 1437696 | tf_op jit(solution)/shard_map/all_gather | solution.py:454
  102.5 1.0 input_grad.1
  103.5 1.1 copy-done
  104.6 0.9 copy-done.7
  105.5 5.2 %all-to-all-start.2 = ((bf16[4,96,1024]{2,1,0:T(8,128)(2,1)}), bf16[4,96,1024]{2,1,0:T(8,128)(2,1)S(1)}, u32[]{:S(2)}, u32[]{:S(2)}) async-start(bf16[4,96,1024]{2,1,0:T(8,128)(2,1)} %copy-done.7), calls=%async_computation.2 | async-start | bytes 1572864 | tf_op jit(solution)/shard_map/all_to_all | solution.py:459
  111.0 1.3 copy-done.1
  112.3 1.2 sides.1
  113.5 0.8 copy-done.11
  114.3 2.0 %collective-permute-start.4 = (bf16[384,768]{1,0:T(8,128)(2,1)}, bf16[384,768]{1,0:T(8,128)(2,1)}, u32[]{:S(2)}, u32[]{:S(2)}) collective-permute-start(bf16[384,768]{1,0:T(8,128)(2,1)} %get-tuple-element.24), channel_id=1, source_target_pairs={{0,24},{24,0},{8,16},{16,8},{1,25},{25,1},{9,17},{17,9},{2,26},{26... | collective-permute-start | bytes 1769480 | tf_op jit(solution)/shard_map/ppermute | solution.py:434
  116.9 4.9 %all-to-all-done.2.in_ref = bf16[4,96,1024]{2,1,0:T(8,128)(2,1)S(1)} async-done(((bf16[4,96,1024]{2,1,0:T(8,128)(2,1)}), bf16[4,96,1024]{2,1,0:T(8,128)(2,1)S(1)}, u32[]{:S(2)}, u32[]{:S(2)}) %all-to-all-start.2) | async-done | bytes 786464 | tf_op jit(solution)/shard_map/all_to_all | solution.py:459
  122.6 6.5 %all-to-all-start.3 = ((bf16[8,8,1536]{2,1,0:T(8,128)(2,1)}), bf16[8,8,1536]{2,1,0:T(8,128)(2,1)S(1)}, u32[]{:S(2)}, u32[]{:S(2)}) async-start(bf16[8,8,1536]{2,1,0:T(8,128)(2,1)} %copy-done.14), calls=%async_computation.3 | async-start | bytes 393216 | tf_op jit(solution)/shard_map/all_to_all | solution.py:472
  129.1 2.8 %collective-permute-done.4.pair_ref = bf16[384,768]{1,0:T(8,128)(2,1)} collective-permute-done((bf16[384,768]{1,0:T(8,128)(2,1)}, bf16[384,768]{1,0:T(8,128)(2,1)}, u32[]{:S(2)}, u32[]{:S(2)}) %collective-permute-start.4) | collective-permute-done | bytes 589856 | tf_op jit(solution)/shard_map/ppermute | solution.py:434
  131.9 1.1 copy-done.12
  133.0 3.4 %gate_up_grads.1 = (bf16[1024,256]{1,0:T(8,128)(2,1)}, bf16[1024,256]{1,0:T(8,128)(2,1)}) custom-call(bf16[384,768]{1,0:T(8,128)(2,1)S(1)} %copy-done.12, bf16[384,768]{1,0:T(8,128)(2,1)} %collective-permute-done.4.pair_ref, bf16[2,192,1024]{2,1,0:T(8,128)(2,1)S(1)} %unpack.1.tokens_ref.refs_0_, bf16[2,192,1024]{2,1,0:T(8,128)(2,1)S(1)} %copy-done.5, ...), custom_call_target="tpu_custom_call" | custom-call | flops 805306368 | bytes 3145728 | tf_op jit(solution)/shard_map/gate_up_grads/pallas_call | solution.py:268
  136.4 2.7 %down_grad.1 = bf16[256,1024]{1,0:T(8,128)(2,1)} custom-call(bf16[384,768]{1,0:T(8,128)(2,1)S(1)} %copy-done.13, bf16[384,768]{1,0:T(8,128)(2,1)} %collective-permute-done.4.pair_ref, bf16[2,384,256]{2,1,0:T(8,128)(2,1)S(1)} %maximum_maximum_fusion.keep_ref, bf16[2,192,1024]{2,1,0:T(8,128)(2,1)S(1)} %unpack.1.tokens_ref.refs_0_, ...), custom_call_target="tpu_custom_call" | custom-call | flops 402653184 | bytes 3145728 | tf_op jit(solution)/shard_map/down_grad/pallas_call | solution.py:289
  139.1 8.2 %all-to-all-done.3.in_ref = bf16[8,8,1536]{2,1,0:T(8,128)(2,1)S(1)} async-done(((bf16[8,8,1536]{2,1,0:T(8,128)(2,1)}), bf16[8,8,1536]{2,1,0:T(8,128)(2,1)S(1)}, u32[]{:S(2)}, u32[]{:S(2)}) %all-to-all-start.3) | async-done | bytes 196640 | tf_op jit(solution)/shard_map/all_to_all | solution.py:472
  (48 shorter events, 2.2 us)
Async XLA Ops:
  0.6 5.9 %copy-start.15 = (bf16[12,1024]{1,0:T(8,128)(2,1)S(1)}, bf16[12,1024]{1,0:T(8,128)(2,1)}, u32[]{:S(2)}) copy-start(bf16[12,1024]{1,0:T(8,128)(2,1)} %refs_0_.3) | copy-start | bytes 73732
  0.6 5.9 %copy-start.16 = (bf16[12,1024]{1,0:T(8,128)(2,1)S(1)}, bf16[12,1024]{1,0:T(8,128)(2,1)}, u32[]{:S(2)}) copy-start(bf16[12,1024]{1,0:T(8,128)(2,1)} %refs_1_.3) | copy-start | bytes 73732
  2.9 49.4 %copy-start.2 = (bf16[1024,256]{1,0:T(8,128)(2,1)S(1)}, bf16[1024,256]{1,0:T(8,128)(2,1)}, u32[]{:S(2)}) copy-start(bf16[1024,256]{1,0:T(8,128)(2,1)} %wg_ref.3) | copy-start | bytes 1572868
  2.9 49.4 %copy-start.3 = (bf16[1024,256]{1,0:T(8,128)(2,1)S(1)}, bf16[1024,256]{1,0:T(8,128)(2,1)}, u32[]{:S(2)}) copy-start(bf16[1024,256]{1,0:T(8,128)(2,1)} %wu_ref.3) | copy-start | bytes 1572868
  2.9 49.4 %copy-start.6 = (bf16[256,1024]{1,0:T(8,128)(2,1)S(1)}, bf16[256,1024]{1,0:T(8,128)(2,1)}, u32[]{:S(2)}) copy-start(bf16[256,1024]{1,0:T(8,128)(2,1)} %refs_2_.3) | copy-start | bytes 1572868
  3.0 49.4 %collective-permute-start.1 = (bf16[3,1024,256]{2,1,0:T(8,128)(2,1)}, bf16[3,1024,256]{2,1,0:T(8,128)(2,1)S(1)}, u32[]{:S(2)}, u32[]{:S(2)}) collective-permute-start(bf16[3,1024,256]{2,1,0:T(8,128)(2,1)} %stack_weights.1), channel_id=1, source_target_pairs={{0,24},{24,0},{8,16},{16,8},{1,25},{25,1},{9,17},{17,9},{2,26},{26... | collective-permute-start | bytes 4718600 | tf_op jit(solution)/shard_map/ppermute | solution.py:434
  46.9 15.8 %collective-permute-start = (bf16[2,192,1024]{2,1,0:T(8,128)(2,1)S(1)}, bf16[2,192,1024]{2,1,0:T(8,128)(2,1)S(1)}, u32[]{:S(2)}, u32[]{:S(2)}) collective-permute-start(bf16[2,192,1024]{2,1,0:T(8,128)(2,1)S(1)} %unpack.1.tokens_ref.refs_0_), channel_id=1, source_target_pairs={{0,8},{8,0},{1,9},{9,1},{2,10},{10,2},{3,11},{11,3},{4,12},{12,4},... | collective-permute-start | bytes 2359304 | tf_op jit(solution)/shard_map/ppermute | solution.py:445
  50.4 19.9 %collective-permute-start.2 = (bf16[2,192,1024]{2,1,0:T(8,128)(2,1)S(1)}, bf16[2,192,1024]{2,1,0:T(8,128)(2,1)S(1)}, u32[]{:S(2)}, u32[]{:S(2)}) collective-permute-start(bf16[2,192,1024]{2,1,0:T(8,128)(2,1)S(1)} %unpack.1.tokens_ref.refs_0_), channel_id=1, source_target_pairs={{0,24},{24,0},{8,16},{16,8},{1,25},{25,1},{9,17},{17,9},{2,26},{26... | collective-permute-start | bytes 2359304 | tf_op jit(solution)/shard_map/ppermute | solution.py:434
  62.7 1.2 copy-start.4
  69.4 0.8 copy-start.10
  70.3 0.9 copy-start.8
  71.2 15.5 %all-to-all-start.1 = ((s16[4,304,256]{2,1,0:T(8,128)(2,1)}), s16[4,304,256]{2,1,0:T(8,128)(2,1)}, u32[]{:S(2)}, u32[]{:S(2)}) async-start(s16[4,304,256]{2,1,0:T(8,128)(2,1)} %copy-done.10), calls=%async_computation.1 | async-start | bytes 1245184 | tf_op jit(solution)/shard_map/all_to_all | solution.py:454
  75.8 26.7 %collective-permute-start.3 = (bf16[2,192,1024]{2,1,0:T(8,128)(2,1)}, bf16[2,192,1024]{2,1,0:T(8,128)(2,1)}, u32[]{:S(2)}, u32[]{:S(2)}) collective-permute-start(bf16[2,192,1024]{2,1,0:T(8,128)(2,1)} %copy-done.4), channel_id=1, source_target_pairs={{0,24},{24,0},{8,16},{16,8},{1,25},{25,1},{9,17},{17,9},{2,26},{26... | collective-permute-start | bytes 2359304 | tf_op jit(solution)/shard_map/ppermute | solution.py:434
  103.5 1.1 copy-start
  104.6 0.9 copy-start.7
  105.5 5.3 %copy-start.17 = (s32[12,2]{0,1:T(2,128)S(1)}, s32[12,2]{0,1:T(2,128)}, u32[]{:S(2)}) copy-start(s32[12,2]{0,1:T(2,128)} %param.11) | copy-start | bytes 292
  105.5 16.3 %all-to-all-start.2 = ((bf16[4,96,1024]{2,1,0:T(8,128)(2,1)}), bf16[4,96,1024]{2,1,0:T(8,128)(2,1)S(1)}, u32[]{:S(2)}, u32[]{:S(2)}) async-start(bf16[4,96,1024]{2,1,0:T(8,128)(2,1)} %copy-done.7), calls=%async_computation.2 | async-start | bytes 1572864 | tf_op jit(solution)/shard_map/all_to_all | solution.py:459
  110.9 1.3 copy-start.1
  113.5 0.8 copy-start.11
  114.3 17.6 %copy-start.5 = (bf16[2,192,1024]{2,1,0:T(8,128)(2,1)S(1)}, bf16[2,192,1024]{2,1,0:T(8,128)(2,1)}, u32[]{:S(2)}) copy-start(bf16[2,192,1024]{2,1,0:T(8,128)(2,1)} %copy-done.4) | copy-start | bytes 2359300
  114.3 17.6 %copy-start.9 = (bf16[2,192,1024]{2,1,0:T(8,128)(2,1)S(1)}, bf16[2,192,1024]{2,1,0:T(8,128)(2,1)}, u32[]{:S(2)}) copy-start(bf16[2,192,1024]{2,1,0:T(8,128)(2,1)} %copy-done.8) | copy-start | bytes 2359300
  114.3 17.6 %collective-permute-start.4 = (bf16[384,768]{1,0:T(8,128)(2,1)}, bf16[384,768]{1,0:T(8,128)(2,1)}, u32[]{:S(2)}, u32[]{:S(2)}) collective-permute-start(bf16[384,768]{1,0:T(8,128)(2,1)} %get-tuple-element.24), channel_id=1, source_target_pairs={{0,24},{24,0},{8,16},{16,8},{1,25},{25,1},{9,17},{17,9},{2,26},{26... | collective-permute-start | bytes 1769480 | tf_op jit(solution)/shard_map/ppermute | solution.py:434
  121.9 0.7 copy-start.14
  122.6 24.7 %all-to-all-start.3 = ((bf16[8,8,1536]{2,1,0:T(8,128)(2,1)}), bf16[8,8,1536]{2,1,0:T(8,128)(2,1)S(1)}, u32[]{:S(2)}, u32[]{:S(2)}) async-start(bf16[8,8,1536]{2,1,0:T(8,128)(2,1)} %copy-done.14), calls=%async_computation.3 | async-start | bytes 393216 | tf_op jit(solution)/shard_map/all_to_all | solution.py:472
  131.9 1.1 copy-start.12
  133.0 3.4 %copy-start.13 = (bf16[384,768]{1,0:T(8,128)(2,1)S(1)}, bf16[384,768]{1,0:T(8,128)(2,1)}, u32[]{:S(2)}) copy-start(bf16[384,768]{1,0:T(8,128)(2,1)} %copy-done.11) | copy-start | bytes 1769476

commit v8 on v7

--- a/solution.py
+++ b/solution.py
@@ -449,14 +449,12 @@
     parts = forward(1, other, weights, parts, rows, nc, ny)
     summed = core_sum(lax.all_to_all(parts, "c", 0, 0), rows)
     own_2 = to_partner(own)
-    summed, own_2, other_late = lax.optimization_barrier((summed, own_2, other))
-    other_2 = to_partner(other_late)
+    summed, own_2 = lax.optimization_barrier((summed, own_2))
     coded = lax.all_gather(pointwise(lax.all_to_all(summed, "y", 0, 0), rows), ("y", "c"))
-    coded, other_2 = lax.optimization_barrier((coded, other_2))
-
     result = input_grad(coded, (w_gate, w_up, w_2), nx)
-    result, coded = lax.optimization_barrier((result, coded))
+    result, coded, own_2 = lax.optimization_barrier((result, coded, own_2))
     arrived = lax.all_to_all(result, ("zb", "xl"), 0, 0)
+    other_2 = lax.ppermute(own_2, "xl", ring(2, 1))
     mine, pair = sides(coded, hidden)
     pair = to_partner(pair)
     x = lax.axis_index(("xh", "xl"))

time: 149 us -> 146 us (0.980)
  the two profiles are of different devices: /device:TPU:2 before, /device:TPU:6 now
where the time goes in v8:
time: 146 us; the launch traced here: 144 us
  blocking collectives  68.8 us (47%)
  starting transfers between devices  34.3 us (23%)
  waiting for transfers between devices  19.3 us (13%)
  Pallas kernels  16.8 us (12%)
  local copies, waits for them, and re-layouts  2.51 us (2%)
    all_gather x1, blocking collectives, shards(): along_z = lax.all_gather(pack(inputs, cotangent), ('zq', 'zb'))  34.7 us
    ppermute x3, starting transfers between devices, to_partner(): return lax.ppermute(a, ('xh', 'xl'), [(0, 3), (3, 0), (1, 2), (2, 1)])  18.2 us
    all_to_all x1, blocking collectives, shards(): lax.all_to_all(summed, 'y', 0, 0)  15.1 us
    all_gather x1, blocking collectives, shards(): lax.all_gather(pointwise(lax.all_to_all(summed, 'y', 0, 0), rows), ('y',...  14.3 us
    ppermute x1, waiting for transfers between devices, shards(): other = lax.ppermute(own, 'xl', ring(2, 1))  7.85 us
    all_to_all x1, starting transfers between devices, shards(): grad_input = z_sum(lax.all_to_all(grad_sum, 'zq', 0, 0), own_tokens, width)  6.52 us
    all_to_all x1, blocking collectives, shards(): summed = core_sum(lax.all_to_all(parts, 'c', 0, 0), rows)  4.73 us
    all_to_all x1, starting transfers between devices, shards(): arrived = lax.all_to_all(result, ('zb', 'xl'), 0, 0)  4.56 us
  transfers between devices with their start and end apart: 7, of which 5 were waited for; matrix products, arithmetic and copies ran while one was open for 1% of the time, Pallas kernels for 9%

profile of v8, /device:TPU:6, one launch (start us, length us, event | category | flops | bytes accessed | tf_op | source)
XLA Modules:
  0.0 143.5 jit_solution(8532872372975886740)
XLA Ops:
  0.7 2.2 %stack_weights.1 = bf16[3,1024,256]{2,1,0:T(8,128)(2,1)} custom-call(bf16[1024,256]{1,0:T(8,128)(2,1)} %wg_ref.3, bf16[1024,256]{1,0:T(8,128)(2,1)} %wu_ref.3, bf16[256,1024]{1,0:T(8,128)(2,1)} %refs_2_.3), custom_call_target="tpu_custom_call" | custom-call | bytes 3145728 | tf_op jit(solution)/shard_map/stack_weights/pallas_call | solution.py:146
  2.9 7.9 %collective-permute-start.1 = (bf16[3,1024,256]{2,1,0:T(8,128)(2,1)}, bf16[3,1024,256]{2,1,0:T(8,128)(2,1)S(1)}, u32[]{:S(2)}, u32[]{:S(2)}) collective-permute-start(bf16[3,1024,256]{2,1,0:T(8,128)(2,1)} %stack_weights.1), channel_id=1, source_target_pairs={{0,24},{24,0},{8,16},{16,8},{1,25},{25,1},{9,17},{17,9},{2,26},{26... | collective-permute-start | bytes 4718600 | tf_op jit(solution)/shard_map/ppermute | solution.py:434
  10.9 34.7 %all-gather = bf16[256,1536]{1,0:T(8,128)(2,1)S(1)} all-gather(bf16[16,1536]{1,0:T(8,128)(2,1)S(1)} %pack.1), channel_id=2, replica_groups=mesh['zq'=8,'zb'=2,'xh'=2,'xl'=2,'y'=4,'c'=2] {'zq','zb'}, dimensions={0}, use_global_device_ids=true | all-gather | bytes 835584 | tf_op jit(solution)/shard_map/all_gather | solution.py:437
  45.7 3.0 %collective-permute-start = (bf16[2,192,1024]{2,1,0:T(8,128)(2,1)S(1)}, bf16[2,192,1024]{2,1,0:T(8,128)(2,1)S(1)}, u32[]{:S(2)}, u32[]{:S(2)}) collective-permute-start(bf16[2,192,1024]{2,1,0:T(8,128)(2,1)S(1)} %unpack.1.tokens_ref.refs_0_), channel_id=1, source_target_pairs={{0,8},{8,0},{1,9},{9,1},{2,10},{10,2},{3,11},{11,3},{4,12},{12,4},... | collective-permute-start | bytes 2359304 | tf_op jit(solution)/shard_map/ppermute | solution.py:445
  48.7 4.0 %collective-permute-start.2 = (bf16[2,192,1024]{2,1,0:T(8,128)(2,1)S(1)}, bf16[2,192,1024]{2,1,0:T(8,128)(2,1)S(1)}, u32[]{:S(2)}, u32[]{:S(2)}) collective-permute-start(bf16[2,192,1024]{2,1,0:T(8,128)(2,1)S(1)} %unpack.1.tokens_ref.refs_0_), channel_id=1, source_target_pairs={{0,24},{24,0},{8,16},{16,8},{1,25},{25,1},{9,17},{17,9},{2,26},{26... | collective-permute-start | bytes 2359304 | tf_op jit(solution)/shard_map/ppermute | solution.py:434
  52.7 1.2 forward.2.refs_4_
  53.9 7.8 %collective-permute-done.tokens_ref.refs_1_ = bf16[2,192,1024]{2,1,0:T(8,128)(2,1)S(1)} collective-permute-done((bf16[2,192,1024]{2,1,0:T(8,128)(2,1)S(1)}, bf16[2,192,1024]{2,1,0:T(8,128)(2,1)S(1)}, u32[]{:S(2)}, u32[]{:S(2)}) %collective-permute-start) | collective-permute-done | bytes 786464 | tf_op jit(solution)/shard_map/ppermute | solution.py:445
  61.7 1.2 forward.3
  62.9 4.7 %all_to_all.20.in_ref = s16[2,4,304,256]{3,2,1,0:T(8,128)(2,1)S(1)} all-to-all(s16[2,4,304,256]{3,2,1,0:T(8,128)(2,1)S(1)} %forward.3), channel_id=1, replica_groups=mesh['zq'=8,'zb'=2,'xh'=2,'xl'=2,'y'=4,'c'=2] {'c'}, dimensions={0} | all-to-all | bytes 2490368 | tf_op jit(solution)/shard_map/all_to_all | solution.py:450
  67.6 0.8 core_sum.1
  68.5 15.1 %all_to_all.21.in_ref = s16[4,304,256]{2,1,0:T(8,128)(2,1)S(1)} all-to-all(s16[4,304,256]{2,1,0:T(8,128)(2,1)S(1)} %core_sum.1), channel_id=1, replica_groups=mesh['zq'=8,'zb'=2,'xh'=2,'xl'=2,'y'=4,'c'=2] {'y'}, dimensions={0} | all-to-all | bytes 1245184 | tf_op jit(solution)/shard_map/all_to_all | solution.py:453
  83.6 0.4 pointwise.1
  84.0 14.3 %all-gather.3 = s16[384,1664]{1,0:T(8,128)(2,1)S(1)} all-gather(s16[48,1664]{1,0:T(8,128)(2,1)S(1)} %pointwise.1), channel_id=3, replica_groups=mesh['zq'=8,'zb'=2,'xh'=2,'xl'=2,'y'=4,'c'=2] {'y','c'}, dimensions={0}, use_global_device_ids=true | all-gather | bytes 1437696 | tf_op jit(solution)/shard_map/all_gather | solution.py:453
  98.3 1.0 input_grad.1
  99.4 0.9 copy-done.3
  100.2 4.6 %all-to-all-start.2 = ((bf16[4,96,1024]{2,1,0:T(8,128)(2,1)}), bf16[4,96,1024]{2,1,0:T(8,128)(2,1)}, u32[]{:S(2)}, u32[]{:S(2)}) async-start(bf16[4,96,1024]{2,1,0:T(8,128)(2,1)} %copy-done.3), calls=%async_computation.2 | async-start | bytes 1572864 | tf_op jit(solution)/shard_map/all_to_all | solution.py:456
  104.8 2.0 %collective-permute-start.4 = (bf16[2,192,1024]{2,1,0:T(8,128)(2,1)}, bf16[2,192,1024]{2,1,0:T(8,128)(2,1)}, u32[]{:S(2)}, u32[]{:S(2)}) collective-permute-start(bf16[2,192,1024]{2,1,0:T(8,128)(2,1)} %copy-done.4), channel_id=1, source_target_pairs={{0,8},{8,0},{1,9},{9,1},{2,10},{10,2},{3,11},{11,3},{4,12},{12,4},... | collective-permute-start | bytes 2359304 | tf_op jit(solution)/shard_map/ppermute | solution.py:457
  107.0 1.2 sides.1
  108.2 6.3 %collective-permute-start.3 = (bf16[384,768]{1,0:T(8,128)(2,1)}, bf16[384,768]{1,0:T(8,128)(2,1)}, u32[]{:S(2)}, u32[]{:S(2)}) collective-permute-start(bf16[384,768]{1,0:T(8,128)(2,1)} %get-tuple-element.21), channel_id=1, source_target_pairs={{0,24},{24,0},{8,16},{16,8},{1,25},{25,1},{9,17},{17,9},{2,26},{26... | collective-permute-start | bytes 1769480 | tf_op jit(solution)/shard_map/ppermute | solution.py:434
  114.5 0.1 broadcast_in_dim.62
  114.6 0.1 broadcast_in_dim.61
  115.0 0.8 maximum_maximum_fusion.keep_ref
  115.8 0.2 all-to-all-done.2.in_ref
  116.0 1.9 %x_sum.1 = bf16[8,8,1536]{2,1,0:T(8,128)(2,1)} custom-call(bf16[4,96,1024]{2,1,0:T(8,128)(2,1)} %all-to-all-done.2.in_ref), custom_call_target="tpu_custom_call" | custom-call | bytes 786432 | tf_op jit(solution)/shard_map/x_sum/pallas_call | solution.py:397
  117.9 6.5 %all-to-all-start.3 = ((bf16[8,8,1536]{2,1,0:T(8,128)(2,1)}), bf16[8,8,1536]{2,1,0:T(8,128)(2,1)S(1)}, u32[]{:S(2)}, u32[]{:S(2)}) async-start(bf16[8,8,1536]{2,1,0:T(8,128)(2,1)} %x_sum.1), calls=%async_computation.3 | async-start | bytes 393216 | tf_op jit(solution)/shard_map/all_to_all | solution.py:470
  124.4 3.7 %collective-permute-done.3.pair_ref = bf16[384,768]{1,0:T(8,128)(2,1)} collective-permute-done((bf16[384,768]{1,0:T(8,128)(2,1)}, bf16[384,768]{1,0:T(8,128)(2,1)}, u32[]{:S(2)}, u32[]{:S(2)}) %collective-permute-start.3) | collective-permute-done | bytes 589856 | tf_op jit(solution)/shard_map/ppermute | solution.py:434
  128.1 3.5 %collective-permute-done.4.refs_3_ = bf16[2,192,1024]{2,1,0:T(8,128)(2,1)} collective-permute-done((bf16[2,192,1024]{2,1,0:T(8,128)(2,1)}, bf16[2,192,1024]{2,1,0:T(8,128)(2,1)}, u32[]{:S(2)}, u32[]{:S(2)}) %collective-permute-start.4) | collective-permute-done | bytes 786464 | tf_op jit(solution)/shard_map/ppermute | solution.py:457
  131.6 1.1 copy-done.5
  132.7 3.4 %gate_up_grads.1 = (bf16[1024,256]{1,0:T(8,128)(2,1)}, bf16[1024,256]{1,0:T(8,128)(2,1)}) custom-call(bf16[384,768]{1,0:T(8,128)(2,1)S(1)} %get-tuple-element.20.own_ref, bf16[384,768]{1,0:T(8,128)(2,1)} %collective-permute-done.3.pair_ref, bf16[2,192,1024]{2,1,0:T(8,128)(2,1)S(1)} %unpack.1.tokens_ref.refs_0_, ...), custom_call_target="tpu_custom_call" | custom-call | flops 805306368 | bytes 3145728 | tf_op jit(solution)/shard_map/gate_up_grads/pallas_call | solution.py:268
  136.1 2.7 %down_grad.1 = bf16[256,1024]{1,0:T(8,128)(2,1)} custom-call(bf16[384,768]{1,0:T(8,128)(2,1)S(1)} %get-tuple-element.20.own_ref, bf16[384,768]{1,0:T(8,128)(2,1)} %collective-permute-done.3.pair_ref, bf16[2,384,256]{2,1,0:T(8,128)(2,1)S(1)} %copy-done.7, bf16[2,192,1024]{2,1,0:T(8,128)(2,1)S(1)} %unpack.1.tokens_ref.refs_0_, ...), custom_call_target="tpu_custom_call" | custom-call | flops 402653184 | bytes 3145728 | tf_op jit(solution)/shard_map/down_grad/pallas_call | solution.py:289
  138.9 4.0 %all-to-all-done.3.in_ref = bf16[8,8,1536]{2,1,0:T(8,128)(2,1)S(1)} async-done(((bf16[8,8,1536]{2,1,0:T(8,128)(2,1)}), bf16[8,8,1536]{2,1,0:T(8,128)(2,1)S(1)}, u32[]{:S(2)}, u32[]{:S(2)}) %all-to-all-start.3) | async-done | bytes 196640 | tf_op jit(solution)/shard_map/all_to_all | solution.py:470
  142.9 0.6 z_sum.1
  (33 shorter events, 0.5 us)
Async XLA Ops:
  0.6 10.2 %copy-start.8 = (bf16[12,1024]{1,0:T(8,128)(2,1)S(1)}, bf16[12,1024]{1,0:T(8,128)(2,1)}, u32[]{:S(2)}) copy-start(bf16[12,1024]{1,0:T(8,128)(2,1)} %refs_0_.3) | copy-start | bytes 73732
  0.6 10.2 %copy-start.9 = (bf16[12,1024]{1,0:T(8,128)(2,1)S(1)}, bf16[12,1024]{1,0:T(8,128)(2,1)}, u32[]{:S(2)}) copy-start(bf16[12,1024]{1,0:T(8,128)(2,1)} %refs_1_.3) | copy-start | bytes 73732
  2.9 49.8 %copy-start = (bf16[1024,256]{1,0:T(8,128)(2,1)S(1)}, bf16[1024,256]{1,0:T(8,128)(2,1)}, u32[]{:S(2)}) copy-start(bf16[1024,256]{1,0:T(8,128)(2,1)} %wg_ref.3) | copy-start | bytes 1572868
  2.9 49.8 %copy-start.1 = (bf16[1024,256]{1,0:T(8,128)(2,1)S(1)}, bf16[1024,256]{1,0:T(8,128)(2,1)}, u32[]{:S(2)}) copy-start(bf16[1024,256]{1,0:T(8,128)(2,1)} %wu_ref.3) | copy-start | bytes 1572868
  2.9 49.8 %copy-start.2 = (bf16[256,1024]{1,0:T(8,128)(2,1)S(1)}, bf16[256,1024]{1,0:T(8,128)(2,1)}, u32[]{:S(2)}) copy-start(bf16[256,1024]{1,0:T(8,128)(2,1)} %refs_2_.3) | copy-start | bytes 1572868
  2.9 49.7 %collective-permute-start.1 = (bf16[3,1024,256]{2,1,0:T(8,128)(2,1)}, bf16[3,1024,256]{2,1,0:T(8,128)(2,1)S(1)}, u32[]{:S(2)}, u32[]{:S(2)}) collective-permute-start(bf16[3,1024,256]{2,1,0:T(8,128)(2,1)} %stack_weights.1), channel_id=1, source_target_pairs={{0,24},{24,0},{8,16},{16,8},{1,25},{25,1},{9,17},{17,9},{2,26},{26... | collective-permute-start | bytes 4718600 | tf_op jit(solution)/shard_map/ppermute | solution.py:434
  45.7 16.1 %collective-permute-start = (bf16[2,192,1024]{2,1,0:T(8,128)(2,1)S(1)}, bf16[2,192,1024]{2,1,0:T(8,128)(2,1)S(1)}, u32[]{:S(2)}, u32[]{:S(2)}) collective-permute-start(bf16[2,192,1024]{2,1,0:T(8,128)(2,1)S(1)} %unpack.1.tokens_ref.refs_0_), channel_id=1, source_target_pairs={{0,8},{8,0},{1,9},{9,1},{2,10},{10,2},{3,11},{11,3},{4,12},{12,4},... | collective-permute-start | bytes 2359304 | tf_op jit(solution)/shard_map/ppermute | solution.py:445
  48.7 19.8 %collective-permute-start.2 = (bf16[2,192,1024]{2,1,0:T(8,128)(2,1)S(1)}, bf16[2,192,1024]{2,1,0:T(8,128)(2,1)S(1)}, u32[]{:S(2)}, u32[]{:S(2)}) collective-permute-start(bf16[2,192,1024]{2,1,0:T(8,128)(2,1)S(1)} %unpack.1.tokens_ref.refs_0_), channel_id=1, source_target_pairs={{0,24},{24,0},{8,16},{16,8},{1,25},{25,1},{9,17},{17,9},{2,26},{26... | collective-permute-start | bytes 2359304 | tf_op jit(solution)/shard_map/ppermute | solution.py:434
  68.5 29.8 %copy-start.4 = (bf16[2,192,1024]{2,1,0:T(8,128)(2,1)}, bf16[2,192,1024]{2,1,0:T(8,128)(2,1)S(1)}, u32[]{:S(2)}) copy-start(bf16[2,192,1024]{2,1,0:T(8,128)(2,1)S(1)} %collective-permute-done.2.refs_2_) | copy-start | bytes 2359300
  99.3 0.9 copy-start.3
  100.2 4.6 %copy-start.10 = (s32[12,2]{0,1:T(2,128)S(1)}, s32[12,2]{0,1:T(2,128)}, u32[]{:S(2)}) copy-start(s32[12,2]{0,1:T(2,128)} %param.11) | copy-start | bytes 292
  100.2 15.7 %all-to-all-start.2 = ((bf16[4,96,1024]{2,1,0:T(8,128)(2,1)}), bf16[4,96,1024]{2,1,0:T(8,128)(2,1)}, u32[]{:S(2)}, u32[]{:S(2)}) async-start(bf16[4,96,1024]{2,1,0:T(8,128)(2,1)} %copy-done.3), calls=%async_computation.2 | async-start | bytes 1572864 | tf_op jit(solution)/shard_map/all_to_all | solution.py:456
  104.8 26.8 %collective-permute-start.4 = (bf16[2,192,1024]{2,1,0:T(8,128)(2,1)}, bf16[2,192,1024]{2,1,0:T(8,128)(2,1)}, u32[]{:S(2)}, u32[]{:S(2)}) collective-permute-start(bf16[2,192,1024]{2,1,0:T(8,128)(2,1)} %copy-done.4), channel_id=1, source_target_pairs={{0,8},{8,0},{1,9},{9,1},{2,10},{10,2},{3,11},{11,3},{4,12},{12,4},... | collective-permute-start | bytes 2359304 | tf_op jit(solution)/shard_map/ppermute | solution.py:457
  108.2 19.9 %collective-permute-start.3 = (bf16[384,768]{1,0:T(8,128)(2,1)}, bf16[384,768]{1,0:T(8,128)(2,1)}, u32[]{:S(2)}, u32[]{:S(2)}) collective-permute-start(bf16[384,768]{1,0:T(8,128)(2,1)} %get-tuple-element.21), channel_id=1, source_target_pairs={{0,24},{24,0},{8,16},{16,8},{1,25},{25,1},{9,17},{17,9},{2,26},{26... | collective-permute-start | bytes 1769480 | tf_op jit(solution)/shard_map/ppermute | solution.py:434
  117.9 25.0 %all-to-all-start.3 = ((bf16[8,8,1536]{2,1,0:T(8,128)(2,1)}), bf16[8,8,1536]{2,1,0:T(8,128)(2,1)S(1)}, u32[]{:S(2)}, u32[]{:S(2)}) async-start(bf16[8,8,1536]{2,1,0:T(8,128)(2,1)} %x_sum.1), calls=%async_computation.3 | async-start | bytes 393216 | tf_op jit(solution)/shard_map/all_to_all | solution.py:470
  131.6 1.1 copy-start.5
  132.7 3.4 %copy-start.6 = (bf16[2,192,1024]{2,1,0:T(8,128)(2,1)S(1)}, bf16[2,192,1024]{2,1,0:T(8,128)(2,1)}, u32[]{:S(2)}) copy-start(bf16[2,192,1024]{2,1,0:T(8,128)(2,1)} %copy-done.4) | copy-start | bytes 2359300
  132.7 3.4 %copy-start.7 = (bf16[2,384,256]{2,1,0:T(8,128)(2,1)S(1)}, bf16[2,384,256]{2,1,0:T(8,128)(2,1)}, u32[]{:S(2)}) copy-start(bf16[2,384,256]{2,1,0:T(8,128)(2,1)} %maximum_maximum_fusion.keep_ref) | copy-start | bytes 1179652

commit v9 on v8

--- a/solution.py
+++ b/solution.py
@@ -374,15 +374,15 @@
     )(coded, *weights)
 
 
-def x_sum_kernel(in_ref, out_ref):
+def x_sum_kernel(*refs):
+    *in_refs, out_ref = refs
     blocks = out_ref.shape[0]
-    width = in_ref.shape[2]
-    half = width // 2
+    half = in_refs[0].shape[1] // 2
     for first in range(0, blocks, 4):
         main = pl.ds(first * 8, 32)
         rest = pl.ds(blocks * 8 + first * 4, 16)
         main, rest = (
-            sum((in_ref[i, rows].astype(F32) for i in range(1, in_ref.shape[0])), in_ref[0, rows].astype(F32))
+            sum((r[rows].astype(F32) for r in in_refs[1:]), in_refs[0][rows].astype(F32))
             for rows in (main, rest)
         )
         for i in range(4):
@@ -393,14 +393,17 @@
 
 
 def x_sum(arrived, blocks):
-    width = arrived.shape[2]
+    parts, rows, width = arrived.shape
     return pl.pallas_call(
         x_sum_kernel,
         out_shape=jax.ShapeDtypeStruct((blocks, 8, 3 * width // 2), BF16),
+        grid=(1,),
+        in_specs=[pl.BlockSpec((None, rows, width), lambda i, k=k: (k, 0, 0)) for k in range(parts)],
+        out_specs=pl.BlockSpec((blocks, 8, 3 * width // 2), lambda i: (0, 0, 0)),
+        compiler_params=params(5),
         cost_estimate=cost(0, 2 * arrived.size),
-        compiler_params=params(5),
         name="x_sum",
-    )(arrived)
+    )(*[arrived] * parts)
 
 
 def z_sum_kernel(in_ref, out_ref):

time: 146 us -> 144 us (0.986)
  transfers between devices with their start and end apart: 7 -> 7, of which waited for: 5 -> 5; matrix products, arithmetic and copies ran while one was open for 1% -> 1% of each run, Pallas kernels for 9% -> 8%
where the time goes in v9:
time: 144 us; the launch traced here: 142 us
  blocking collectives  68.8 us (48%)
  starting transfers between devices  33.6 us (23%)
  waiting for transfers between devices  19.4 us (13%)
  Pallas kernels  15.7 us (11%)
  local copies, waits for them, and re-layouts  2.53 us (2%)
    all_gather x1, blocking collectives, shards(): along_z = lax.all_gather(pack(inputs, cotangent), ('zq', 'zb'))  34.7 us
    ppermute x3, starting transfers between devices, to_partner(): return lax.ppermute(a, ('xh', 'xl'), [(0, 3), (3, 0), (1, 2), (2, 1)])  18.2 us
    all_to_all x1, blocking collectives, shards(): lax.all_to_all(summed, 'y', 0, 0)  15.1 us
    all_gather x1, blocking collectives, shards(): lax.all_gather(pointwise(lax.all_to_all(summed, 'y', 0, 0), rows), ('y',...  14.3 us
    ppermute x1, waiting for transfers between devices, shards(): other = lax.ppermute(own, 'xl', ring(2, 1))  7.84 us
    all_to_all x1, starting transfers between devices, shards(): grad_input = z_sum(lax.all_to_all(grad_sum, 'zq', 0, 0), own_tokens, width)  6.5 us
    ppermute x3, waiting for transfers between devices, to_partner(): return lax.ppermute(a, ('xh', 'xl'), [(0, 3), (3, 0), (1, 2), (2, 1)])  4.96 us
    all_to_all x1, blocking collectives, shards(): summed = core_sum(lax.all_to_all(parts, 'c', 0, 0), rows)  4.73 us
  transfers between devices with their start and end apart: 7, of which 5 were waited for; matrix products, arithmetic and copies ran while one was open for 1% of the time, Pallas kernels for 8%

profile of v9, /device:TPU:6, one launch (start us, length us, event | category | flops | bytes accessed | tf_op | source)
XLA Modules:
  0.0 141.9 jit_solution(7218384489408358522)
XLA Ops:
  0.7 2.3 %stack_weights.1 = bf16[3,1024,256]{2,1,0:T(8,128)(2,1)} custom-call(bf16[1024,256]{1,0:T(8,128)(2,1)} %wg_ref.3, bf16[1024,256]{1,0:T(8,128)(2,1)} %wu_ref.3, bf16[256,1024]{1,0:T(8,128)(2,1)} %refs_2_.3), custom_call_target="tpu_custom_call" | custom-call | bytes 3145728 | tf_op jit(solution)/shard_map/stack_weights/pallas_call | solution.py:146
  3.0 7.9 %collective-permute-start.1 = (bf16[3,1024,256]{2,1,0:T(8,128)(2,1)}, bf16[3,1024,256]{2,1,0:T(8,128)(2,1)S(1)}, u32[]{:S(2)}, u32[]{:S(2)}) collective-permute-start(bf16[3,1024,256]{2,1,0:T(8,128)(2,1)} %stack_weights.1), channel_id=1, source_target_pairs={{0,24},{24,0},{8,16},{16,8},{1,25},{25,1},{9,17},{17,9},{2,26},{26... | collective-permute-start | bytes 4718600 | tf_op jit(solution)/shard_map/ppermute | solution.py:437
  10.9 34.7 %all-gather = bf16[256,1536]{1,0:T(8,128)(2,1)S(1)} all-gather(bf16[16,1536]{1,0:T(8,128)(2,1)S(1)} %pack.1), channel_id=2, replica_groups=mesh['zq'=8,'zb'=2,'xh'=2,'xl'=2,'y'=4,'c'=2] {'zq','zb'}, dimensions={0}, use_global_device_ids=true | all-gather | bytes 835584 | tf_op jit(solution)/shard_map/all_gather | solution.py:440
  45.7 3.0 %collective-permute-start = (bf16[2,192,1024]{2,1,0:T(8,128)(2,1)S(1)}, bf16[2,192,1024]{2,1,0:T(8,128)(2,1)S(1)}, u32[]{:S(2)}, u32[]{:S(2)}) collective-permute-start(bf16[2,192,1024]{2,1,0:T(8,128)(2,1)S(1)} %unpack.1.tokens_ref.refs_0_), channel_id=1, source_target_pairs={{0,8},{8,0},{1,9},{9,1},{2,10},{10,2},{3,11},{11,3},{4,12},{12,4},... | collective-permute-start | bytes 2359304 | tf_op jit(solution)/shard_map/ppermute | solution.py:448
  48.7 4.0 %collective-permute-start.2 = (bf16[2,192,1024]{2,1,0:T(8,128)(2,1)S(1)}, bf16[2,192,1024]{2,1,0:T(8,128)(2,1)S(1)}, u32[]{:S(2)}, u32[]{:S(2)}) collective-permute-start(bf16[2,192,1024]{2,1,0:T(8,128)(2,1)S(1)} %unpack.1.tokens_ref.refs_0_), channel_id=1, source_target_pairs={{0,24},{24,0},{8,16},{16,8},{1,25},{25,1},{9,17},{17,9},{2,26},{26... | collective-permute-start | bytes 2359304 | tf_op jit(solution)/shard_map/ppermute | solution.py:437
  52.7 1.2 forward.2.refs_4_
  53.9 7.8 %collective-permute-done.tokens_ref.refs_1_ = bf16[2,192,1024]{2,1,0:T(8,128)(2,1)S(1)} collective-permute-done((bf16[2,192,1024]{2,1,0:T(8,128)(2,1)S(1)}, bf16[2,192,1024]{2,1,0:T(8,128)(2,1)S(1)}, u32[]{:S(2)}, u32[]{:S(2)}) %collective-permute-start) | collective-permute-done | bytes 786464 | tf_op jit(solution)/shard_map/ppermute | solution.py:448
  61.7 1.2 forward.3
  62.9 4.7 %all_to_all.20.in_ref = s16[2,4,304,256]{3,2,1,0:T(8,128)(2,1)S(1)} all-to-all(s16[2,4,304,256]{3,2,1,0:T(8,128)(2,1)S(1)} %forward.3), channel_id=1, replica_groups=mesh['zq'=8,'zb'=2,'xh'=2,'xl'=2,'y'=4,'c'=2] {'c'}, dimensions={0} | all-to-all | bytes 2490368 | tf_op jit(solution)/shard_map/all_to_all | solution.py:453
  67.7 0.8 core_sum.1
  68.5 15.1 %all_to_all.21.in_ref = s16[4,304,256]{2,1,0:T(8,128)(2,1)S(1)} all-to-all(s16[4,304,256]{2,1,0:T(8,128)(2,1)S(1)} %core_sum.1), channel_id=1, replica_groups=mesh['zq'=8,'zb'=2,'xh'=2,'xl'=2,'y'=4,'c'=2] {'y'}, dimensions={0} | all-to-all | bytes 1245184 | tf_op jit(solution)/shard_map/all_to_all | solution.py:456
  83.6 0.4 pointwise.1
  84.0 14.3 %all-gather.3 = s16[384,1664]{1,0:T(8,128)(2,1)S(1)} all-gather(s16[48,1664]{1,0:T(8,128)(2,1)S(1)} %pointwise.1), channel_id=3, replica_groups=mesh['zq'=8,'zb'=2,'xh'=2,'xl'=2,'y'=4,'c'=2] {'y','c'}, dimensions={0}, use_global_device_ids=true | all-gather | bytes 1437696 | tf_op jit(solution)/shard_map/all_gather | solution.py:456
  98.3 1.0 input_grad.1
  99.4 0.9 copy-done.5
  100.3 3.9 %all-to-all-start.2 = ((bf16[4,96,1024]{2,1,0:T(8,128)(2,1)}), bf16[4,96,1024]{2,1,0:T(8,128)(2,1)S(1)}, u32[]{:S(2)}, u32[]{:S(2)}) async-start(bf16[4,96,1024]{2,1,0:T(8,128)(2,1)} %copy-done.5), calls=%async_computation.2 | async-start | bytes 1572864 | tf_op jit(solution)/shard_map/all_to_all | solution.py:459
  104.2 2.0 %collective-permute-start.4 = (bf16[2,192,1024]{2,1,0:T(8,128)(2,1)}, bf16[2,192,1024]{2,1,0:T(8,128)(2,1)}, u32[]{:S(2)}, u32[]{:S(2)}) collective-permute-start(bf16[2,192,1024]{2,1,0:T(8,128)(2,1)} %copy-done.6), channel_id=1, source_target_pairs={{0,8},{8,0},{1,9},{9,1},{2,10},{10,2},{3,11},{11,3},{4,12},{12,4},... | collective-permute-start | bytes 2359304 | tf_op jit(solution)/shard_map/ppermute | solution.py:460
  106.3 1.2 sides.1
  107.5 6.3 %collective-permute-start.3 = (bf16[384,768]{1,0:T(8,128)(2,1)}, bf16[384,768]{1,0:T(8,128)(2,1)}, u32[]{:S(2)}, u32[]{:S(2)}) collective-permute-start(bf16[384,768]{1,0:T(8,128)(2,1)} %get-tuple-element.21), channel_id=1, source_target_pairs={{0,24},{24,0},{8,16},{16,8},{1,25},{25,1},{9,17},{17,9},{2,26},{26... | collective-permute-start | bytes 1769480 | tf_op jit(solution)/shard_map/ppermute | solution.py:437
  114.0 0.1 broadcast_in_dim.61
  114.1 0.1 broadcast_in_dim.60
  114.2 0.1 broadcast_in_dim.57
  114.4 0.8 maximum_maximum_fusion.keep_ref
  115.2 0.8 x_sum.1
  116.0 6.5 %all-to-all-start.3 = ((bf16[8,8,1536]{2,1,0:T(8,128)(2,1)}), bf16[8,8,1536]{2,1,0:T(8,128)(2,1)S(1)}, u32[]{:S(2)}, u32[]{:S(2)}) async-start(bf16[8,8,1536]{2,1,0:T(8,128)(2,1)} %x_sum.1), calls=%async_computation.3 | async-start | bytes 393216 | tf_op jit(solution)/shard_map/all_to_all | solution.py:473
  122.5 5.0 %collective-permute-done.3.pair_ref = bf16[384,768]{1,0:T(8,128)(2,1)} collective-permute-done((bf16[384,768]{1,0:T(8,128)(2,1)}, bf16[384,768]{1,0:T(8,128)(2,1)}, u32[]{:S(2)}, u32[]{:S(2)}) %collective-permute-start.3) | collective-permute-done | bytes 589856 | tf_op jit(solution)/shard_map/ppermute | solution.py:437
  127.5 3.5 %collective-permute-done.4.refs_3_ = bf16[2,192,1024]{2,1,0:T(8,128)(2,1)} collective-permute-done((bf16[2,192,1024]{2,1,0:T(8,128)(2,1)}, bf16[2,192,1024]{2,1,0:T(8,128)(2,1)}, u32[]{:S(2)}, u32[]{:S(2)}) %collective-permute-start.4) | collective-permute-done | bytes 786464 | tf_op jit(solution)/shard_map/ppermute | solution.py:460
  131.0 1.1 copy-done.7
  132.1 3.4 %gate_up_grads.1 = (bf16[1024,256]{1,0:T(8,128)(2,1)}, bf16[1024,256]{1,0:T(8,128)(2,1)}) custom-call(bf16[384,768]{1,0:T(8,128)(2,1)S(1)} %get-tuple-element.20.own_ref, bf16[384,768]{1,0:T(8,128)(2,1)} %collective-permute-done.3.pair_ref, bf16[2,192,1024]{2,1,0:T(8,128)(2,1)S(1)} %unpack.1.tokens_ref.refs_0_, bf16[2,192,1024]{2,1,0:T(8,128)(2,1)S(1)} %copy-done.3, ...), custom_call_target="tpu_custom_call" | custom-call | flops 805306368 | bytes 3145728 | tf_op jit(solution)/shard_map/gate_up_grads/pallas_call | solution.py:268
  135.5 2.7 %down_grad.1 = bf16[256,1024]{1,0:T(8,128)(2,1)} custom-call(bf16[384,768]{1,0:T(8,128)(2,1)S(1)} %get-tuple-element.20.own_ref, bf16[384,768]{1,0:T(8,128)(2,1)} %collective-permute-done.3.pair_ref, bf16[2,384,256]{2,1,0:T(8,128)(2,1)S(1)} %copy-done.9, bf16[2,192,1024]{2,1,0:T(8,128)(2,1)S(1)} %unpack.1.tokens_ref.refs_0_, ...), custom_call_target="tpu_custom_call" | custom-call | flops 402653184 | bytes 3145728 | tf_op jit(solution)/shard_map/down_grad/pallas_call | solution.py:289
  138.2 3.0 %all-to-all-done.3.in_ref = bf16[8,8,1536]{2,1,0:T(8,128)(2,1)S(1)} async-done(((bf16[8,8,1536]{2,1,0:T(8,128)(2,1)}), bf16[8,8,1536]{2,1,0:T(8,128)(2,1)S(1)}, u32[]{:S(2)}, u32[]{:S(2)}) %all-to-all-start.3) | async-done | bytes 196640 | tf_op jit(solution)/shard_map/all_to_all | solution.py:473
  141.2 0.6 z_sum.1
  (37 shorter events, 0.5 us)
Async XLA Ops:
  0.6 10.2 %copy-start.10 = (bf16[12,1024]{1,0:T(8,128)(2,1)S(1)}, bf16[12,1024]{1,0:T(8,128)(2,1)}, u32[]{:S(2)}) copy-start(bf16[12,1024]{1,0:T(8,128)(2,1)} %refs_0_.3) | copy-start | bytes 73732
  0.6 10.2 %copy-start.11 = (bf16[12,1024]{1,0:T(8,128)(2,1)S(1)}, bf16[12,1024]{1,0:T(8,128)(2,1)}, u32[]{:S(2)}) copy-start(bf16[12,1024]{1,0:T(8,128)(2,1)} %refs_1_.3) | copy-start | bytes 73732
  2.9 49.8 %copy-start = (bf16[1024,256]{1,0:T(8,128)(2,1)S(1)}, bf16[1024,256]{1,0:T(8,128)(2,1)}, u32[]{:S(2)}) copy-start(bf16[1024,256]{1,0:T(8,128)(2,1)} %wg_ref.3) | copy-start | bytes 1572868
  2.9 49.8 %copy-start.1 = (bf16[1024,256]{1,0:T(8,128)(2,1)S(1)}, bf16[1024,256]{1,0:T(8,128)(2,1)}, u32[]{:S(2)}) copy-start(bf16[1024,256]{1,0:T(8,128)(2,1)} %wu_ref.3) | copy-start | bytes 1572868
  2.9 49.8 %copy-start.4 = (bf16[256,1024]{1,0:T(8,128)(2,1)S(1)}, bf16[256,1024]{1,0:T(8,128)(2,1)}, u32[]{:S(2)}) copy-start(bf16[256,1024]{1,0:T(8,128)(2,1)} %refs_2_.3) | copy-start | bytes 1572868
  3.0 49.7 %collective-permute-start.1 = (bf16[3,1024,256]{2,1,0:T(8,128)(2,1)}, bf16[3,1024,256]{2,1,0:T(8,128)(2,1)S(1)}, u32[]{:S(2)}, u32[]{:S(2)}) collective-permute-start(bf16[3,1024,256]{2,1,0:T(8,128)(2,1)} %stack_weights.1), channel_id=1, source_target_pairs={{0,24},{24,0},{8,16},{16,8},{1,25},{25,1},{9,17},{17,9},{2,26},{26... | collective-permute-start | bytes 4718600 | tf_op jit(solution)/shard_map/ppermute | solution.py:437
  45.7 16.1 %collective-permute-start = (bf16[2,192,1024]{2,1,0:T(8,128)(2,1)S(1)}, bf16[2,192,1024]{2,1,0:T(8,128)(2,1)S(1)}, u32[]{:S(2)}, u32[]{:S(2)}) collective-permute-start(bf16[2,192,1024]{2,1,0:T(8,128)(2,1)S(1)} %unpack.1.tokens_ref.refs_0_), channel_id=1, source_target_pairs={{0,8},{8,0},{1,9},{9,1},{2,10},{10,2},{3,11},{11,3},{4,12},{12,4},... | collective-permute-start | bytes 2359304 | tf_op jit(solution)/shard_map/ppermute | solution.py:448
  48.7 19.8 %collective-permute-start.2 = (bf16[2,192,1024]{2,1,0:T(8,128)(2,1)S(1)}, bf16[2,192,1024]{2,1,0:T(8,128)(2,1)S(1)}, u32[]{:S(2)}, u32[]{:S(2)}) collective-permute-start(bf16[2,192,1024]{2,1,0:T(8,128)(2,1)S(1)} %unpack.1.tokens_ref.refs_0_), channel_id=1, source_target_pairs={{0,24},{24,0},{8,16},{16,8},{1,25},{25,1},{9,17},{17,9},{2,26},{26... | collective-permute-start | bytes 2359304 | tf_op jit(solution)/shard_map/ppermute | solution.py:437
  61.7 1.2 copy-start.2
  68.5 29.8 %copy-start.6 = (bf16[2,192,1024]{2,1,0:T(8,128)(2,1)}, bf16[2,192,1024]{2,1,0:T(8,128)(2,1)S(1)}, u32[]{:S(2)}) copy-start(bf16[2,192,1024]{2,1,0:T(8,128)(2,1)S(1)} %collective-permute-done.2.refs_2_) | copy-start | bytes 2359300
  99.4 0.9 copy-start.5
  100.3 3.9 %copy-start.12 = (s32[12,2]{0,1:T(2,128)S(1)}, s32[12,2]{0,1:T(2,128)}, u32[]{:S(2)}) copy-start(s32[12,2]{0,1:T(2,128)} %param.11) | copy-start | bytes 292
  100.3 15.0 %all-to-all-start.2 = ((bf16[4,96,1024]{2,1,0:T(8,128)(2,1)}), bf16[4,96,1024]{2,1,0:T(8,128)(2,1)S(1)}, u32[]{:S(2)}, u32[]{:S(2)}) async-start(bf16[4,96,1024]{2,1,0:T(8,128)(2,1)} %copy-done.5), calls=%async_computation.2 | async-start | bytes 1572864 | tf_op jit(solution)/shard_map/all_to_all | solution.py:459
  104.2 26.8 %collective-permute-start.4 = (bf16[2,192,1024]{2,1,0:T(8,128)(2,1)}, bf16[2,192,1024]{2,1,0:T(8,128)(2,1)}, u32[]{:S(2)}, u32[]{:S(2)}) collective-permute-start(bf16[2,192,1024]{2,1,0:T(8,128)(2,1)} %copy-done.6), channel_id=1, source_target_pairs={{0,8},{8,0},{1,9},{9,1},{2,10},{10,2},{3,11},{11,3},{4,12},{12,4},... | collective-permute-start | bytes 2359304 | tf_op jit(solution)/shard_map/ppermute | solution.py:460
  107.5 19.9 %collective-permute-start.3 = (bf16[384,768]{1,0:T(8,128)(2,1)}, bf16[384,768]{1,0:T(8,128)(2,1)}, u32[]{:S(2)}, u32[]{:S(2)}) collective-permute-start(bf16[384,768]{1,0:T(8,128)(2,1)} %get-tuple-element.21), channel_id=1, source_target_pairs={{0,24},{24,0},{8,16},{16,8},{1,25},{25,1},{9,17},{17,9},{2,26},{26... | collective-permute-start | bytes 1769480 | tf_op jit(solution)/shard_map/ppermute | solution.py:437
  115.1 15.8 %copy-start.3 = (bf16[2,192,1024]{2,1,0:T(8,128)(2,1)S(1)}, bf16[2,192,1024]{2,1,0:T(8,128)(2,1)}, u32[]{:S(2)}) copy-start(bf16[2,192,1024]{2,1,0:T(8,128)(2,1)} %copy-done.2) | copy-start | bytes 2359300
  116.0 25.2 %all-to-all-start.3 = ((bf16[8,8,1536]{2,1,0:T(8,128)(2,1)}), bf16[8,8,1536]{2,1,0:T(8,128)(2,1)S(1)}, u32[]{:S(2)}, u32[]{:S(2)}) async-start(bf16[8,8,1536]{2,1,0:T(8,128)(2,1)} %x_sum.1), calls=%async_computation.3 | async-start | bytes 393216 | tf_op jit(solution)/shard_map/all_to_all | solution.py:473
  131.0 1.1 copy-start.7
  132.1 3.4 %copy-start.8 = (bf16[2,192,1024]{2,1,0:T(8,128)(2,1)S(1)}, bf16[2,192,1024]{2,1,0:T(8,128)(2,1)}, u32[]{:S(2)}) copy-start(bf16[2,192,1024]{2,1,0:T(8,128)(2,1)} %copy-done.6) | copy-start | bytes 2359300
  132.1 3.4 %copy-start.9 = (bf16[2,384,256]{2,1,0:T(8,128)(2,1)S(1)}, bf16[2,384,256]{2,1,0:T(8,128)(2,1)}, u32[]{:S(2)}) copy-start(bf16[2,384,256]{2,1,0:T(8,128)(2,1)} %maximum_maximum_fusion.keep_ref) | copy-start | bytes 1179652

commit v10 on v9

--- a/solution.py
+++ b/solution.py
@@ -120,10 +120,11 @@
 
 def stack_kernel(wg_ref, wu_ref, wd_ref, out_ref, held, sems):
     hidden, width = wd_ref.shape
-    copies = []
-    for first in range(0, width, hidden):
-        part = pl.ds(first, hidden)
-        for k, source in enumerate((wg_ref.at[part], wu_ref.at[part], wd_ref.at[:, part])):
+    copies, half = [], hidden // 2
+    for first in range(0, width, half):
+        part = pl.ds(first, half)
+        block, upper = pl.ds(first // hidden * hidden, hidden), pl.ds(first % hidden, half)
+        for k, source in enumerate((wg_ref.at[part], wu_ref.at[part], wd_ref.at[upper, block])):
             place, sem = held.at[k, part], sems.at[len(copies)]
             copies.append(
                 (
@@ -150,7 +151,7 @@
         out_specs=spec,
         scratch_shapes=[
             pltpu.VMEM((3, width, hidden), BF16),
-            pltpu.SemaphoreType.DMA((3 * (width // hidden),)),
+            pltpu.SemaphoreType.DMA((6 * (width // hidden),)),
         ],
         compiler_params=params(56),
         cost_estimate=cost(0, 12 * width * hidden),

time: 144 us -> 145 us (level)
  no operation moved by 1% of the time
where the time goes in v10:
time: 145 us; the launch traced here: 142 us
  blocking collectives  68.8 us (47%)
  starting transfers between devices  33.6 us (23%)
  waiting for transfers between devices  19.4 us (13%)
  Pallas kernels  15.7 us (11%)
  local copies, waits for them, and re-layouts  2.53 us (2%)
    all_gather x1, blocking collectives, shards(): along_z = lax.all_gather(pack(inputs, cotangent), ('zq', 'zb'))  34.7 us
    ppermute x3, starting transfers between devices, to_partner(): return lax.ppermute(a, ('xh', 'xl'), [(0, 3), (3, 0), (1, 2), (2, 1)])  18.2 us
    all_to_all x1, blocking collectives, shards(): lax.all_to_all(summed, 'y', 0, 0)  15.1 us
    all_gather x1, blocking collectives, shards(): lax.all_gather(pointwise(lax.all_to_all(summed, 'y', 0, 0), rows), ('y',...  14.3 us
    ppermute x1, waiting for transfers between devices, shards(): other = lax.ppermute(own, 'xl', ring(2, 1))  7.84 us
    all_to_all x1, starting transfers between devices, shards(): grad_input = z_sum(lax.all_to_all(grad_sum, 'zq', 0, 0), own_tokens, width)  6.5 us
    ppermute x3, waiting for transfers between devices, to_partner(): return lax.ppermute(a, ('xh', 'xl'), [(0, 3), (3, 0), (1, 2), (2, 1)])  4.96 us
    all_to_all x1, blocking collectives, shards(): summed = core_sum(lax.all_to_all(parts, 'c', 0, 0), rows)  4.73 us
  transfers between devices with their start and end apart: 7, of which 5 were waited for; matrix products, arithmetic and copies ran while one was open for 1% of the time, Pallas kernels for 8%

profile of v10, /device:TPU:6, one launch (start us, length us, event | category | flops | bytes accessed | tf_op | source)
XLA Modules:
  0.0 141.9 jit_solution(18192298718963975268)
XLA Ops:
  0.7 2.3 %stack_weights.1 = bf16[3,1024,256]{2,1,0:T(8,128)(2,1)} custom-call(bf16[1024,256]{1,0:T(8,128)(2,1)} %wg_ref.3, bf16[1024,256]{1,0:T(8,128)(2,1)} %wu_ref.3, bf16[256,1024]{1,0:T(8,128)(2,1)} %refs_2_.3), custom_call_target="tpu_custom_call" | custom-call | bytes 3145728 | tf_op jit(solution)/shard_map/stack_weights/pallas_call | solution.py:147
  3.0 7.9 %collective-permute-start.1 = (bf16[3,1024,256]{2,1,0:T(8,128)(2,1)}, bf16[3,1024,256]{2,1,0:T(8,128)(2,1)S(1)}, u32[]{:S(2)}, u32[]{:S(2)}) collective-permute-start(bf16[3,1024,256]{2,1,0:T(8,128)(2,1)} %stack_weights.1), channel_id=1, source_target_pairs={{0,24},{24,0},{8,16},{16,8},{1,25},{25,1},{9,17},{17,9},{2,26},{26... | collective-permute-start | bytes 4718600 | tf_op jit(solution)/shard_map/ppermute | solution.py:438
  10.9 34.7 %all-gather = bf16[256,1536]{1,0:T(8,128)(2,1)S(1)} all-gather(bf16[16,1536]{1,0:T(8,128)(2,1)S(1)} %pack.1), channel_id=2, replica_groups=mesh['zq'=8,'zb'=2,'xh'=2,'xl'=2,'y'=4,'c'=2] {'zq','zb'}, dimensions={0}, use_global_device_ids=true | all-gather | bytes 835584 | tf_op jit(solution)/shard_map/all_gather | solution.py:441
  45.7 3.0 %collective-permute-start = (bf16[2,192,1024]{2,1,0:T(8,128)(2,1)S(1)}, bf16[2,192,1024]{2,1,0:T(8,128)(2,1)S(1)}, u32[]{:S(2)}, u32[]{:S(2)}) collective-permute-start(bf16[2,192,1024]{2,1,0:T(8,128)(2,1)S(1)} %unpack.1.tokens_ref.refs_0_), channel_id=1, source_target_pairs={{0,8},{8,0},{1,9},{9,1},{2,10},{10,2},{3,11},{11,3},{4,12},{12,4},... | collective-permute-start | bytes 2359304 | tf_op jit(solution)/shard_map/ppermute | solution.py:449
  48.7 4.0 %collective-permute-start.2 = (bf16[2,192,1024]{2,1,0:T(8,128)(2,1)S(1)}, bf16[2,192,1024]{2,1,0:T(8,128)(2,1)S(1)}, u32[]{:S(2)}, u32[]{:S(2)}) collective-permute-start(bf16[2,192,1024]{2,1,0:T(8,128)(2,1)S(1)} %unpack.1.tokens_ref.refs_0_), channel_id=1, source_target_pairs={{0,24},{24,0},{8,16},{16,8},{1,25},{25,1},{9,17},{17,9},{2,26},{26... | collective-permute-start | bytes 2359304 | tf_op jit(solution)/shard_map/ppermute | solution.py:438
  52.8 1.2 forward.2.refs_4_
  53.9 7.8 %collective-permute-done.tokens_ref.refs_1_ = bf16[2,192,1024]{2,1,0:T(8,128)(2,1)S(1)} collective-permute-done((bf16[2,192,1024]{2,1,0:T(8,128)(2,1)S(1)}, bf16[2,192,1024]{2,1,0:T(8,128)(2,1)S(1)}, u32[]{:S(2)}, u32[]{:S(2)}) %collective-permute-start) | collective-permute-done | bytes 786464 | tf_op jit(solution)/shard_map/ppermute | solution.py:449
  61.8 1.2 forward.3
  63.0 4.7 %all_to_all.20.in_ref = s16[2,4,304,256]{3,2,1,0:T(8,128)(2,1)S(1)} all-to-all(s16[2,4,304,256]{3,2,1,0:T(8,128)(2,1)S(1)} %forward.3), channel_id=1, replica_groups=mesh['zq'=8,'zb'=2,'xh'=2,'xl'=2,'y'=4,'c'=2] {'c'}, dimensions={0} | all-to-all | bytes 2490368 | tf_op jit(solution)/shard_map/all_to_all | solution.py:454
  67.7 0.8 core_sum.1
  68.6 15.1 %all_to_all.21.in_ref = s16[4,304,256]{2,1,0:T(8,128)(2,1)S(1)} all-to-all(s16[4,304,256]{2,1,0:T(8,128)(2,1)S(1)} %core_sum.1), channel_id=1, replica_groups=mesh['zq'=8,'zb'=2,'xh'=2,'xl'=2,'y'=4,'c'=2] {'y'}, dimensions={0} | all-to-all | bytes 1245184 | tf_op jit(solution)/shard_map/all_to_all | solution.py:457
  83.7 0.4 pointwise.1
  84.1 14.3 %all-gather.3 = s16[384,1664]{1,0:T(8,128)(2,1)S(1)} all-gather(s16[48,1664]{1,0:T(8,128)(2,1)S(1)} %pointwise.1), channel_id=3, replica_groups=mesh['zq'=8,'zb'=2,'xh'=2,'xl'=2,'y'=4,'c'=2] {'y','c'}, dimensions={0}, use_global_device_ids=true | all-gather | bytes 1437696 | tf_op jit(solution)/shard_map/all_gather | solution.py:457
  98.4 1.0 input_grad.1
  99.4 0.9 copy-done.5
  100.3 3.9 %all-to-all-start.2 = ((bf16[4,96,1024]{2,1,0:T(8,128)(2,1)}), bf16[4,96,1024]{2,1,0:T(8,128)(2,1)S(1)}, u32[]{:S(2)}, u32[]{:S(2)}) async-start(bf16[4,96,1024]{2,1,0:T(8,128)(2,1)} %copy-done.5), calls=%async_computation.2 | async-start | bytes 1572864 | tf_op jit(solution)/shard_map/all_to_all | solution.py:460
  104.2 2.0 %collective-permute-start.4 = (bf16[2,192,1024]{2,1,0:T(8,128)(2,1)}, bf16[2,192,1024]{2,1,0:T(8,128)(2,1)}, u32[]{:S(2)}, u32[]{:S(2)}) collective-permute-start(bf16[2,192,1024]{2,1,0:T(8,128)(2,1)} %copy-done.6), channel_id=1, source_target_pairs={{0,8},{8,0},{1,9},{9,1},{2,10},{10,2},{3,11},{11,3},{4,12},{12,4},... | collective-permute-start | bytes 2359304 | tf_op jit(solution)/shard_map/ppermute | solution.py:461
  106.4 1.2 sides.1
  107.6 6.3 %collective-permute-start.3 = (bf16[384,768]{1,0:T(8,128)(2,1)}, bf16[384,768]{1,0:T(8,128)(2,1)}, u32[]{:S(2)}, u32[]{:S(2)}) collective-permute-start(bf16[384,768]{1,0:T(8,128)(2,1)} %get-tuple-element.21), channel_id=1, source_target_pairs={{0,24},{24,0},{8,16},{16,8},{1,25},{25,1},{9,17},{17,9},{2,26},{26... | collective-permute-start | bytes 1769480 | tf_op jit(solution)/shard_map/ppermute | solution.py:438
  113.9 0.1 broadcast_in_dim.62
  114.0 0.1 broadcast_in_dim.61
  114.2 0.1 broadcast_in_dim.60
  114.4 0.8 maximum_maximum_fusion.keep_ref
  115.3 0.8 x_sum.1
  116.0 6.5 %all-to-all-start.3 = ((bf16[8,8,1536]{2,1,0:T(8,128)(2,1)}), bf16[8,8,1536]{2,1,0:T(8,128)(2,1)S(1)}, u32[]{:S(2)}, u32[]{:S(2)}) async-start(bf16[8,8,1536]{2,1,0:T(8,128)(2,1)} %x_sum.1), calls=%async_computation.3 | async-start | bytes 393216 | tf_op jit(solution)/shard_map/all_to_all | solution.py:474
  122.5 5.0 %collective-permute-done.3.pair_ref = bf16[384,768]{1,0:T(8,128)(2,1)} collective-permute-done((bf16[384,768]{1,0:T(8,128)(2,1)}, bf16[384,768]{1,0:T(8,128)(2,1)}, u32[]{:S(2)}, u32[]{:S(2)}) %collective-permute-start.3) | collective-permute-done | bytes 589856 | tf_op jit(solution)/shard_map/ppermute | solution.py:438
  127.5 3.5 %collective-permute-done.4.refs_3_ = bf16[2,192,1024]{2,1,0:T(8,128)(2,1)} collective-permute-done((bf16[2,192,1024]{2,1,0:T(8,128)(2,1)}, bf16[2,192,1024]{2,1,0:T(8,128)(2,1)}, u32[]{:S(2)}, u32[]{:S(2)}) %collective-permute-start.4) | collective-permute-done | bytes 786464 | tf_op jit(solution)/shard_map/ppermute | solution.py:461
  131.0 1.1 copy-done.7
  132.2 3.4 %gate_up_grads.1 = (bf16[1024,256]{1,0:T(8,128)(2,1)}, bf16[1024,256]{1,0:T(8,128)(2,1)}) custom-call(bf16[384,768]{1,0:T(8,128)(2,1)S(1)} %get-tuple-element.20.own_ref, bf16[384,768]{1,0:T(8,128)(2,1)} %collective-permute-done.3.pair_ref, bf16[2,192,1024]{2,1,0:T(8,128)(2,1)S(1)} %unpack.1.tokens_ref.refs_0_, bf16[2,192,1024]{2,1,0:T(8,128)(2,1)S(1)} %copy-done.3, ...), custom_call_target="tpu_custom_call" | custom-call | flops 805306368 | bytes 3145728 | tf_op jit(solution)/shard_map/gate_up_grads/pallas_call | solution.py:269
  135.6 2.7 %down_grad.1 = bf16[256,1024]{1,0:T(8,128)(2,1)} custom-call(bf16[384,768]{1,0:T(8,128)(2,1)S(1)} %get-tuple-element.20.own_ref, bf16[384,768]{1,0:T(8,128)(2,1)} %collective-permute-done.3.pair_ref, bf16[2,384,256]{2,1,0:T(8,128)(2,1)S(1)} %copy-done.9, bf16[2,192,1024]{2,1,0:T(8,128)(2,1)S(1)} %unpack.1.tokens_ref.refs_0_, ...), custom_call_target="tpu_custom_call" | custom-call | flops 402653184 | bytes 3145728 | tf_op jit(solution)/shard_map/down_grad/pallas_call | solution.py:290
  138.3 3.0 %all-to-all-done.3.in_ref = bf16[8,8,1536]{2,1,0:T(8,128)(2,1)S(1)} async-done(((bf16[8,8,1536]{2,1,0:T(8,128)(2,1)}), bf16[8,8,1536]{2,1,0:T(8,128)(2,1)S(1)}, u32[]{:S(2)}, u32[]{:S(2)}) %all-to-all-start.3) | async-done | bytes 196640 | tf_op jit(solution)/shard_map/all_to_all | solution.py:474
  141.3 0.6 z_sum.1
  (37 shorter events, 0.5 us)
Async XLA Ops:
  0.6 10.3 %copy-start.10 = (bf16[12,1024]{1,0:T(8,128)(2,1)S(1)}, bf16[12,1024]{1,0:T(8,128)(2,1)}, u32[]{:S(2)}) copy-start(bf16[12,1024]{1,0:T(8,128)(2,1)} %refs_0_.3) | copy-start | bytes 73732
  0.6 10.3 %copy-start.11 = (bf16[12,1024]{1,0:T(8,128)(2,1)S(1)}, bf16[12,1024]{1,0:T(8,128)(2,1)}, u32[]{:S(2)}) copy-start(bf16[12,1024]{1,0:T(8,128)(2,1)} %refs_1_.3) | copy-start | bytes 73732
  3.0 49.8 %copy-start = (bf16[1024,256]{1,0:T(8,128)(2,1)S(1)}, bf16[1024,256]{1,0:T(8,128)(2,1)}, u32[]{:S(2)}) copy-start(bf16[1024,256]{1,0:T(8,128)(2,1)} %wg_ref.3) | copy-start | bytes 1572868
  3.0 49.8 %copy-start.1 = (bf16[1024,256]{1,0:T(8,128)(2,1)S(1)}, bf16[1024,256]{1,0:T(8,128)(2,1)}, u32[]{:S(2)}) copy-start(bf16[1024,256]{1,0:T(8,128)(2,1)} %wu_ref.3) | copy-start | bytes 1572868
  3.0 49.8 %copy-start.4 = (bf16[256,1024]{1,0:T(8,128)(2,1)S(1)}, bf16[256,1024]{1,0:T(8,128)(2,1)}, u32[]{:S(2)}) copy-start(bf16[256,1024]{1,0:T(8,128)(2,1)} %refs_2_.3) | copy-start | bytes 1572868
  3.0 49.7 %collective-permute-start.1 = (bf16[3,1024,256]{2,1,0:T(8,128)(2,1)}, bf16[3,1024,256]{2,1,0:T(8,128)(2,1)S(1)}, u32[]{:S(2)}, u32[]{:S(2)}) collective-permute-start(bf16[3,1024,256]{2,1,0:T(8,128)(2,1)} %stack_weights.1), channel_id=1, source_target_pairs={{0,24},{24,0},{8,16},{16,8},{1,25},{25,1},{9,17},{17,9},{2,26},{26... | collective-permute-start | bytes 4718600 | tf_op jit(solution)/shard_map/ppermute | solution.py:438
  45.7 16.1 %collective-permute-start = (bf16[2,192,1024]{2,1,0:T(8,128)(2,1)S(1)}, bf16[2,192,1024]{2,1,0:T(8,128)(2,1)S(1)}, u32[]{:S(2)}, u32[]{:S(2)}) collective-permute-start(bf16[2,192,1024]{2,1,0:T(8,128)(2,1)S(1)} %unpack.1.tokens_ref.refs_0_), channel_id=1, source_target_pairs={{0,8},{8,0},{1,9},{9,1},{2,10},{10,2},{3,11},{11,3},{4,12},{12,4},... | collective-permute-start | bytes 2359304 | tf_op jit(solution)/shard_map/ppermute | solution.py:449
  48.7 19.8 %collective-permute-start.2 = (bf16[2,192,1024]{2,1,0:T(8,128)(2,1)S(1)}, bf16[2,192,1024]{2,1,0:T(8,128)(2,1)S(1)}, u32[]{:S(2)}, u32[]{:S(2)}) collective-permute-start(bf16[2,192,1024]{2,1,0:T(8,128)(2,1)S(1)} %unpack.1.tokens_ref.refs_0_), channel_id=1, source_target_pairs={{0,24},{24,0},{8,16},{16,8},{1,25},{25,1},{9,17},{17,9},{2,26},{26... | collective-permute-start | bytes 2359304 | tf_op jit(solution)/shard_map/ppermute | solution.py:438
  61.8 1.2 copy-start.2
  68.6 29.8 %copy-start.6 = (bf16[2,192,1024]{2,1,0:T(8,128)(2,1)}, bf16[2,192,1024]{2,1,0:T(8,128)(2,1)S(1)}, u32[]{:S(2)}) copy-start(bf16[2,192,1024]{2,1,0:T(8,128)(2,1)S(1)} %collective-permute-done.2.refs_2_) | copy-start | bytes 2359300
  99.4 0.9 copy-start.5
  100.3 3.9 %copy-start.12 = (s32[12,2]{0,1:T(2,128)S(1)}, s32[12,2]{0,1:T(2,128)}, u32[]{:S(2)}) copy-start(s32[12,2]{0,1:T(2,128)} %param.11) | copy-start | bytes 292
  100.3 15.0 %all-to-all-start.2 = ((bf16[4,96,1024]{2,1,0:T(8,128)(2,1)}), bf16[4,96,1024]{2,1,0:T(8,128)(2,1)S(1)}, u32[]{:S(2)}, u32[]{:S(2)}) async-start(bf16[4,96,1024]{2,1,0:T(8,128)(2,1)} %copy-done.5), calls=%async_computation.2 | async-start | bytes 1572864 | tf_op jit(solution)/shard_map/all_to_all | solution.py:460
  104.2 26.8 %collective-permute-start.4 = (bf16[2,192,1024]{2,1,0:T(8,128)(2,1)}, bf16[2,192,1024]{2,1,0:T(8,128)(2,1)}, u32[]{:S(2)}, u32[]{:S(2)}) collective-permute-start(bf16[2,192,1024]{2,1,0:T(8,128)(2,1)} %copy-done.6), channel_id=1, source_target_pairs={{0,8},{8,0},{1,9},{9,1},{2,10},{10,2},{3,11},{11,3},{4,12},{12,4},... | collective-permute-start | bytes 2359304 | tf_op jit(solution)/shard_map/ppermute | solution.py:461
  107.6 19.9 %collective-permute-start.3 = (bf16[384,768]{1,0:T(8,128)(2,1)}, bf16[384,768]{1,0:T(8,128)(2,1)}, u32[]{:S(2)}, u32[]{:S(2)}) collective-permute-start(bf16[384,768]{1,0:T(8,128)(2,1)} %get-tuple-element.21), channel_id=1, source_target_pairs={{0,24},{24,0},{8,16},{16,8},{1,25},{25,1},{9,17},{17,9},{2,26},{26... | collective-permute-start | bytes 1769480 | tf_op jit(solution)/shard_map/ppermute | solution.py:438
  115.2 15.8 %copy-start.3 = (bf16[2,192,1024]{2,1,0:T(8,128)(2,1)S(1)}, bf16[2,192,1024]{2,1,0:T(8,128)(2,1)}, u32[]{:S(2)}) copy-start(bf16[2,192,1024]{2,1,0:T(8,128)(2,1)} %copy-done.2) | copy-start | bytes 2359300
  116.0 25.2 %all-to-all-start.3 = ((bf16[8,8,1536]{2,1,0:T(8,128)(2,1)}), bf16[8,8,1536]{2,1,0:T(8,128)(2,1)S(1)}, u32[]{:S(2)}, u32[]{:S(2)}) async-start(bf16[8,8,1536]{2,1,0:T(8,128)(2,1)} %x_sum.1), calls=%async_computation.3 | async-start | bytes 393216 | tf_op jit(solution)/shard_map/all_to_all | solution.py:474
  131.0 1.1 copy-start.7
  132.1 3.4 %copy-start.8 = (bf16[2,192,1024]{2,1,0:T(8,128)(2,1)S(1)}, bf16[2,192,1024]{2,1,0:T(8,128)(2,1)}, u32[]{:S(2)}) copy-start(bf16[2,192,1024]{2,1,0:T(8,128)(2,1)} %copy-done.6) | copy-start | bytes 2359300
  132.2 3.4 %copy-start.9 = (bf16[2,384,256]{2,1,0:T(8,128)(2,1)S(1)}, bf16[2,384,256]{2,1,0:T(8,128)(2,1)}, u32[]{:S(2)}) copy-start(bf16[2,384,256]{2,1,0:T(8,128)(2,1)} %maximum_maximum_fusion.keep_ref) | copy-start | bytes 1179652
